TPU v7x, 32 devices: a whole 2x2x4 slice. The times are simulated.
32 devices in a mesh: groups: 2 (over y), ctx: 4 (over z), heads: 2 (over x), dp: 2 (over core).
Axes of the slice: x: 2, y: 2, z: 4, core: 2. Of those that a mesh axis runs over, the one named last changes fastest.
Arguments:
- tokens: bfloat16 [4, 2048, 1024], P(('groups', 'dp'), 'ctx', 'heads'), parts along dimension 0, may hold values from -12 to 12
- w_qkv: bfloat16 [3, 1024, 1024], P(None, None, 'heads'), may hold values from -0.375 to 0.375
- w_out: bfloat16 [1024, 1024], P('heads'), may hold values from -0.1875 to 0.1875
- ln_gain: float32 [1024], P('heads'), may hold values from 0.5 to 1.5
- ln_bias: float32 [1024], P('heads'), may hold values from -3 to 3
- random_blocks: int32 [4, 16, 3], P(('groups', 'dp'), 'ctx'), parts along dimension 0, may hold values from 0 to 15, as said below
- summary_pos: int32 [4, 16], P(('groups', 'dp')), parts along dimension 0, may hold values from 0 to 2047, as said below
- summary_blocks: int32 [4, 16, 8], P(('groups', 'dp')), parts along dimension 0, may hold values from 0 to 15, as said below
- pair_lengths: int32 [4, 4], P(('groups', 'dp')), parts along dimension 0, may hold values from 1 to 1536, 2048 in all within a row
Outputs:
- normed: bfloat16 [4, 2048, 1024], P(('groups', 'dp'), 'ctx', 'heads'), parts along dimension 0
There are 2 independent parts, one for each index of `groups`. A program takes and returns all parts, laid end to end along the dimension named above; an argument that names none is the same for every part. Nothing has to cross between parts.
Inputs may be any that keep to these rules, and one draw needn't show every extreme that they name: `random_blocks`: the 4 x 3 entries of one device's range name at most 3 blocks of any one device's range of 4 blocks, repeats counted; in every draw some range is named exactly 3 times from every device's range. `summary_pos`: each range of 512 positions of a sequence holds exactly 4 of them; they are distinct and increasing. `summary_blocks`: the first entry of each list is the block holding that row's summary position; entries may repeat.
All inputs are finite; a program needn't handle non-finite values.
Results may differ from a plain program's by a relative error of at most 0.012.
The roundings to bfloat16 on the way count: a program that leaves them out, or rounds other values in their place, can miss the bound.
Values may be sent and summed in bfloat16 or wider, within the bound.
No kernel may reach another device: no remote copies, remote signals or barrier semaphores. Data moves between devices by JAX's collectives and lax.ppermute only.
A program may use at most 64 MiB of HBM per device.

v0:
```python
import jax
import jax.numpy as jnp
from jax import lax
from jax.sharding import PartitionSpec as P

HEAD = 64
BLOCK = 128


MASKED = -1e30


def extended(x, sides, width):
    for axis, dim in sides:
        size, length = (lax.axis_size(axis), x.shape[dim])
        up = [(i, (i + 1) % size) for i in range(size - 1)]
        down = [(j, i) for i, j in up]
        last = lax.slice_in_dim(x, length - width, length, axis=dim)
        first = lax.slice_in_dim(x, 0, width, axis=dim)
        before = lax.ppermute(last, axis, up)
        after = lax.ppermute(first, axis, down)
        x = jnp.concatenate([before, x, after], axis=dim)
    return x


def segment_ids(positions, bounds):
    return jnp.sum((positions[..., None] >= bounds).astype(jnp.int32), axis=-1)


def attend(queries, keys, values, allowed, head_count):
    group_count, query_len, all_width = queries.shape
    key_len = keys.shape[1]
    query_heads = queries.reshape(group_count, query_len, head_count, HEAD)
    key_heads = keys.reshape(group_count, key_len, head_count, HEAD)
    value_heads = values.reshape(group_count, key_len, head_count, HEAD)
    scores = jnp.einsum(
        "gqhe,gkhe->ghqk", query_heads, key_heads, preferred_element_type=jnp.float32
    ) * HEAD ** (-0.5)
    scores = jnp.where(allowed[:, None], scores, MASKED)
    maxima = jnp.max(scores, axis=-1, keepdims=True)
    weights = jnp.where(allowed[:, None], jnp.exp(scores - maxima), 0.0)
    totals = jnp.sum(weights, axis=-1)
    mixture = jnp.einsum(
        "ghqk,gkhe->gqhe",
        weights.astype(jnp.bfloat16),
        value_heads,
        preferred_element_type=jnp.float32,
    )
    mixture = mixture / jnp.transpose(totals, (0, 2, 1))[..., None]
    return mixture.reshape(group_count, query_len, all_width).astype(jnp.bfloat16)


def three_views(window_span, group_size, axis_pos):
    views = []
    for shift_index in range(3):
        piece = lax.slice_in_dim(
            window_span,
            shift_index * BLOCK,
            shift_index * BLOCK + group_size * BLOCK,
            axis=axis_pos,
        )
        new_shape = (
            window_span.shape[:axis_pos] + (group_size, BLOCK) + window_span.shape[axis_pos + 1 :]
        )
        views.append(piece.reshape(new_shape))
    return jnp.concatenate(views, axis=axis_pos + 1)


def shards(
    tokens, w_qkv, w_out, ln_gain, ln_bias, random_blocks, summary_pos, summary_blocks, pair_lengths
):
    tok_rows = tokens.shape[1]
    head_cols = tokens.shape[2]
    heads_here = head_cols // HEAD
    full_width = w_out.shape[1]
    ctx_count = lax.axis_size("ctx")
    ctx_index = lax.axis_index("ctx")
    block_count = tok_rows // BLOCK
    seq_total = tok_rows * ctx_count
    bounds = jnp.cumsum(pair_lengths[0])
    own_tokens = tokens[0]
    projected = jnp.einsum(
        "nc,kcd->knd",
        lax.all_gather(own_tokens, "heads", axis=1, tiled=True),
        w_qkv,
        preferred_element_type=jnp.float32,
    ).astype(jnp.bfloat16)
    queries = projected[0]
    own_kv = projected[1:3]
    rim_kv = extended(own_kv, (("ctx", 1),), BLOCK)
    query_pos = ctx_index * tok_rows + jnp.arange(tok_rows, dtype=jnp.int32)
    own_seg = segment_ids(query_pos, bounds)
    rim_pos = ctx_index * tok_rows - BLOCK + jnp.arange(tok_rows + 2 * BLOCK, dtype=jnp.int32)
    rim_ok = (rim_pos >= 0) & (rim_pos < seq_total)
    rim_seg = segment_ids(rim_pos, bounds)
    rand_count = random_blocks.shape[2]
    picked = random_blocks[0].reshape(-1)
    pick_count = picked.shape[0]
    capacity = max(2, -(-pick_count // ctx_count))
    owners = picked // block_count
    within = picked % block_count
    slot_order = jnp.arange(pick_count, dtype=jnp.int32)
    earlier = (owners[:, None] == owners[None, :]) & (slot_order[None, :] < slot_order[:, None])
    pick_rank = jnp.sum(earlier.astype(jnp.int32), axis=1)
    pick_slot = owners * capacity + pick_rank
    slot_table = (
        pick_slot[:, None] == jnp.arange(ctx_count * capacity, dtype=jnp.int32)[None, :]
    ).astype(jnp.int32)
    requests = jnp.sum(slot_table * within[:, None], axis=0).reshape(ctx_count, capacity)
    own_blocks = own_kv.reshape(2, block_count, BLOCK, head_cols).transpose(1, 0, 2, 3)
    reply = jnp.take(
        own_blocks, lax.all_to_all(requests, "ctx", split_axis=0, concat_axis=0, tiled=True), axis=0
    )
    fetched = lax.all_to_all(reply, "ctx", split_axis=0, concat_axis=0, tiled=True)
    flat_blocks = fetched.reshape(ctx_count * capacity, 2, BLOCK, head_cols)
    far_kv = jnp.take(flat_blocks, pick_slot, axis=0).reshape(
        block_count, rand_count, 2, BLOCK, head_cols
    )
    far_kv = far_kv.transpose(2, 0, 1, 3, 4).reshape(2, block_count, rand_count * BLOCK, head_cols)
    far_pos = (
        picked.reshape(block_count, rand_count)[:, :, None] * BLOCK
        + jnp.arange(BLOCK, dtype=jnp.int32)
    ).reshape(block_count, rand_count * BLOCK)
    far_seg = segment_ids(far_pos, bounds)
    group_size = min(4, block_count)
    group_steps = block_count // group_size

    def window_step(unused, step_index):
        near_kv = three_views(rim_kv, group_size, 1)
        near_ok = three_views(rim_ok, group_size, 0)
        near_seg = three_views(rim_seg, group_size, 0)
        key_set = jnp.concatenate([near_kv, far_kv], axis=2)
        key_seg = jnp.concatenate([near_seg, far_seg], axis=1)
        key_ok = jnp.concatenate([near_ok, jnp.ones(far_seg.shape, jnp.bool_)], axis=1)
        query_seg = own_seg.reshape(group_size, BLOCK)
        allowed = key_ok[:, None, :] & (key_seg[:, None, :] == query_seg[:, :, None])
        query_group = queries.reshape(group_size, BLOCK, head_cols)
        return (unused, attend(query_group, key_set[0], key_set[1], allowed, heads_here))

    _, window_out = lax.scan(window_step, 0, jnp.arange(group_steps, dtype=jnp.int32))
    attention = window_out.reshape(tok_rows, head_cols)
    summary_rows = summary_pos[0]
    summary_lists = summary_blocks[0]
    summaries = summary_rows.shape[0]
    per_device = summaries // ctx_count
    mine = (
        lax.dynamic_slice_in_dim(summary_rows, ctx_index * per_device, per_device, 0)
        - ctx_index * tok_rows
    )
    summary_query = jnp.take(queries, mine, axis=0)
    all_queries = lax.all_gather(summary_query, "ctx", axis=0, tiled=True)
    summary_seg = segment_ids(summary_rows, bounds)
    key_block = ctx_index * block_count + jnp.arange(block_count, dtype=jnp.int32)
    listed = jnp.any(summary_lists[:, :, None] == key_block[None, None, :], axis=1)
    key_heads = own_kv[0].reshape(tok_rows, heads_here, HEAD)
    value_heads = own_kv[1].reshape(tok_rows, heads_here, HEAD)
    summary_group = min(128, summaries)
    group_total = summaries // summary_group

    def group_scores():
        query_part = all_queries.reshape(summary_group, heads_here, HEAD)
        allowed = jnp.broadcast_to(listed[:, :, None], (summary_group, block_count, BLOCK)).reshape(
            summary_group, tok_rows
        )
        allowed = allowed & (own_seg[None, :] == summary_seg[:, None])
        scores = jnp.einsum(
            "qhe,khe->hqk", query_part, key_heads, preferred_element_type=jnp.float32
        ) * HEAD ** (-0.5)
        return (jnp.where(allowed[None], scores, MASKED), allowed)

    def weigh(scores, allowed, maxima):
        weights = jnp.where(allowed[None], jnp.exp(scores - maxima[:, :, None]), 0.0)
        totals = jnp.sum(weights, axis=-1)
        mixture = jnp.einsum(
            "hqk,khe->qhe",
            weights.astype(jnp.bfloat16),
            value_heads,
            preferred_element_type=jnp.float32,
        )
        return (totals.T, mixture.reshape(summary_group, head_cols))

    def max_step(unused, group_index):
        scores, allowed = group_scores()
        return (unused, jnp.max(scores, axis=-1).T)

    _, maxima_all = lax.scan(max_step, 0, jnp.arange(group_total, dtype=jnp.int32))
    maxima_all = lax.pmax(maxima_all.reshape(summaries, heads_here), "ctx")

    def sum_step(unused, group_index):
        scores, allowed = group_scores()
        maxima = maxima_all.T
        return (unused, weigh(scores, allowed, maxima))

    _, (totals_all, mixture_all) = lax.scan(sum_step, 0, jnp.arange(group_total, dtype=jnp.int32))
    totals_all = totals_all.reshape(summaries, heads_here)
    mixture_all = mixture_all.reshape(summaries, head_cols)
    totals_all, mixture_all = (
        lax.psum(totals_all.astype(jnp.bfloat16), "ctx").astype(jnp.float32),
        lax.psum(mixture_all.astype(jnp.bfloat16), "ctx").astype(jnp.float32),
    )
    own_totals = lax.dynamic_slice_in_dim(totals_all, ctx_index * per_device, per_device, 0)
    own_mixture = lax.dynamic_slice_in_dim(mixture_all, ctx_index * per_device, per_device, 0)
    summary_out = (own_mixture / jnp.repeat(own_totals, HEAD, axis=1)).astype(jnp.bfloat16)
    attention = attention.at[mine].set(summary_out)
    partial_value = jnp.dot(attention, w_out, preferred_element_type=jnp.float32)
    summed = lax.psum_scatter(
        partial_value.astype(jnp.bfloat16), "heads", scatter_dimension=1, tiled=True
    ).astype(jnp.float32)
    hidden = own_tokens.astype(jnp.float32) + summed
    row_sums = lax.psum((jnp.sum(hidden, axis=1), jnp.sum(hidden * hidden, axis=1)), "heads")
    row_mean = row_sums[0] / full_width
    row_var = row_sums[1] / full_width - row_mean * row_mean
    normed = (hidden - row_mean[:, None]) * lax.rsqrt(row_var + 1e-05)[:, None] * ln_gain + ln_bias
    return normed.astype(jnp.bfloat16)[None]


def solution(mesh):
    in_specs = (
        P(("groups", "dp"), "ctx", "heads"),
        P(None, None, "heads"),
        P("heads", None),
        P("heads"),
        P("heads"),
        P(("groups", "dp"), "ctx", None),
        P(("groups", "dp"), None),
        P(("groups", "dp"), None, None),
        P(("groups", "dp"), None),
    )
    out_specs = P(("groups", "dp"), "ctx", "heads")
    return jax.shard_map(shards, mesh=mesh, in_specs=in_specs, out_specs=out_specs, check_vma=False)
```

profile of v0, /device:TPU:0, one launch (start us, length us, event | category | flops | bytes accessed | tf_op | source)
XLA Modules:
  0.0 255.9 jit_solution(4831505476906459526)
XLA Ops:
  9.3 6.3 %all-to-all-start = ((s32[4,1,3]{2,1,0:T(1,128)}), s32[4,1,3]{2,1,0:T(1,128)S(1)}, u32[]{:S(2)}, u32[]{:S(2)}) async-start(s32[4,1,3]{2,1,0:T(1,128)} %bitcast.7), calls=%async_computation | async-start | bytes 4096 | tf_op jit(solution)/shard_map/all_to_all | solution.py:112
  17.1 4.0 %all-to-all-done = s32[4,1,3]{2,1,0:T(1,128)S(1)} async-done(((s32[4,1,3]{2,1,0:T(1,128)}), s32[4,1,3]{2,1,0:T(1,128)S(1)}, u32[]{:S(2)}, u32[]{:S(2)}) %all-to-all-start) | async-done | bytes 80 | tf_op jit(solution)/shard_map/all_to_all | solution.py:112
  21.4 11.6 %all-gather.4.cloned.1.call-done = bf16[1,512,1024]{2,1,0:T(8,128)(2,1)} async-done(((bf16[1,512,512]{2,1,0:T(8,128)(2,1)}), bf16[1,512,1024]{2,1,0:T(8,128)(2,1)}) %all-gather.4.cloned.1.call-update) | async-done | bytes 1048592 | tf_op jit(solution)/shard_map/all_gather | solution.py:84
  33.0 3.1 %fusion.7 = bf16[3,512,512]{1,2,0:T(8,128)(2,1)S(1)} fusion(bf16[3,1024,512]{2,1,0:T(8,128)(2,1)S(1)} %copy-done, bf16[1,512,1024]{2,1,0:T(8,128)(2,1)} %all-gather.4.cloned.1.call-done), kind=kOutput, calls=%fused_computation.18 | convolution fusion | flops 1611399168 | bytes 5767168 | tf_op jit(solution)/shard_map/nc,kcd->knd/dot_general | solution.py:82
  39.3 2.6 gather_fusion
  41.9 3.9 %broadcast_select_fusion = bf16[4,3,2,128,512]{4,3,2,1,0:T(8,128)(2,1)} fusion(bf16[4,3,2,128,512]{4,3,2,1,0:T(8,128)(2,1)} %bitcast.115, pred[4,3]{1,0:T(4,128)(4,1)S(1)} %compare_and_fusion.2), kind=kLoop, calls=%fused_computation.15 | loop fusion | flops 1572864 | bytes 6291468 | tf_op jit(solution)/shard_map/jit(_take)/select_n | solution.py:111
  45.8 4.7 %all-to-all-start.1 = ((bf16[4,3,2,128,512]{4,3,2,1,0:T(8,128)(2,1)}), bf16[4,3,2,128,512]{4,3,2,1,0:T(8,128)(2,1)S(1)}, u32[]{:S(2)}, u32[]{:S(2)}) async-start(bf16[4,3,2,128,512]{4,3,2,1,0:T(8,128)(2,1)} %broadcast_select_fusion), calls=%async_computation.1 | async-start | bytes 6291456 | tf_op jit(solution)/shard_map/all_to_all | solution.py:114
  54.9 4.6 %collective-permute-start = (bf16[2,128,512]{1,2,0:T(8,128)(2,1)}, bf16[2,128,512]{1,2,0:T(8,128)(2,1)}, u32[]{:S(2)}, u32[]{:S(2)}) collective-permute-start(bf16[2,128,512]{1,2,0:T(8,128)(2,1)} %get-tuple-element.76), channel_id=1, source_target_pairs={{0,4},{4,8},{8,12},{1,5},{5,9},{9,13},{2,6},{6,10},{10,14},{3,7},{... | collective-permute-start | bytes 786440 | tf_op jit(solution)/shard_map/ppermute | solution.py:20
  60.9 2.8 %fusion.58 = (bf16[1,512,512]{1,2,0:T(8,128)(2,1)}, bf16[512,512]{0,1:T(8,128)(2,1)}, bf16[1,512,512]{1,2,0:T(8,128)(2,1)}, bf16[1,512,512]{1,2,0:T(8,128)(2,1)}) fusion(bf16[3,512,512]{1,2,0:T(8,128)(2,1)} %copy-done.4), kind=kLoop, calls=%fused_computation.124 | loop fusion | bytes 3670016 | tf_op jit(solution)/shard_map/slice | solution.py:156
  67.4 64.8 %all-gather.1 = bf16[4,4,512]{2,1,0:T(4,128)(2,1)S(1)} all-gather(bf16[1,4,512]{2,1,0:T(4,128)(2,1)S(1)} %select_bitcast_fusion.1), channel_id=1, replica_groups=mesh['groups'=2,'ctx'=4,'heads'=2,'dp'=2] {'ctx'}, dimensions={0}, use_global_device_ids=true | all-gather | bytes 20480 | tf_op jit(solution)/shard_map/all_gather | solution.py:151
  133.7 10.7 %pmax.7 = f32[8,16]{1,0:T(8,128)S(1)} all-reduce(f32[8,16]{1,0:T(8,128)S(1)} %get-tuple-element.114), channel_id=1, replica_groups=mesh['groups'=2,'ctx'=4,'heads'=2,'dp'=2] {'ctx'}, use_global_device_ids=true, to_apply=%region_11.12 | all-reduce | flops 128 | bytes 1024 | tf_op jit(solution)/shard_map/pmax | solution.py:187
  145.7 2.4 copy.98
  148.5 16.7 %all-reduce.1 = (bf16[16,8]{0,1:T(8,128)(2,1)S(1)}, bf16[16,512]{1,0:T(8,128)(2,1)}) all-reduce(bf16[16,8]{0,1:T(8,128)(2,1)S(1)} %bitcast.127, bf16[16,512]{1,0:T(8,128)(2,1)S(1)} %convert_element_type.88), channel_id=1, replica_groups=mesh['groups'=2,'ctx'=4,'heads'=2,'dp'=2] {'ctx'}, use_global_device_ids=true, to_apply=%region_14.15 | all-reduce | flops 8320 | bytes 33280 | tf_op jit(solution)/shard_map/psum | solution.py:198
  167.5 3.1 %pad_maximum_fusion.2 = (bf16[2,512,512]{1,2,0:T(8,128)(2,1)}, bf16[2,512,512]{1,2,0:T(8,128)(2,1)}) fusion(bf16[2,512,512]{1,2,0:T(8,128)(2,1)} %copy-done.2, bf16[2,128,512]{1,2,0:T(8,128)(2,1)} %collective-permute-done, bf16[2,128,512]{1,2,0:T(8,128)(2,1)} %collective-permute-done.1), kind=kLoop, calls=%fused_computation.29 | loop fusion | flops 4194304 | bytes 3670016 | tf_op jit(solution)/shard_map/concatenate | solution.py:22
  175.2 2.5 gather_fusion.1
  181.8 5.1 %pad_maximum_fusion = bf16[2,4,768,512]{3,2,1,0:T(8,128)(2,1)S(1)} fusion(bf16[2,4,384,512]{3,2,1,0:T(8,128)(2,1)S(1)} %bitcast.117, bf16[2,4,128,512]{3,2,1,0:T(8,128)(2,1)S(1)} %bitcast.119, bf16[2,4,128,512]{3,2,1,0:T(8,128)(2,1)S(1)} %copy-done.5, bf16[2,4,128,512]{3,2,1,0:T(8,128)(2,1)S(1)} %bitcast.118), kind=kLoop, calls=%fused_computation.8 | loop fusion | flops 25165824 | bytes 12582912 | tf_op jit(solution)/shard_map/while/body/eval_jaxpr/concatenate | solution.py:132
  189.2 4.7 %copy.102 = bf16[1,4,768,512]{2,3,1,0:T(8,128)(2,1)} copy(bf16[1,4,768,512]{3,2,1,0:T(8,128)(2,1)} %get-tuple-element.70) | data formatting | bytes 6291456 | tf_op jit(solution)/shard_map/while/body/eval_jaxpr/slice | solution.py:138
  194.0 2.8 %copy.100 = bf16[1,4,768,512]{2,3,1,0:T(8,128)(2,1)} copy(bf16[1,4,768,512]{3,2,1,0:T(8,128)(2,1)S(1)} %get-tuple-element.71) | data formatting | bytes 6291456 | tf_op jit(solution)/shard_map/while/body/eval_jaxpr/slice | solution.py:138
  196.8 10.1 %fusion.61 = (f32[4,8,128]{2,1,0:T(8,128)}, bf16[4,8,128,768]{3,2,1,0:T(8,128)(2,1)}) fusion(pred[4,128,768]{2,1,0:T(8,128)(4,1)S(1)} %copy-done.9, bf16[4,768,8,64]{1,3,2,0:T(8,128)(2,1)} %bitcast.120, bf16[4,128,8,64]{1,0,3,2:T(4,128)(2,1)} %reshape_squeeze.20), kind=kOutput, calls=%fused_computation.127 | convolution fusion | flops 421528320 | bytes 10371072 | tf_op jit(solution)/shard_map/while/body/eval_jaxpr/sub | solution.py:41
  206.8 5.8 %fusion.14 = bf16[4,128,8,64]{1,3,2,0:T(8,128)(2,1)} fusion(bf16[4,768,8,64]{1,3,2,0:T(8,128)(2,1)S(1)} %bitcast.121, bf16[4,8,128,768]{3,2,1,0:T(8,128)(2,1)} %get-tuple-element.113, f32[4,128,8]{1,2,0:T(8,128)} %bitcast.135), kind=kOutput, calls=%fused_computation.22 | convolution fusion | flops 403177472 | bytes 9977856 | tf_op jit(solution)/shard_map/while/body/eval_jaxpr/ghqk,gkhe->gqhe/dot_general | solution.py:43
  215.7 2.8 %scatter_custom_fusion = bf16[512,512]{1,0:T(8,128)(2,1)} fusion(bf16[512,512]{1,0:T(8,128)(2,1)} %reshape.487, s32[4]{0:T(128)S(1)} %fusion.53, f32[4,512]{1,0:T(4,128)S(1)} %reshape.447, bf16[16,512]{1,0:T(8,128)(2,1)} %get-tuple-element.69, s32[]{:T(128)S(6)} %select_n.139, s32[]{:T(128)} %constant.131.clone.1), kind=kCustom, calls=%fused_computation.64 | custom fusion | flops 6144 | bytes 537092 | tf_op jit(solution)/shard_map/scatter | solution.py:204
  218.5 3.1 %convolution_convert_fusion.1 = bf16[512,1024]{1,0:T(8,128)(2,1)} fusion(bf16[512,512]{1,0:T(8,128)(2,1)} %scatter_custom_fusion, bf16[512,1024]{1,0:T(8,128)(2,1)} %param.11), kind=kOutput, calls=%fused_computation.19 | convolution fusion | flops 537395200 | bytes 2621440 | tf_op jit(solution)/shard_map/dot_general | solution.py:205
  221.6 18.7 %reduce-scatter.2.cloned.1.call-done = bf16[512,512]{1,0:T(8,128)(2,1)} async-done(((bf16[512,1024]{1,0:T(8,128)(2,1)}), bf16[512,512]{1,0:T(8,128)(2,1)}) %reduce-scatter.2.cloned.1.call-update) | async-done | bytes 524304 | tf_op jit(solution)/shard_map/reduce_scatter | solution.py:206
  241.8 4.9 %all-reduce = (f32[512]{0:T(512)S(1)}, f32[512]{0:T(512)S(1)}) all-reduce(f32[512]{0:T(512)S(1)} %get-tuple-element.58, f32[512]{0:T(512)S(1)} %get-tuple-element.57), channel_id=1, replica_groups=mesh['groups'=2,'ctx'=4,'heads'=2,'dp'=2] {'heads'}, use_global_device_ids=true, to_apply=%region_20.21 | all-reduce | flops 1024 | bytes 8192 | tf_op jit(solution)/shard_map/psum | solution.py:210
  (110 shorter events, 40.3 us)
Async XLA Ops:
  6.5 26.5 %copy-start = (bf16[3,1024,512]{2,1,0:T(8,128)(2,1)S(1)}, bf16[3,1024,512]{2,1,0:T(8,128)(2,1)}, u32[]{:S(2)}) copy-start(bf16[3,1024,512]{2,1,0:T(8,128)(2,1)} %param.10) | copy-start | bytes 9437188
  6.5 26.5 %all-gather.4.cloned.1.call-start = ((), (), s32[]{:S(2)}) async-start(), calls=%async_computation.4 | async-start | bytes 1572864 | tf_op jit(solution)/shard_map/all_gather | solution.py:84
  9.3 11.8 %all-to-all-start = ((s32[4,1,3]{2,1,0:T(1,128)}), s32[4,1,3]{2,1,0:T(1,128)S(1)}, u32[]{:S(2)}, u32[]{:S(2)}) async-start(s32[4,1,3]{2,1,0:T(1,128)} %bitcast.7), calls=%async_computation | async-start | bytes 4096 | tf_op jit(solution)/shard_map/all_to_all | solution.py:112
  36.1 1.1 copy-start.4
  37.3 1.1 copy-start.2
  38.7 3.2 %copy-start.3 = (bf16[2,4,128,512]{2,1,3,0:T(4,128)(2,1)}, bf16[2,4,128,512]{2,1,3,0:T(4,128)(2,1)S(1)}, u32[]{:S(2)}) copy-start(bf16[2,4,128,512]{2,1,3,0:T(4,128)(2,1)S(1)} %reshape.439) | copy-start | bytes 3145732
  45.8 4.7 %copy-start.12 = (s32[1,16]{1,0:T(1,128)S(1)}, s32[1,16]{1,0:T(1,128)}, u32[]{:S(2)}) copy-start(s32[1,16]{1,0:T(1,128)} %param.15) | copy-start | bytes 196
  45.8 5.0 %copy-start.13 = (s32[1,4]{1,0:T(1,128)S(1)}, s32[1,4]{1,0:T(1,128)}, u32[]{:S(2)}) copy-start(s32[1,4]{1,0:T(1,128)} %param.17) | copy-start | bytes 52
  45.8 129.3 %all-to-all-start.1 = ((bf16[4,3,2,128,512]{4,3,2,1,0:T(8,128)(2,1)}), bf16[4,3,2,128,512]{4,3,2,1,0:T(8,128)(2,1)S(1)}, u32[]{:S(2)}, u32[]{:S(2)}) async-start(bf16[4,3,2,128,512]{4,3,2,1,0:T(8,128)(2,1)} %broadcast_select_fusion), calls=%async_computation.1 | async-start | bytes 6291456 | tf_op jit(solution)/shard_map/all_to_all | solution.py:114
  50.6 189.8 %reduce-scatter.2.cloned.1.call-start = ((), (), s32[]{:S(2)}) async-start(), calls=%async_computation.3 | async-start | bytes 1572864 | tf_op jit(solution)/shard_map/reduce_scatter | solution.py:206
  54.9 112.5 %collective-permute-start = (bf16[2,128,512]{1,2,0:T(8,128)(2,1)}, bf16[2,128,512]{1,2,0:T(8,128)(2,1)}, u32[]{:S(2)}, u32[]{:S(2)}) collective-permute-start(bf16[2,128,512]{1,2,0:T(8,128)(2,1)} %get-tuple-element.76), channel_id=1, source_target_pairs={{0,4},{4,8},{8,12},{1,5},{5,9},{9,13},{2,6},{6,10},{10,14},{3,7},{... | collective-permute-start | bytes 786440 | tf_op jit(solution)/shard_map/ppermute | solution.py:20
  59.6 107.9 %collective-permute-start.1 = (bf16[2,128,512]{1,2,0:T(8,128)(2,1)}, bf16[2,128,512]{1,2,0:T(8,128)(2,1)}, u32[]{:S(2)}, u32[]{:S(2)}) collective-permute-start(bf16[2,128,512]{1,2,0:T(8,128)(2,1)} %get-tuple-element.77), channel_id=1, source_target_pairs={{4,0},{8,4},{12,8},{5,1},{9,5},{13,9},{6,2},{10,6},{14,10},{7,3},{... | collective-permute-start | bytes 786440 | tf_op jit(solution)/shard_map/ppermute | solution.py:21
  179.9 1.2 copy-start.5
  179.9 1.5 copy-start.6
  180.0 1.8 copy-start.7
  194.0 2.8 %copy-start.9 = (pred[4,128,768]{2,1,0:T(8,128)(4,1)S(1)}, pred[4,128,768]{2,1,0:T(8,128)(4,1)}, u32[]{:S(2)}) copy-start(pred[4,128,768]{2,1,0:T(8,128)(4,1)} %compare_and_fusion) | copy-start | bytes 1179652
  196.8 10.1 %copy-start.8 = (bf16[1,4,768,512]{2,3,1,0:T(8,128)(2,1)S(1)}, bf16[1,4,768,512]{2,3,1,0:T(8,128)(2,1)}, u32[]{:S(2)}) copy-start(bf16[1,4,768,512]{2,3,1,0:T(8,128)(2,1)} %copy.100) | copy-start | bytes 9437188
  215.6 31.1 %copy-start.10 = (f32[512]{0:T(512)S(1)}, f32[512]{0:T(512)}, u32[]{:S(2)}) copy-start(f32[512]{0:T(512)} %param.13) | copy-start | bytes 6148
  215.6 31.1 %copy-start.11 = (f32[512]{0:T(512)S(1)}, f32[512]{0:T(512)}, u32[]{:S(2)}) copy-start(f32[512]{0:T(512)} %param.12) | copy-start | bytes 6148
  215.7 33.4 %copy-start.1 = (bf16[3,1024,512]{2,1,0:T(8,128)(2,1)S(1)}, bf16[3,1024,512]{2,1,0:T(8,128)(2,1)}, u32[]{:S(2)}) copy-start(bf16[3,1024,512]{2,1,0:T(8,128)(2,1)} %param.10) | copy-start | bytes 9437188
Sparse Core Ops, SparseCore 0:
  8.9 24.0 all-gather.3
  221.7 18.5 reduce-scatter.1
where the time goes:
time: 257 us; the launch traced here: 256 us
  blocking collectives  97.2 us (38%)
  local copies, waits for them, and re-layouts  43.4 us (17%)
  waiting for transfers between devices  35 us (14%)
  other arithmetic  25 us (10%)
  matrix products  24.7 us (10%)
  starting transfers between devices  17 us (7%)
  between operations  13.7 us (5%)
    all_gather x1, blocking collectives, shards(): all_queries = lax.all_gather(summary_query, 'ctx', axis=0, tiled=True)  64.8 us
    reduce_scatter x1, waiting for transfers between devices, shards(): lax.psum_scatter(partial_value.astype(jnp.bfloat16), 'heads', scatter_dim...  18.7 us
    psum x1, blocking collectives, shards(): lax.psum(totals_all.astype(jnp.bfloat16), 'ctx').astype(jnp.float32)  16.7 us
    all_gather x1, waiting for transfers between devices, shards(): lax.all_gather(own_tokens, 'heads', axis=1, tiled=True)  11.6 us
    pmax x1, blocking collectives, shards(): maxima_all = lax.pmax(maxima_all.reshape(summaries, heads_here), 'ctx')  10.7 us
    sub x1, matrix products, attend(): weights = jnp.where(allowed[:, None], jnp.exp(scores - maxima), 0.0)  10.1 us
    reshape x5, local copies, waits for them, and re-layouts, three_views(): views.append(piece.reshape(new_shape))  7.97 us
    slice x2, local copies, waits for them, and re-layouts, window_step(): key_set[0]  7.1 us
  transfers between devices with their start and end apart: 6, of which 3 were waited for; matrix products, arithmetic and copies ran while one was open for 12% of the time, Pallas kernels for 0%

commit v1 on v0

--- a/solution.py
+++ b/solution.py
@@ -1,6 +1,9 @@
+import functools
 import jax
 import jax.numpy as jnp
 from jax import lax
+from jax.experimental import pallas as pl
+from jax.experimental.pallas import tpu as pltpu
 from jax.sharding import PartitionSpec as P
 
 HEAD = 64
@@ -66,7 +69,7 @@
     return jnp.concatenate(views, axis=axis_pos + 1)
 
 
-def shards(
+def requested(
     tokens, w_qkv, w_out, ln_gain, ln_bias, random_blocks, summary_pos, summary_blocks, pair_lengths
 ):
     tok_rows = tokens.shape[1]
@@ -214,6 +217,473 @@
     return normed.astype(jnp.bfloat16)[None]
 
 
+LANES = 128
+PAIR = LANES // HEAD
+VMEM_LIMIT = 48 * 1024 * 1024
+F32 = jnp.float32
+BF16 = jnp.bfloat16
+NT = (((1,), (1,)), ((), ()))
+
+
+def whole_block(shape):
+    return pl.BlockSpec(shape, lambda *_: (0,) * len(shape))
+
+
+def params(*semantics):
+    return pltpu.CompilerParams(
+        dimension_semantics=semantics or None, vmem_limit_bytes=VMEM_LIMIT
+    )
+
+
+def project_kernel(side_ref, here_ref, there_ref, w_ref, *refs):
+    out_ref = refs[-1]
+    half = here_ref.shape[1]
+    low = pl.multiple_of(side_ref[0] * half, half)
+    high = pl.multiple_of((1 - side_ref[0]) * half, half)
+    product = jnp.dot(here_ref[...], w_ref[0, pl.ds(low, half), :], preferred_element_type=F32)
+    product += jnp.dot(there_ref[...], w_ref[0, pl.ds(high, half), :], preferred_element_type=F32)
+    out_ref[0] = product.astype(BF16)
+
+
+def project(side, here, there, w_qkv, first, total_rows, row_block, held):
+    rows, half = here.shape
+    cols = w_qkv.shape[2]
+    in_specs = [
+        pl.BlockSpec(memory_space=pltpu.SMEM),
+        whole_block((rows, half)),
+        whole_block((rows, half)),
+        pl.BlockSpec((1, 2 * half, cols), lambda j: (j + first, 0, 0)),
+    ]
+    args = [side, here, there, w_qkv]
+    aliases = {}
+    if held is not None:
+        in_specs.append(pl.BlockSpec(memory_space=pl.ANY))
+        args.append(held)
+        aliases = {4: 0}
+    count = 3 - first
+    return pl.pallas_call(
+        project_kernel,
+        grid=(count,),
+        in_specs=in_specs,
+        out_specs=pl.BlockSpec((1, rows, cols), lambda j: (j + first, row_block, 0)),
+        out_shape=jax.ShapeDtypeStruct((3, total_rows, cols), BF16),
+        input_output_aliases=aliases,
+        compiler_params=params("arbitrary"),
+        cost_estimate=pl.CostEstimate(
+            flops=4 * rows * half * cols * count,
+            bytes_accessed=2 * count * (2 * half * cols + rows * cols) + 4 * rows * half,
+            transcendentals=0,
+        ),
+        name="project",
+    )(*args)
+
+
+def segments_of(position, bounds_ref, pair_count):
+    segment = jnp.zeros(position.shape, jnp.int32)
+    for pair in range(pair_count):
+        segment += (position >= bounds_ref[pair]).astype(jnp.int32)
+    return segment
+
+
+def item_bias(query_seg, key_pos, bounds_ref, pair_count):
+    lane = lax.broadcasted_iota(jnp.int32, (1, BLOCK), 1)
+    key_seg = segments_of(key_pos + lane, bounds_ref, pair_count)
+    key_seg = jnp.where(key_pos >= 0, key_seg, -1)
+    return jnp.where(query_seg == key_seg, 0.0, MASKED)
+
+
+def split_heads(pair_queries):
+    lane = lax.broadcasted_iota(jnp.int32, pair_queries.shape, 1)
+    scaled = pair_queries.astype(F32) * HEAD ** (-0.5)
+    low = jnp.where(lane < HEAD, scaled, 0.0)
+    high = jnp.where(lane >= HEAD, scaled, 0.0)
+    return jnp.concatenate([low, high], axis=0).astype(BF16)
+
+
+def join_heads(stacked):
+    rows = stacked.shape[0] // PAIR
+    lane = lax.broadcasted_iota(jnp.int32, (rows, LANES), 1)
+    return jnp.where(lane < HEAD, stacked[:rows], stacked[rows:])
+
+
+def spread_pair(low, high):
+    lane = lax.broadcasted_iota(jnp.int32, (low.shape[0], LANES), 1)
+    return jnp.where(lane < HEAD, low, high)
+
+
+def summary_queries(rows_ref, q_ref, head_count):
+    tok_rows, cols = q_ref.shape
+    row = lax.broadcasted_iota(jnp.int32, (8, tok_rows), 0)
+    col = lax.broadcasted_iota(jnp.int32, (8, tok_rows), 1)
+    chosen = jnp.zeros((8, tok_rows), F32)
+    for u in range(rows_ref.shape[0]):
+        chosen = jnp.where((row == u) & (col == rows_ref[u]), 1.0, chosen)
+    picked = jnp.dot(chosen.astype(BF16), q_ref[...], preferred_element_type=F32)
+    picked = picked * HEAD ** (-0.5)
+    lane = lax.broadcasted_iota(jnp.int32, (8, cols), 1)
+    parts = [
+        jnp.where((lane >= h * HEAD) & (lane < (h + 1) * HEAD), picked, 0.0)
+        for h in range(head_count)
+    ]
+    return jnp.concatenate(parts, axis=0).astype(BF16)
+
+
+def early_kernel(
+    off_ref, pos_ref, bounds_ref, mine_ref, base_ref,
+    q_ref, q_all_ref, k_ref, v_ref, sbias_ref,
+    acc_ref, ml_ref, sacc_ref, sml_ref,
+    bias_ref, *, items, pair_count, head_count,
+):
+    step = pl.program_id(0)
+    row = lax.broadcasted_iota(jnp.int32, (BLOCK, 1), 0)
+    query_seg = segments_of(base_ref[0] + step * BLOCK + row, bounds_ref, pair_count)
+    offsets = []
+    for item in range(items):
+        at = step * items + item
+        offsets.append(pl.multiple_of(off_ref[at], BLOCK))
+        bias = item_bias(query_seg, pos_ref[at], bounds_ref, pair_count)
+        bias_ref[:BLOCK, item * BLOCK : (item + 1) * BLOCK] = bias
+        bias_ref[BLOCK:, item * BLOCK : (item + 1) * BLOCK] = bias
+    lane = lax.broadcasted_iota(jnp.int32, (BLOCK, LANES), 1)
+    state = jnp.zeros((BLOCK, LANES), F32)
+    for pair in range(head_count // PAIR):
+        cols = slice(pair * LANES, (pair + 1) * LANES)
+        stacked = split_heads(q_ref[0, :, cols])
+        scores = [
+            lax.dot_general(
+                stacked, k_ref[0, pl.ds(offsets[i], BLOCK), cols], NT, preferred_element_type=F32
+            )
+            + bias_ref[:, i * BLOCK : (i + 1) * BLOCK]
+            for i in range(items)
+        ]
+        top = functools.reduce(jnp.maximum, scores)
+        top = jnp.max(top, axis=1, keepdims=True)
+        weights = [jnp.exp(s - top) for s in scores]
+        total = jnp.sum(functools.reduce(jnp.add, weights), axis=1, keepdims=True)
+        mixture = functools.reduce(
+            jnp.add,
+            [
+                jnp.dot(
+                    weights[i].astype(BF16),
+                    v_ref[0, pl.ds(offsets[i], BLOCK), cols],
+                    preferred_element_type=F32,
+                )
+                for i in range(items)
+            ],
+        )
+        acc_ref[:, cols] = join_heads(mixture)
+        for j in range(PAIR):
+            h = pair * PAIR + j
+            rows = slice(j * BLOCK, (j + 1) * BLOCK)
+            state = jnp.where(lane == h, top[rows], state)
+            state = jnp.where(lane == head_count + h, total[rows], state)
+    ml_ref[...] = state
+
+    @pl.when(step == 0)
+    def _():
+        queries = summary_queries(mine_ref, q_all_ref.at[0], head_count)
+        keys = k_ref.shape[1]
+        scores = lax.dot_general(queries, k_ref[0], NT, preferred_element_type=F32)
+        scores = scores + jnp.concatenate([sbias_ref[:, :keys]] * head_count, axis=0)
+        top = jnp.max(scores, axis=1, keepdims=True)
+        weights = jnp.exp(scores - top)
+        total = jnp.sum(weights, axis=1, keepdims=True)
+        sacc_ref[...] = jnp.dot(weights.astype(BF16), v_ref[0], preferred_element_type=F32)
+        slane = lax.broadcasted_iota(jnp.int32, sml_ref.shape, 1)
+        sml_ref[...] = jnp.where(slane == 0, top, total)
+
+
+def late_kernel(
+    valid_ref, block_ref, off_ref, pos_ref, bounds_ref, mine_ref, base_ref, side_ref,
+    q_ref, q_all_ref, k_ref, v_ref, sbias_ref, acc_ref, ml_ref, sacc_ref, sml_ref, w_ref,
+    own_ref, other_ref,
+    mix_ref, state_ref, sum_ref, *, items, pair_count, head_count, early_keys,
+):
+    step = pl.program_id(0)
+    cols_all = head_count * HEAD
+    lane = lax.broadcasted_iota(jnp.int32, (BLOCK, LANES), 1)
+
+    @pl.when(step == 0)
+    def _():
+        queries = summary_queries(mine_ref, q_all_ref.at[0], head_count)
+        scores = lax.dot_general(queries, k_ref[0], NT, preferred_element_type=F32)
+        scores = scores + jnp.concatenate([sbias_ref[:, early_keys:]] * head_count, axis=0)
+        before = sml_ref[:, 0:1]
+        top = jnp.maximum(before, jnp.max(scores, axis=1, keepdims=True))
+        weights = jnp.exp(scores - top)
+        fade = jnp.exp(before - top)
+        total = sml_ref[:, 1:2] * fade + jnp.sum(weights, axis=1, keepdims=True)
+        mixture = sacc_ref[...] * fade + jnp.dot(
+            weights.astype(BF16), v_ref[0], preferred_element_type=F32
+        )
+        mixture = mixture / total
+        slane = lax.broadcasted_iota(jnp.int32, (8, cols_all), 1)
+        joined = jnp.zeros((8, cols_all), F32)
+        for h in range(head_count):
+            joined = jnp.where(
+                (slane >= h * HEAD) & (slane < (h + 1) * HEAD), mixture[h * 8 : (h + 1) * 8], joined
+            )
+        sum_ref[...] = joined
+
+    mix_ref[...] = acc_ref[...]
+    state_ref[...] = ml_ref[...]
+    row = lax.broadcasted_iota(jnp.int32, (BLOCK, 1), 0)
+    query_seg = segments_of(base_ref[0] + step * BLOCK + row, bounds_ref, pair_count)
+    for item in range(items):
+
+        @pl.when((valid_ref[item] == 1) & (block_ref[item] == step))
+        def _():
+            offset = pl.multiple_of(off_ref[item], BLOCK)
+            bias = item_bias(query_seg, pos_ref[item], bounds_ref, pair_count)
+            bias = jnp.concatenate([bias] * PAIR, axis=0)
+            state = state_ref[...]
+            fresh = state
+            for pair in range(head_count // PAIR):
+                cols = slice(pair * LANES, (pair + 1) * LANES)
+                heads = [pair * PAIR + j for j in range(PAIR)]
+                scores = (
+                    lax.dot_general(
+                        split_heads(q_ref[0, :, cols]),
+                        k_ref[0, pl.ds(offset, BLOCK), cols],
+                        NT,
+                        preferred_element_type=F32,
+                    )
+                    + bias
+                )
+                before = jnp.concatenate([state[:, h : h + 1] for h in heads], axis=0)
+                count = jnp.concatenate(
+                    [state[:, head_count + h : head_count + h + 1] for h in heads], axis=0
+                )
+                top = jnp.maximum(before, jnp.max(scores, axis=1, keepdims=True))
+                weights = jnp.exp(scores - top)
+                fade = jnp.exp(before - top)
+                total = count * fade + jnp.sum(weights, axis=1, keepdims=True)
+                mixture = jnp.dot(
+                    weights.astype(BF16),
+                    v_ref[0, pl.ds(offset, BLOCK), cols],
+                    preferred_element_type=F32,
+                )
+                mix_ref[:, cols] = mix_ref[:, cols] * spread_pair(
+                    fade[:BLOCK], fade[BLOCK:]
+                ) + join_heads(mixture)
+                for j, h in enumerate(heads):
+                    rows = slice(j * BLOCK, (j + 1) * BLOCK)
+                    fresh = jnp.where(lane == h, top[rows], fresh)
+                    fresh = jnp.where(lane == head_count + h, total[rows], fresh)
+            state_ref[...] = fresh
+
+    state = state_ref[...]
+    for pair in range(head_count // PAIR):
+        cols = slice(pair * LANES, (pair + 1) * LANES)
+        h = head_count + pair * PAIR
+        totals = spread_pair(state[:, h : h + 1], state[:, h + 1 : h + 2])
+        mix_ref[:, cols] = mix_ref[:, cols] / totals
+    attention = mix_ref[...]
+    here = step * BLOCK + row
+    for u in range(mine_ref.shape[0]):
+        attention = jnp.where(here == mine_ref[u], sum_ref[u : u + 1, :], attention)
+    attention = attention.astype(BF16)
+    half = w_ref.shape[1] // 2
+    low = pl.multiple_of(side_ref[0] * half, half)
+    high = pl.multiple_of((1 - side_ref[0]) * half, half)
+    own_ref[...] = jnp.dot(
+        attention, w_ref[:, pl.ds(low, half)], preferred_element_type=F32
+    ).astype(BF16)
+    other_ref[...] = jnp.dot(
+        attention, w_ref[:, pl.ds(high, half)], preferred_element_type=F32
+    ).astype(BF16)
+
+
+def gathered(
+    tokens, w_qkv, w_out, ln_gain, ln_bias, random_blocks, summary_pos, summary_blocks, pair_lengths
+):
+    tok_rows, half = tokens.shape[1:]
+    cols = w_qkv.shape[2]
+    head_count = cols // HEAD
+    full_width = w_out.shape[1]
+    ctx_count = lax.axis_size("ctx")
+    ctx_index = lax.axis_index("ctx")
+    side = lax.axis_index("heads").astype(jnp.int32).reshape(1)
+    block_count = tok_rows // BLOCK
+    total_blocks = block_count * ctx_count
+    pair_count = pair_lengths.shape[1]
+    own_tokens = tokens[0]
+    swap = [(0, 1), (1, 0)]
+    last = ctx_count - 1
+
+    def other_half(x):
+        return lax.ppermute(x, "heads", swap)
+
+    def from_slot(x, slot):
+        return lax.ppermute(x, "ctx", [(i, i ^ slot) for i in range(ctx_count)])
+
+    bounds = jnp.cumsum(pair_lengths[0]).astype(jnp.int32)
+    base = (ctx_index * tok_rows).astype(jnp.int32).reshape(1)
+    picks = random_blocks[0]
+    rand_count = picks.shape[1]
+    block_ids = ctx_index * block_count + jnp.arange(block_count, dtype=jnp.int32)
+    window = block_ids[:, None] + jnp.arange(-1, 2, dtype=jnp.int32)[None, :]
+    listed = jnp.concatenate([window, picks], axis=1)
+    inside = (listed >= 0) & (listed < total_blocks)
+    slot_of = (listed // block_count) ^ ctx_index
+    within = listed % block_count
+    early = inside & (slot_of != last)
+    items = listed.shape[1]
+    early_off = jnp.where(early, (slot_of * block_count + within) * BLOCK, 0).reshape(-1)
+    early_pos = jnp.where(early, listed * BLOCK, -(2**30)).reshape(-1)
+    late = (inside & (slot_of == last)).reshape(-1)
+    pick_count = block_count * rand_count
+    late_items = min(max(2, -(-pick_count // ctx_count)) + 2, block_count * items)
+    rank = jnp.cumsum(late.astype(jnp.int32)) - 1
+    place = late[None, :] & (rank[None, :] == jnp.arange(late_items, dtype=jnp.int32)[:, None])
+
+    def compact(x):
+        return jnp.sum(jnp.where(place, x.reshape(-1)[None, :], 0), axis=1).astype(jnp.int32)
+
+    late_valid = jnp.any(place, axis=1).astype(jnp.int32)
+    late_block = compact(jnp.broadcast_to(jnp.arange(block_count)[:, None], listed.shape))
+    late_off = compact(within * BLOCK)
+    late_pos = compact(listed * BLOCK)
+    summaries = summary_pos.shape[1]
+    per_device = summaries // ctx_count
+    mine_pos = lax.dynamic_slice_in_dim(summary_pos[0], ctx_index * per_device, per_device, 0)
+    mine_lists = lax.dynamic_slice_in_dim(summary_blocks[0], ctx_index * per_device, per_device, 0)
+    mine = (mine_pos - ctx_index * tok_rows).astype(jnp.int32)
+    slot_blocks = (
+        (jnp.arange(ctx_count, dtype=jnp.int32) ^ ctx_index)[:, None] * block_count
+        + jnp.arange(block_count, dtype=jnp.int32)
+    ).reshape(-1)
+    in_list = jnp.any(mine_lists[:, :, None] == slot_blocks[None, None, :], axis=1)
+    slot_pos = (slot_blocks[:, None] * BLOCK + jnp.arange(BLOCK, dtype=jnp.int32)).reshape(-1)
+    seen = jnp.repeat(in_list, BLOCK, axis=1) & (
+        segment_ids(slot_pos, bounds)[None, :] == segment_ids(mine_pos, bounds)[:, None]
+    )
+    sbias = jnp.pad(jnp.where(seen, 0.0, MASKED), ((0, 8 - per_device), (0, 0)))
+
+    there = [other_half(own_tokens)]
+    here = [own_tokens]
+    for slot in range(1, last):
+        here.append(from_slot(own_tokens, slot))
+        there.append(other_half(here[-1]))
+    split = 2
+    piece = tok_rows // split
+    late_here = [from_slot(own_tokens[i * piece : (i + 1) * piece], last) for i in range(split)]
+    late_there = [other_half(x) for x in late_here]
+
+    early_rows = last * tok_rows
+    held = project(side, here[0], there[0], w_qkv, 0, early_rows, 0, None)
+    for slot in range(1, last):
+        held = project(side, here[slot], there[slot], w_qkv, 1, early_rows, slot, held)
+    late_held = None
+    for i in range(split):
+        late_held = project(side, late_here[i], late_there[i], w_qkv, 1, tok_rows, i, late_held)
+
+    smem = pl.BlockSpec(memory_space=pltpu.SMEM)
+    rows_spec = pl.BlockSpec((BLOCK, cols), lambda i: (i, 0))
+    ml_spec = pl.BlockSpec((BLOCK, LANES), lambda i: (i, 0))
+    q_spec = pl.BlockSpec((1, BLOCK, cols), lambda i: (0, i, 0))
+    q_all_spec = pl.BlockSpec((1, tok_rows, cols), lambda i: (0, 0, 0))
+
+    def kv_spec(j, rows):
+        return pl.BlockSpec((1, rows, cols), lambda i: (j, 0, 0))
+
+    srows = 8 * head_count
+    acc, ml, sacc, sml = pl.pallas_call(
+        functools.partial(
+            early_kernel, items=items, pair_count=pair_count, head_count=head_count
+        ),
+        grid=(block_count,),
+        in_specs=[smem] * 5
+        + [
+            q_spec,
+            q_all_spec,
+            kv_spec(1, early_rows),
+            kv_spec(2, early_rows),
+            whole_block(sbias.shape),
+        ],
+        out_specs=[rows_spec, ml_spec, whole_block((srows, cols)), whole_block((srows, LANES))],
+        out_shape=[
+            jax.ShapeDtypeStruct((tok_rows, cols), F32),
+            jax.ShapeDtypeStruct((tok_rows, LANES), F32),
+            jax.ShapeDtypeStruct((srows, cols), F32),
+            jax.ShapeDtypeStruct((srows, LANES), F32),
+        ],
+        scratch_shapes=[pltpu.VMEM((PAIR * BLOCK, items * BLOCK), F32)],
+        compiler_params=params("arbitrary"),
+        cost_estimate=pl.CostEstimate(
+            flops=8 * tok_rows * items * BLOCK * cols,
+            bytes_accessed=4 * early_rows * cols + 8 * tok_rows * cols,
+            transcendentals=tok_rows * items * BLOCK * head_count,
+        ),
+        name="early_attention",
+    )(early_off, early_pos, bounds, mine, base, held, held, held, held, sbias)
+
+    own_term, other_term = pl.pallas_call(
+        functools.partial(
+            late_kernel,
+            items=late_items,
+            pair_count=pair_count,
+            head_count=head_count,
+            early_keys=early_rows,
+        ),
+        grid=(block_count,),
+        in_specs=[smem] * 8
+        + [
+            q_spec,
+            q_all_spec,
+            kv_spec(1, tok_rows),
+            kv_spec(2, tok_rows),
+            whole_block(sbias.shape),
+            rows_spec,
+            ml_spec,
+            whole_block((srows, cols)),
+            whole_block((srows, LANES)),
+            whole_block(w_out.shape),
+        ],
+        out_specs=[pl.BlockSpec((BLOCK, half), lambda i: (i, 0))] * 2,
+        out_shape=[jax.ShapeDtypeStruct((tok_rows, half), BF16)] * 2,
+        scratch_shapes=[
+            pltpu.VMEM((BLOCK, cols), F32),
+            pltpu.VMEM((BLOCK, LANES), F32),
+            pltpu.VMEM((8, cols), F32),
+        ],
+        compiler_params=params("arbitrary"),
+        cost_estimate=pl.CostEstimate(
+            flops=4 * tok_rows * cols * full_width,
+            bytes_accessed=12 * tok_rows * cols,
+            transcendentals=late_items * BLOCK * BLOCK * head_count,
+        ),
+        name="late_attention",
+    )(
+        late_valid, late_block, late_off, late_pos, bounds, mine, base, side,
+        held, held, late_held, late_held, sbias, acc, ml, sacc, sml, w_out,
+    )
+
+    received = other_half(other_term)
+    hidden = own_tokens.astype(F32) + (own_term.astype(F32) + received.astype(F32))
+    sums = jnp.stack([jnp.sum(hidden, axis=1), jnp.sum(hidden * hidden, axis=1)])
+    sums = sums + other_half(sums)
+    row_mean = sums[0] / full_width
+    row_var = sums[1] / full_width - row_mean * row_mean
+    normed = (hidden - row_mean[:, None]) * lax.rsqrt(row_var + 1e-05)[:, None] * ln_gain + ln_bias
+    return normed.astype(BF16)[None]
+
+
+def shards(*arrays):
+    tokens, w_qkv, random_blocks = arrays[0], arrays[1], arrays[5]
+    ctx_count = lax.axis_size("ctx")
+    picked = random_blocks.shape[1] * random_blocks.shape[2]
+    if (
+        lax.axis_size("heads") == 2
+        and 2 <= ctx_count <= picked
+        and ctx_count & (ctx_count - 1) == 0
+        and w_qkv.shape[2] % LANES == 0
+        and arrays[6].shape[1] // ctx_count <= 8
+    ):
+        return gathered(*arrays)
+    return requested(*arrays)
+
+
 def solution(mesh):
     in_specs = (
         P(("groups", "dp"), "ctx", "heads"),

time: 257 us -> 117 us (0.46)
  the two profiles are of different devices: /device:TPU:0 before, /device:TPU:8 now
where the time goes in v1:
time: 117 us
  waiting for transfers between devices  66.5 us (57%)
  Pallas kernels  29.4 us (25%)
  starting transfers between devices  11.8 us (10%)
  other arithmetic  4.34 us (4%)
  local copies, waits for them, and re-layouts  4.33 us (4%)
    ppermute x4, waiting for transfers between devices, from_slot(): return lax.ppermute(x, 'ctx', [(i, i ^ slot) for i in range(ctx_count)])  36.4 us
    ppermute x7, waiting for transfers between devices, other_half(): return lax.ppermute(x, 'heads', swap)  30.1 us
    pallas_call x1, Pallas kernels, gathered(): pl.pallas_call(functools.partial(late_kernel, items=late_items, pair_coun...  10.4 us
    pallas_call x1, Pallas kernels, gathered(): pl.pallas_call(functools.partial(early_kernel, items=items, pair_count=pa...  9.73 us
    pallas_call x5, Pallas kernels, project(): pl.pallas_call(project_kernel, grid=(count,), in_specs=in_specs, out_spec...  9.28 us
    ppermute x7, starting transfers between devices, other_half(): return lax.ppermute(x, 'heads', swap)  6.65 us
    ppermute x4, starting transfers between devices, from_slot(): return lax.ppermute(x, 'ctx', [(i, i ^ slot) for i in range(ctx_count)])  5.13 us
    unnamed x16, local copies, waits for them, and re-layouts  2.77 us
  transfers between devices with their start and end apart: 11, of which 7 were waited for; matrix products, arithmetic and copies ran while one was open for 4% of the time, Pallas kernels for 6%

profile of v1, /device:TPU:8, one launch (start us, length us, event | category | flops | bytes accessed | tf_op | source)
XLA Modules:
  0.0 116.6 jit_solution(11981760477831337883)
XLA Ops:
  0.0 1.5 %collective-permute-start.4 = (bf16[512,512]{1,0:T(8,128)(2,1)}, bf16[512,512]{1,0:T(8,128)(2,1)S(1)}, u32[]{:S(2)}, u32[]{:S(2)}) collective-permute-start(bf16[512,512]{1,0:T(8,128)(2,1)} %bitcast.31), channel_id=1, source_target_pairs={{0,2},{2,0},{1,3},{3,1},{4,6},{6,4},{5,7},{7,5},{8,10},{10,8},{9,1... | collective-permute-start | bytes 1572872 | tf_op jit(solution)/shard_map/ppermute | solution.py:515
  1.9 2.6 %collective-permute-start = (bf16[512,512]{1,0:T(8,128)(2,1)}, bf16[512,512]{1,0:T(8,128)(2,1)S(1)}, u32[]{:S(2)}, u32[]{:S(2)}) collective-permute-start(bf16[512,512]{1,0:T(8,128)(2,1)} %bitcast.33), channel_id=1, source_target_pairs={{0,8},{4,12},{8,0},{12,4},{1,9},{5,13},{9,1},{13,5},{2,10},{6,14},... | collective-permute-start | bytes 1572872 | tf_op jit(solution)/shard_map/ppermute | solution.py:518
  4.5 1.1 slice_bitcast_fusion
  6.1 1.6 %collective-permute-start.5 = (bf16[256,512]{1,0:T(8,128)(2,1)S(1)}, bf16[256,512]{1,0:T(8,128)(2,1)S(1)}, u32[]{:S(2)}, u32[]{:S(2)}) collective-permute-start(bf16[256,512]{1,0:T(8,128)(2,1)S(1)} %get-tuple-element.28), channel_id=1, source_target_pairs={{0,12},{4,8},{8,4},{12,0},{1,13},{5,9},{9,5},{13,1},{2,14},{6,10},... | collective-permute-start | bytes 786440 | tf_op jit(solution)/shard_map/ppermute | solution.py:518
  7.7 0.8 copy.29
  8.8 0.8 reduce-window.17
  10.2 0.7 broadcast_subtract_fusion
  11.4 34.7 %collective-permute-done.7.here_ref = bf16[256,512]{1,0:T(8,128)(2,1)S(1)} collective-permute-done((bf16[256,512]{1,0:T(8,128)(2,1)S(1)}, bf16[256,512]{1,0:T(8,128)(2,1)S(1)}, u32[]{:S(2)}, u32[]{:S(2)}) %collective-permute-start.7) | collective-permute-done | bytes 262176 | tf_op jit(solution)/shard_map/ppermute | solution.py:518
  46.7 1.5 %collective-permute-start.3 = (bf16[512,512]{1,0:T(8,128)(2,1)S(1)}, bf16[512,512]{1,0:T(8,128)(2,1)S(1)}, u32[]{:S(2)}, u32[]{:S(2)}) collective-permute-start(bf16[512,512]{1,0:T(8,128)(2,1)S(1)} %collective-permute-done.2.here_ref), channel_id=1, source_target_pairs={{0,2},{2,0},{1,3},{3,1},{4,6},{6,4},{5,7},{7,5},{8,10},{10,8},{9,1... | collective-permute-start | bytes 1572872 | tf_op jit(solution)/shard_map/ppermute | solution.py:515
  48.4 1.7 %collective-permute-done.5.here_ref = bf16[256,512]{1,0:T(8,128)(2,1)S(1)} collective-permute-done((bf16[256,512]{1,0:T(8,128)(2,1)S(1)}, bf16[256,512]{1,0:T(8,128)(2,1)S(1)}, u32[]{:S(2)}, u32[]{:S(2)}) %collective-permute-start.5) | collective-permute-done | bytes 262176 | tf_op jit(solution)/shard_map/ppermute | solution.py:518
  50.6 1.5 %collective-permute-start.1 = (bf16[512,512]{1,0:T(8,128)(2,1)S(1)}, bf16[512,512]{1,0:T(8,128)(2,1)S(1)}, u32[]{:S(2)}, u32[]{:S(2)}) collective-permute-start(bf16[512,512]{1,0:T(8,128)(2,1)S(1)} %collective-permute-done.here_ref), channel_id=1, source_target_pairs={{0,2},{2,0},{1,3},{3,1},{4,6},{6,4},{5,7},{7,5},{8,10},{10,8},{9,1... | collective-permute-start | bytes 1572872 | tf_op jit(solution)/shard_map/ppermute | solution.py:515
  52.4 3.0 %collective-permute-done.8.there_ref = bf16[256,512]{1,0:T(8,128)(2,1)S(1)} collective-permute-done((bf16[256,512]{1,0:T(8,128)(2,1)S(1)}, bf16[256,512]{1,0:T(8,128)(2,1)S(1)}, u32[]{:S(2)}, u32[]{:S(2)}) %collective-permute-start.8) | collective-permute-done | bytes 262176 | tf_op jit(solution)/shard_map/ppermute | solution.py:515
  55.4 1.9 %copy-done.1 = bf16[3,1024,512]{2,1,0:T(8,128)(2,1)S(1)} copy-done((bf16[3,1024,512]{2,1,0:T(8,128)(2,1)S(1)}, bf16[3,1024,512]{2,1,0:T(8,128)(2,1)}, u32[]{:S(2)}) %copy-start.1) | copy-done | bytes 3145752
  57.3 0.9 project.8.refs_0_
  58.2 14.0 %collective-permute-done.6.there_ref = bf16[256,512]{1,0:T(8,128)(2,1)S(1)} collective-permute-done((bf16[256,512]{1,0:T(8,128)(2,1)S(1)}, bf16[256,512]{1,0:T(8,128)(2,1)S(1)}, u32[]{:S(2)}, u32[]{:S(2)}) %collective-permute-start.6) | collective-permute-done | bytes 262176 | tf_op jit(solution)/shard_map/ppermute | solution.py:515
  72.2 0.9 project.9.k_ref.v_ref
  73.1 3.0 %project.5.refs_0_ = bf16[3,1536,512]{2,1,0:T(8,128)(2,1)} custom-call(s32[1]{0:T(128)} %bitcast.6.side_ref, bf16[512,512]{1,0:T(8,128)(2,1)S(1)} %bitcast.34, bf16[512,512]{1,0:T(8,128)(2,1)S(1)} %collective-permute-done.4.there_ref, bf16[3,1024,512]{2,1,0:T(8,128)(2,1)S(1)} %copy-done.2), custom_call_target="tpu_custom_call" | custom-call | flops 1610612736 | bytes 5767168 | tf_op jit(solution)/shard_map/project/pallas_call | solution.py:264
  76.2 2.2 %project.6.refs_0_ = bf16[3,1536,512]{2,1,0:T(8,128)(2,1)} custom-call(s32[1]{0:T(128)} %bitcast.6.side_ref, bf16[512,512]{1,0:T(8,128)(2,1)S(1)} %collective-permute-done.2.here_ref, bf16[512,512]{1,0:T(8,128)(2,1)S(1)} %collective-permute-done.3.there_ref, bf16[3,1024,512]{2,1,0:T(8,128)(2,1)S(1)} %copy-done.2, ...), custom_call_target="tpu_custom_call", output_to_operand_aliasing={{}: (4, {})} | custom-call | flops 1073741824 | bytes 4194304 | tf_op jit(solution)/shard_map/project/pallas_call | solution.py:264
  79.1 2.2 %project.7.q_ref.q_all_ref.k_ref.v_ref = bf16[3,1536,512]{2,1,0:T(8,128)(2,1)} custom-call(s32[1]{0:T(128)} %bitcast.6.side_ref, bf16[512,512]{1,0:T(8,128)(2,1)S(1)} %collective-permute-done.here_ref, bf16[512,512]{1,0:T(8,128)(2,1)S(1)} %collective-permute-done.1.there_ref, bf16[3,1024,512]{2,1,0:T(8,128)(2,1)S(1)} %copy-done.2, ...), custom_call_target="tpu_custom_call", output_to_operand_aliasing={{}: (4, {})} | custom-call | flops 1073741824 | bytes 4194304 | tf_op jit(solution)/shard_map/project/pallas_call | solution.py:264
  81.4 9.7 %early_attention.1 = (f32[512,512]{1,0:T(8,128)S(1)}, f32[512,128]{1,0:T(8,128)S(1)}, f32[64,512]{1,0:T(8,128)S(1)}, f32[64,128]{1,0:T(8,128)S(1)}) custom-call(s32[24]{0:T(128)S(1)} %get-tuple-element.31.off_ref, s32[24]{0:T(128)S(1)} %get-tuple-element.22.pos_ref, s32[4]{0:T(128)S(1)} %bitcast.37, s32[4]{0:T(128)S(1)} %get-tuple-element.25.mine_ref, ...), custom_call_target="tpu_custom_call" | custom-call | flops 1610612736 | bytes 5242880 | tf_op jit(solution)/shard_map/early_attention/pallas_call | solution.py:591
  91.1 10.4 %late_attention.1 = (bf16[512,512]{1,0:T(8,128)(2,1)S(1)}, bf16[512,512]{1,0:T(8,128)(2,1)S(1)}) custom-call(s32[5]{0:T(128)S(1)} %convert_element_type.37.valid_ref, s32[5]{0:T(128)S(1)} %get-tuple-element.21.block_ref, s32[5]{0:T(128)S(1)} %get-tuple-element.20.off_ref, s32[5]{0:T(128)S(1)} %get-tuple-element.19.pos_ref, s32[4]{0:T(128)S(1)} %bitcast.38, ...), custom_call_target="tpu_custom_call" | custom-call | flops 1073741824 | bytes 3145728 | tf_op jit(solution)/shard_map/late_attention/pallas_call | solution.py:621
  102.1 9.2 %collective-permute-done.9 = bf16[512,512]{1,0:T(8,128)(2,1)S(1)} collective-permute-done((bf16[512,512]{1,0:T(8,128)(2,1)S(1)}, bf16[512,512]{1,0:T(8,128)(2,1)S(1)}, u32[]{:S(2)}, u32[]{:S(2)}) %collective-permute-start.9) | collective-permute-done | bytes 524320 | tf_op jit(solution)/shard_map/ppermute | solution.py:515
  112.2 3.1 %collective-permute-done.10 = f32[2,512]{1,0:T(2,128)S(1)} collective-permute-done((f32[2,512]{1,0:T(2,128)S(1)}, f32[2,512]{1,0:T(2,128)S(1)}, u32[]{:S(2)}, u32[]{:S(2)}) %collective-permute-start.10) | collective-permute-done | bytes 4128 | tf_op jit(solution)/shard_map/ppermute | solution.py:515
  115.4 1.1 fusion
  (59 shorter events, 6.1 us)
Async XLA Ops:
  0.0 9.6 %copy-start = (s32[1,16,8]{1,2,0:T(8,128)S(1)}, s32[1,16,8]{1,2,0:T(8,128)}, u32[]{:S(2)}) copy-start(s32[1,16,8]{1,2,0:T(8,128)} %param.16) | copy-start | bytes 1540
  0.0 73.1 %collective-permute-start.4 = (bf16[512,512]{1,0:T(8,128)(2,1)}, bf16[512,512]{1,0:T(8,128)(2,1)S(1)}, u32[]{:S(2)}, u32[]{:S(2)}) collective-permute-start(bf16[512,512]{1,0:T(8,128)(2,1)} %bitcast.31), channel_id=1, source_target_pairs={{0,2},{2,0},{1,3},{3,1},{4,6},{6,4},{5,7},{7,5},{8,10},{10,8},{9,1... | collective-permute-start | bytes 1572872 | tf_op jit(solution)/shard_map/ppermute | solution.py:515
  1.5 45.2 %collective-permute-start.2 = (bf16[512,512]{1,0:T(8,128)(2,1)}, bf16[512,512]{1,0:T(8,128)(2,1)S(1)}, u32[]{:S(2)}, u32[]{:S(2)}) collective-permute-start(bf16[512,512]{1,0:T(8,128)(2,1)} %bitcast.32), channel_id=1, source_target_pairs={{0,4},{4,0},{8,12},{12,8},{1,5},{5,1},{9,13},{13,9},{2,6},{6,2},{1... | collective-permute-start | bytes 1572872 | tf_op jit(solution)/shard_map/ppermute | solution.py:518
  1.9 48.6 %collective-permute-start = (bf16[512,512]{1,0:T(8,128)(2,1)}, bf16[512,512]{1,0:T(8,128)(2,1)S(1)}, u32[]{:S(2)}, u32[]{:S(2)}) collective-permute-start(bf16[512,512]{1,0:T(8,128)(2,1)} %bitcast.33), channel_id=1, source_target_pairs={{0,8},{4,12},{8,0},{12,4},{1,9},{5,13},{9,1},{13,5},{2,10},{6,14},... | collective-permute-start | bytes 1572872 | tf_op jit(solution)/shard_map/ppermute | solution.py:518
  5.6 40.5 %collective-permute-start.7 = (bf16[256,512]{1,0:T(8,128)(2,1)S(1)}, bf16[256,512]{1,0:T(8,128)(2,1)S(1)}, u32[]{:S(2)}, u32[]{:S(2)}) collective-permute-start(bf16[256,512]{1,0:T(8,128)(2,1)S(1)} %get-tuple-element.27), channel_id=1, source_target_pairs={{0,12},{4,8},{8,4},{12,0},{1,13},{5,9},{9,5},{13,1},{2,14},{6,10},... | collective-permute-start | bytes 786440 | tf_op jit(solution)/shard_map/ppermute | solution.py:518
  6.1 43.9 %collective-permute-start.5 = (bf16[256,512]{1,0:T(8,128)(2,1)S(1)}, bf16[256,512]{1,0:T(8,128)(2,1)S(1)}, u32[]{:S(2)}, u32[]{:S(2)}) collective-permute-start(bf16[256,512]{1,0:T(8,128)(2,1)S(1)} %get-tuple-element.28), channel_id=1, source_target_pairs={{0,12},{4,8},{8,4},{12,0},{1,13},{5,9},{9,5},{13,1},{2,14},{6,10},... | collective-permute-start | bytes 786440 | tf_op jit(solution)/shard_map/ppermute | solution.py:518
  46.1 9.2 %collective-permute-start.8 = (bf16[256,512]{1,0:T(8,128)(2,1)S(1)}, bf16[256,512]{1,0:T(8,128)(2,1)S(1)}, u32[]{:S(2)}, u32[]{:S(2)}) collective-permute-start(bf16[256,512]{1,0:T(8,128)(2,1)S(1)} %collective-permute-done.7.here_ref), channel_id=1, source_target_pairs={{0,2},{2,0},{1,3},{3,1},{4,6},{6,4},{5,7},{7,5},{8,10},{10,8},{9,1... | collective-permute-start | bytes 786440 | tf_op jit(solution)/shard_map/ppermute | solution.py:515
  46.7 29.5 %collective-permute-start.3 = (bf16[512,512]{1,0:T(8,128)(2,1)S(1)}, bf16[512,512]{1,0:T(8,128)(2,1)S(1)}, u32[]{:S(2)}, u32[]{:S(2)}) collective-permute-start(bf16[512,512]{1,0:T(8,128)(2,1)S(1)} %collective-permute-done.2.here_ref), channel_id=1, source_target_pairs={{0,2},{2,0},{1,3},{3,1},{4,6},{6,4},{5,7},{7,5},{8,10},{10,8},{9,1... | collective-permute-start | bytes 1572872 | tf_op jit(solution)/shard_map/ppermute | solution.py:515
  50.0 22.2 %collective-permute-start.6 = (bf16[256,512]{1,0:T(8,128)(2,1)S(1)}, bf16[256,512]{1,0:T(8,128)(2,1)S(1)}, u32[]{:S(2)}, u32[]{:S(2)}) collective-permute-start(bf16[256,512]{1,0:T(8,128)(2,1)S(1)} %collective-permute-done.5.here_ref), channel_id=1, source_target_pairs={{0,2},{2,0},{1,3},{3,1},{4,6},{6,4},{5,7},{7,5},{8,10},{10,8},{9,1... | collective-permute-start | bytes 786440 | tf_op jit(solution)/shard_map/ppermute | solution.py:515
  50.6 28.6 %collective-permute-start.1 = (bf16[512,512]{1,0:T(8,128)(2,1)S(1)}, bf16[512,512]{1,0:T(8,128)(2,1)S(1)}, u32[]{:S(2)}, u32[]{:S(2)}) collective-permute-start(bf16[512,512]{1,0:T(8,128)(2,1)S(1)} %collective-permute-done.here_ref), channel_id=1, source_target_pairs={{0,2},{2,0},{1,3},{3,1},{4,6},{6,4},{5,7},{7,5},{8,10},{10,8},{9,1... | collective-permute-start | bytes 1572872 | tf_op jit(solution)/shard_map/ppermute | solution.py:515
  55.4 1.9 %copy-start.1 = (bf16[3,1024,512]{2,1,0:T(8,128)(2,1)S(1)}, bf16[3,1024,512]{2,1,0:T(8,128)(2,1)}, u32[]{:S(2)}) copy-start(bf16[3,1024,512]{2,1,0:T(8,128)(2,1)} %w_ref.10) | copy-start | bytes 9437188
  58.2 15.0 %copy-start.2 = (bf16[3,1024,512]{2,1,0:T(8,128)(2,1)S(1)}, bf16[3,1024,512]{2,1,0:T(8,128)(2,1)}, u32[]{:S(2)}) copy-start(bf16[3,1024,512]{2,1,0:T(8,128)(2,1)} %w_ref.10) | copy-start | bytes 9437188
  58.2 15.0 %copy-start.3 = (bf16[1,512,512]{2,1,0:T(8,128)(2,1)S(1)}, bf16[1,512,512]{2,1,0:T(8,128)(2,1)}, u32[]{:S(2)}) copy-start(bf16[1,512,512]{2,1,0:T(8,128)(2,1)} %param.9) | copy-start | bytes 1572868
  81.4 9.7 %copy-start.4 = (bf16[512,1024]{1,0:T(8,128)(2,1)S(1)}, bf16[512,1024]{1,0:T(8,128)(2,1)}, u32[]{:S(2)}) copy-start(bf16[512,1024]{1,0:T(8,128)(2,1)} %w_ref.11) | copy-start | bytes 3145732
  91.1 24.3 %copy-start.5 = (f32[512]{0:T(512)S(1)}, f32[512]{0:T(512)}, u32[]{:S(2)}) copy-start(f32[512]{0:T(512)} %param.13) | copy-start | bytes 6148
  91.1 24.3 %copy-start.6 = (f32[512]{0:T(512)S(1)}, f32[512]{0:T(512)}, u32[]{:S(2)}) copy-start(f32[512]{0:T(512)} %param.12) | copy-start | bytes 6148
  101.6 9.7 %collective-permute-start.9 = (bf16[512,512]{1,0:T(8,128)(2,1)S(1)}, bf16[512,512]{1,0:T(8,128)(2,1)S(1)}, u32[]{:S(2)}, u32[]{:S(2)}) collective-permute-start(bf16[512,512]{1,0:T(8,128)(2,1)S(1)} %get-tuple-element.16), channel_id=1, source_target_pairs={{0,2},{2,0},{1,3},{3,1},{4,6},{6,4},{5,7},{7,5},{8,10},{10,8},{9,1... | collective-permute-start | bytes 1572872 | tf_op jit(solution)/shard_map/ppermute | solution.py:515
  111.7 3.7 %collective-permute-start.10 = (f32[2,512]{1,0:T(2,128)S(1)}, f32[2,512]{1,0:T(2,128)S(1)}, u32[]{:S(2)}, u32[]{:S(2)}) collective-permute-start(f32[2,512]{1,0:T(2,128)S(1)} %pad_maximum_fusion), channel_id=1, source_target_pairs={{0,2},{2,0},{1,3},{3,1},{4,6},{6,4},{5,7},{7,5},{8,10},{10,8},{9,1... | collective-permute-start | bytes 12296 | tf_op jit(solution)/shard_map/ppermute | solution.py:515

commit v2 on v1

--- a/solution.py
+++ b/solution.py
@@ -331,7 +331,7 @@
 def early_kernel(
     off_ref, pos_ref, bounds_ref, mine_ref, base_ref,
     q_ref, q_all_ref, k_ref, v_ref, sbias_ref,
-    acc_ref, ml_ref, sacc_ref, sml_ref,
+    acc_ref, ml_ref, sacc_ref, sml_ref, squery_ref,
     bias_ref, *, items, pair_count, head_count,
 ):
     step = pl.program_id(0)
@@ -349,28 +349,13 @@
     for pair in range(head_count // PAIR):
         cols = slice(pair * LANES, (pair + 1) * LANES)
         stacked = split_heads(q_ref[0, :, cols])
-        scores = [
-            lax.dot_general(
-                stacked, k_ref[0, pl.ds(offsets[i], BLOCK), cols], NT, preferred_element_type=F32
-            )
-            + bias_ref[:, i * BLOCK : (i + 1) * BLOCK]
-            for i in range(items)
-        ]
-        top = functools.reduce(jnp.maximum, scores)
-        top = jnp.max(top, axis=1, keepdims=True)
-        weights = [jnp.exp(s - top) for s in scores]
-        total = jnp.sum(functools.reduce(jnp.add, weights), axis=1, keepdims=True)
-        mixture = functools.reduce(
-            jnp.add,
-            [
-                jnp.dot(
-                    weights[i].astype(BF16),
-                    v_ref[0, pl.ds(offsets[i], BLOCK), cols],
-                    preferred_element_type=F32,
-                )
-                for i in range(items)
-            ],
-        )
+        keys = jnp.concatenate([k_ref[0, pl.ds(o, BLOCK), cols] for o in offsets], axis=0)
+        values = jnp.concatenate([v_ref[0, pl.ds(o, BLOCK), cols] for o in offsets], axis=0)
+        scores = lax.dot_general(stacked, keys, NT, preferred_element_type=F32) + bias_ref[...]
+        top = jnp.max(scores, axis=1, keepdims=True)
+        weights = jnp.exp(scores - top)
+        total = jnp.sum(weights, axis=1, keepdims=True)
+        mixture = jnp.dot(weights.astype(BF16), values, preferred_element_type=F32)
         acc_ref[:, cols] = join_heads(mixture)
         for j in range(PAIR):
             h = pair * PAIR + j
@@ -382,6 +367,7 @@
     @pl.when(step == 0)
     def _():
         queries = summary_queries(mine_ref, q_all_ref.at[0], head_count)
+        squery_ref[...] = queries
         keys = k_ref.shape[1]
         scores = lax.dot_general(queries, k_ref[0], NT, preferred_element_type=F32)
         scores = scores + jnp.concatenate([sbias_ref[:, :keys]] * head_count, axis=0)
@@ -395,55 +381,33 @@
 
 def late_kernel(
     valid_ref, block_ref, off_ref, pos_ref, bounds_ref, mine_ref, base_ref, side_ref,
-    q_ref, q_all_ref, k_ref, v_ref, sbias_ref, acc_ref, ml_ref, sacc_ref, sml_ref, w_ref,
+    q_ref, k_ref, v_ref, sbias_ref, acc_ref, ml_ref, sacc_ref, sml_ref, squery_ref, w_ref,
     own_ref, other_ref,
-    mix_ref, state_ref, sum_ref, *, items, pair_count, head_count, early_keys,
+    mix_ref, state_ref, *, items, pair_count, head_count, early_keys,
 ):
-    step = pl.program_id(0)
-    cols_all = head_count * HEAD
+    tok_rows, cols_all = mix_ref.shape
     lane = lax.broadcasted_iota(jnp.int32, (BLOCK, LANES), 1)
-
-    @pl.when(step == 0)
-    def _():
-        queries = summary_queries(mine_ref, q_all_ref.at[0], head_count)
-        scores = lax.dot_general(queries, k_ref[0], NT, preferred_element_type=F32)
-        scores = scores + jnp.concatenate([sbias_ref[:, early_keys:]] * head_count, axis=0)
-        before = sml_ref[:, 0:1]
-        top = jnp.maximum(before, jnp.max(scores, axis=1, keepdims=True))
-        weights = jnp.exp(scores - top)
-        fade = jnp.exp(before - top)
-        total = sml_ref[:, 1:2] * fade + jnp.sum(weights, axis=1, keepdims=True)
-        mixture = sacc_ref[...] * fade + jnp.dot(
-            weights.astype(BF16), v_ref[0], preferred_element_type=F32
-        )
-        mixture = mixture / total
-        slane = lax.broadcasted_iota(jnp.int32, (8, cols_all), 1)
-        joined = jnp.zeros((8, cols_all), F32)
-        for h in range(head_count):
-            joined = jnp.where(
-                (slane >= h * HEAD) & (slane < (h + 1) * HEAD), mixture[h * 8 : (h + 1) * 8], joined
-            )
-        sum_ref[...] = joined
-
     mix_ref[...] = acc_ref[...]
     state_ref[...] = ml_ref[...]
     row = lax.broadcasted_iota(jnp.int32, (BLOCK, 1), 0)
-    query_seg = segments_of(base_ref[0] + step * BLOCK + row, bounds_ref, pair_count)
     for item in range(items):
 
-        @pl.when((valid_ref[item] == 1) & (block_ref[item] == step))
+        @pl.when(valid_ref[item] == 1)
         def _():
             offset = pl.multiple_of(off_ref[item], BLOCK)
+            first = pl.multiple_of(block_ref[item] * BLOCK, BLOCK)
+            queries = pl.ds(first, BLOCK)
+            query_seg = segments_of(base_ref[0] + first + row, bounds_ref, pair_count)
             bias = item_bias(query_seg, pos_ref[item], bounds_ref, pair_count)
             bias = jnp.concatenate([bias] * PAIR, axis=0)
-            state = state_ref[...]
+            state = state_ref[queries, :]
             fresh = state
             for pair in range(head_count // PAIR):
                 cols = slice(pair * LANES, (pair + 1) * LANES)
                 heads = [pair * PAIR + j for j in range(PAIR)]
                 scores = (
                     lax.dot_general(
-                        split_heads(q_ref[0, :, cols]),
+                        split_heads(q_ref[0, queries, cols]),
                         k_ref[0, pl.ds(offset, BLOCK), cols],
                         NT,
                         preferred_element_type=F32,
@@ -463,34 +427,51 @@
                     v_ref[0, pl.ds(offset, BLOCK), cols],
                     preferred_element_type=F32,
                 )
-                mix_ref[:, cols] = mix_ref[:, cols] * spread_pair(
+                mix_ref[queries, cols] = mix_ref[queries, cols] * spread_pair(
                     fade[:BLOCK], fade[BLOCK:]
                 ) + join_heads(mixture)
                 for j, h in enumerate(heads):
                     rows = slice(j * BLOCK, (j + 1) * BLOCK)
                     fresh = jnp.where(lane == h, top[rows], fresh)
                     fresh = jnp.where(lane == head_count + h, total[rows], fresh)
-            state_ref[...] = fresh
-
-    state = state_ref[...]
+            state_ref[queries, :] = fresh
+
+    scores = lax.dot_general(squery_ref[...], k_ref[0], NT, preferred_element_type=F32)
+    scores = scores + jnp.concatenate([sbias_ref[:, early_keys:]] * head_count, axis=0)
+    before = sml_ref[:, 0:1]
+    top = jnp.maximum(before, jnp.max(scores, axis=1, keepdims=True))
+    weights = jnp.exp(scores - top)
+    fade = jnp.exp(before - top)
+    total = sml_ref[:, 1:2] * fade + jnp.sum(weights, axis=1, keepdims=True)
+    mixture = sacc_ref[...] * fade + jnp.dot(
+        weights.astype(BF16), v_ref[0], preferred_element_type=F32
+    )
+    mixture = mixture / total
+    slane = lax.broadcasted_iota(jnp.int32, (8, cols_all), 1)
+    summary = jnp.zeros((8, cols_all), F32)
+    for h in range(head_count):
+        summary = jnp.where(
+            (slane >= h * HEAD) & (slane < (h + 1) * HEAD), mixture[h * 8 : (h + 1) * 8], summary
+        )
+
+    all_rows = lax.broadcasted_iota(jnp.int32, (tok_rows, 1), 0)
+    columns = []
     for pair in range(head_count // PAIR):
         cols = slice(pair * LANES, (pair + 1) * LANES)
         h = head_count + pair * PAIR
-        totals = spread_pair(state[:, h : h + 1], state[:, h + 1 : h + 2])
-        mix_ref[:, cols] = mix_ref[:, cols] / totals
-    attention = mix_ref[...]
-    here = step * BLOCK + row
-    for u in range(mine_ref.shape[0]):
-        attention = jnp.where(here == mine_ref[u], sum_ref[u : u + 1, :], attention)
-    attention = attention.astype(BF16)
+        part = mix_ref[:, cols] / spread_pair(state_ref[:, h : h + 1], state_ref[:, h + 1 : h + 2])
+        for u in range(mine_ref.shape[0]):
+            part = jnp.where(all_rows == mine_ref[u], summary[u : u + 1, cols], part)
+        columns.append(part.astype(BF16))
+    attention = jnp.concatenate(columns, axis=1)
     half = w_ref.shape[1] // 2
     low = pl.multiple_of(side_ref[0] * half, half)
     high = pl.multiple_of((1 - side_ref[0]) * half, half)
+    other_ref[...] = jnp.dot(
+        attention, w_ref[:, pl.ds(high, half)], preferred_element_type=F32
+    ).astype(BF16)
     own_ref[...] = jnp.dot(
         attention, w_ref[:, pl.ds(low, half)], preferred_element_type=F32
-    ).astype(BF16)
-    other_ref[...] = jnp.dot(
-        attention, w_ref[:, pl.ds(high, half)], preferred_element_type=F32
     ).astype(BF16)
 
 
@@ -560,23 +541,32 @@
     )
     sbias = jnp.pad(jnp.where(seen, 0.0, MASKED), ((0, 8 - per_device), (0, 0)))
 
-    there = [other_half(own_tokens)]
-    here = [own_tokens]
-    for slot in range(1, last):
-        here.append(from_slot(own_tokens, slot))
-        there.append(other_half(here[-1]))
     split = 2
     piece = tok_rows // split
-    late_here = [from_slot(own_tokens[i * piece : (i + 1) * piece], last) for i in range(split)]
-    late_there = [other_half(x) for x in late_here]
+    pieces = [[own_tokens[i * piece : (i + 1) * piece] for i in range(split)]]
+    here = {0: [own_tokens]}
+    for slot in range(1, ctx_count):
+        low = slot & -slot
+        source = here[0] if slot == 1 else (pieces[0] if slot == low else here[slot - low])
+        here[slot] = [from_slot(x, low) for x in source]
+    there = {}
+    for slot in range(ctx_count):
+        ready = here[slot]
+        if slot >= 2:
+            ready = lax.optimization_barrier((ready, there[slot - 2]))[0]
+        there[slot] = [other_half(x) for x in ready]
 
     early_rows = last * tok_rows
-    held = project(side, here[0], there[0], w_qkv, 0, early_rows, 0, None)
-    for slot in range(1, last):
-        held = project(side, here[slot], there[slot], w_qkv, 1, early_rows, slot, held)
-    late_held = None
-    for i in range(split):
-        late_held = project(side, late_here[i], late_there[i], w_qkv, 1, tok_rows, i, late_held)
+    held, late_held = None, None
+    for slot in range(ctx_count):
+        for i, (a, b) in enumerate(zip(here[slot], there[slot])):
+            if slot == last:
+                late_held = project(side, a, b, w_qkv, 1, tok_rows, i, late_held)
+            else:
+                row_block = slot * len(here[slot]) + i
+                held = project(
+                    side, a, b, w_qkv, 0 if slot == 0 else 1, early_rows, row_block, held
+                )
 
     smem = pl.BlockSpec(memory_space=pltpu.SMEM)
     rows_spec = pl.BlockSpec((BLOCK, cols), lambda i: (i, 0))
@@ -588,7 +578,7 @@
         return pl.BlockSpec((1, rows, cols), lambda i: (j, 0, 0))
 
     srows = 8 * head_count
-    acc, ml, sacc, sml = pl.pallas_call(
+    acc, ml, sacc, sml, squery = pl.pallas_call(
         functools.partial(
             early_kernel, items=items, pair_count=pair_count, head_count=head_count
         ),
@@ -601,12 +591,19 @@
             kv_spec(2, early_rows),
             whole_block(sbias.shape),
         ],
-        out_specs=[rows_spec, ml_spec, whole_block((srows, cols)), whole_block((srows, LANES))],
+        out_specs=[
+            rows_spec,
+            ml_spec,
+            whole_block((srows, cols)),
+            whole_block((srows, LANES)),
+            whole_block((srows, cols)),
+        ],
         out_shape=[
             jax.ShapeDtypeStruct((tok_rows, cols), F32),
             jax.ShapeDtypeStruct((tok_rows, LANES), F32),
             jax.ShapeDtypeStruct((srows, cols), F32),
             jax.ShapeDtypeStruct((srows, LANES), F32),
+            jax.ShapeDtypeStruct((srows, cols), BF16),
         ],
         scratch_shapes=[pltpu.VMEM((PAIR * BLOCK, items * BLOCK), F32)],
         compiler_params=params("arbitrary"),
@@ -626,27 +623,23 @@
             head_count=head_count,
             early_keys=early_rows,
         ),
-        grid=(block_count,),
+        grid=(1,),
         in_specs=[smem] * 8
         + [
-            q_spec,
             q_all_spec,
             kv_spec(1, tok_rows),
             kv_spec(2, tok_rows),
             whole_block(sbias.shape),
-            rows_spec,
-            ml_spec,
+            whole_block((tok_rows, cols)),
+            whole_block((tok_rows, LANES)),
             whole_block((srows, cols)),
             whole_block((srows, LANES)),
+            whole_block((srows, cols)),
             whole_block(w_out.shape),
         ],
-        out_specs=[pl.BlockSpec((BLOCK, half), lambda i: (i, 0))] * 2,
+        out_specs=[whole_block((tok_rows, half))] * 2,
         out_shape=[jax.ShapeDtypeStruct((tok_rows, half), BF16)] * 2,
-        scratch_shapes=[
-            pltpu.VMEM((BLOCK, cols), F32),
-            pltpu.VMEM((BLOCK, LANES), F32),
-            pltpu.VMEM((8, cols), F32),
-        ],
+        scratch_shapes=[pltpu.VMEM((tok_rows, cols), F32), pltpu.VMEM((tok_rows, LANES), F32)],
         compiler_params=params("arbitrary"),
         cost_estimate=pl.CostEstimate(
             flops=4 * tok_rows * cols * full_width,
@@ -656,7 +649,7 @@
         name="late_attention",
     )(
         late_valid, late_block, late_off, late_pos, bounds, mine, base, side,
-        held, held, late_held, late_held, sbias, acc, ml, sacc, sml, w_out,
+        held, late_held, late_held, sbias, acc, ml, sacc, sml, squery, w_out,
     )
 
     received = other_half(other_term)

time: 117 us -> 89.3 us (0.76)
  the two profiles are of different devices: /device:TPU:8 before, /device:TPU:0 now
where the time goes in v2:
time: 89.3 us; the launch traced here: 89 us
  waiting for transfers between devices  37.1 us (42%)
  Pallas kernels  28.1 us (31%)
  starting transfers between devices  13.6 us (15%)
  local copies, waits for them, and re-layouts  5.64 us (6%)
  other arithmetic  4.34 us (5%)
    ppermute x5, waiting for transfers between devices, from_slot(): return lax.ppermute(x, 'ctx', [(i, i ^ slot) for i in range(ctx_count)])  19.9 us
    ppermute x8, waiting for transfers between devices, other_half(): return lax.ppermute(x, 'heads', swap)  17.3 us
    pallas_call x1, Pallas kernels, gathered(): pl.pallas_call(functools.partial(early_kernel, items=items, pair_count=pa...  10.6 us
    pallas_call x6, Pallas kernels, project(): pl.pallas_call(project_kernel, grid=(count,), in_specs=in_specs, out_spec...  10.2 us
    ppermute x8, starting transfers between devices, other_half(): return lax.ppermute(x, 'heads', swap)  8.97 us
    pallas_call x1, Pallas kernels, gathered(): pl.pallas_call(functools.partial(late_kernel, items=late_items, pair_coun...  7.25 us
    ppermute x5, starting transfers between devices, from_slot(): return lax.ppermute(x, 'ctx', [(i, i ^ slot) for i in range(ctx_count)])  4.64 us
    unnamed x18, local copies, waits for them, and re-layouts  4.08 us
  transfers between devices with their start and end apart: 13, of which 8 were waited for; matrix products, arithmetic and copies ran while one was open for 6% of the time, Pallas kernels for 22%

profile of v2, /device:TPU:0, one launch (start us, length us, event | category | flops | bytes accessed | tf_op | source)
XLA Modules:
  0.0 89.0 jit_solution(5718308241548277419)
XLA Ops:
  0.0 2.9 %collective-permute-start.2 = (bf16[512,512]{1,0:T(8,128)(2,1)}, bf16[512,512]{1,0:T(8,128)(2,1)S(1)}, u32[]{:S(2)}, u32[]{:S(2)}) collective-permute-start(bf16[512,512]{1,0:T(8,128)(2,1)} %bitcast.31), channel_id=1, source_target_pairs={{0,2},{2,0},{1,3},{3,1},{4,6},{6,4},{5,7},{7,5},{8,10},{10,8},{9,1... | collective-permute-start | bytes 1572872 | tf_op jit(solution)/shard_map/ppermute | solution.py:496
  2.9 1.6 %collective-permute-start.5 = (bf16[512,512]{1,0:T(8,128)(2,1)}, bf16[512,512]{1,0:T(8,128)(2,1)S(1)}, u32[]{:S(2)}, u32[]{:S(2)}) collective-permute-start(bf16[512,512]{1,0:T(8,128)(2,1)} %bitcast.32), channel_id=1, source_target_pairs={{0,4},{4,0},{8,12},{12,8},{1,5},{5,1},{9,13},{13,9},{2,6},{6,2},{1... | collective-permute-start | bytes 1572872 | tf_op jit(solution)/shard_map/ppermute | solution.py:499
  4.5 1.1 %slice_bitcast_fusion = (bf16[256,512]{1,0:T(8,128)(2,1)S(1)}, bf16[256,512]{1,0:T(8,128)(2,1)S(1)}) fusion(bf16[1,512,512]{2,1,0:T(8,128)(2,1)} %param.9), kind=kLoop, calls=%fused_computation.5 | loop fusion | bytes 1048576 | tf_op jit(solution)/shard_map/slice | solution.py:546
  5.6 2.7 %collective-permute-start = (bf16[256,512]{1,0:T(8,128)(2,1)S(1)}, bf16[256,512]{1,0:T(8,128)(2,1)S(1)}, u32[]{:S(2)}, u32[]{:S(2)}) collective-permute-start(bf16[256,512]{1,0:T(8,128)(2,1)S(1)} %get-tuple-element.38), channel_id=1, source_target_pairs={{0,8},{4,12},{8,0},{12,4},{1,9},{5,13},{9,1},{13,5},{2,10},{6,14},... | collective-permute-start | bytes 786440 | tf_op jit(solution)/shard_map/ppermute | solution.py:499
  12.2 14.5 %collective-permute-done.5.here_ref = bf16[512,512]{1,0:T(8,128)(2,1)S(1)} collective-permute-done((bf16[512,512]{1,0:T(8,128)(2,1)}, bf16[512,512]{1,0:T(8,128)(2,1)S(1)}, u32[]{:S(2)}, u32[]{:S(2)}) %collective-permute-start.5) | collective-permute-done | bytes 524320 | tf_op jit(solution)/shard_map/ppermute | solution.py:499
  27.6 3.4 %collective-permute-done.1.here_ref = bf16[256,512]{1,0:T(8,128)(2,1)S(1)} collective-permute-done((bf16[256,512]{1,0:T(8,128)(2,1)S(1)}, bf16[256,512]{1,0:T(8,128)(2,1)S(1)}, u32[]{:S(2)}, u32[]{:S(2)}) %collective-permute-start.1) | collective-permute-done | bytes 262176 | tf_op jit(solution)/shard_map/ppermute | solution.py:499
  31.7 1.6 %collective-permute-start.3 = (bf16[256,512]{1,0:T(8,128)(2,1)S(1)}, bf16[256,512]{1,0:T(8,128)(2,1)S(1)}, u32[]{:S(2)}, u32[]{:S(2)}) collective-permute-start(bf16[256,512]{1,0:T(8,128)(2,1)S(1)} %collective-permute-done.here_ref), channel_id=1, source_target_pairs={{0,2},{2,0},{1,3},{3,1},{4,6},{6,4},{5,7},{7,5},{8,10},{10,8},{9,1... | collective-permute-start | bytes 786440 | tf_op jit(solution)/shard_map/ppermute | solution.py:496
  33.3 1.9 %copy-done.1 = bf16[3,1024,512]{2,1,0:T(8,128)(2,1)S(1)} copy-done((bf16[3,1024,512]{2,1,0:T(8,128)(2,1)S(1)}, bf16[3,1024,512]{2,1,0:T(8,128)(2,1)}, u32[]{:S(2)}) %copy-start.1) | copy-done | bytes 3145752
  35.2 1.0 %copy-done.3 = bf16[1,512,512]{2,1,0:T(8,128)(2,1)S(1)} copy-done((bf16[1,512,512]{2,1,0:T(8,128)(2,1)S(1)}, bf16[1,512,512]{2,1,0:T(8,128)(2,1)}, u32[]{:S(2)}) %copy-start.3) | copy-done | bytes 524312
  36.2 3.0 %project.6.refs_0_ = bf16[3,1536,512]{2,1,0:T(8,128)(2,1)} custom-call(s32[1]{0:T(128)} %bitcast.6.side_ref, bf16[512,512]{1,0:T(8,128)(2,1)S(1)} %bitcast.33, bf16[512,512]{1,0:T(8,128)(2,1)S(1)} %collective-permute-done.2.there_ref, bf16[3,1024,512]{2,1,0:T(8,128)(2,1)S(1)} %copy-done.1), custom_call_target="tpu_custom_call" | custom-call | flops 1610612736 | bytes 5767168 | tf_op jit(solution)/shard_map/project/pallas_call | solution.py:264
  39.2 1.9 %collective-permute-done.8.here_ref = bf16[256,512]{1,0:T(8,128)(2,1)S(1)} collective-permute-done((bf16[256,512]{1,0:T(8,128)(2,1)S(1)}, bf16[256,512]{1,0:T(8,128)(2,1)S(1)}, u32[]{:S(2)}, u32[]{:S(2)}) %collective-permute-start.8) | collective-permute-done | bytes 262176 | tf_op jit(solution)/shard_map/ppermute | solution.py:499
  42.5 1.1 %collective-permute-start.9 = (bf16[256,512]{1,0:T(8,128)(2,1)S(1)}, bf16[256,512]{1,0:T(8,128)(2,1)S(1)}, u32[]{:S(2)}, u32[]{:S(2)}) collective-permute-start(bf16[256,512]{1,0:T(8,128)(2,1)S(1)} %collective-permute-done.7.here_ref), channel_id=1, source_target_pairs={{0,2},{2,0},{1,3},{3,1},{4,6},{6,4},{5,7},{7,5},{8,10},{10,8},{9,1... | collective-permute-start | bytes 786440 | tf_op jit(solution)/shard_map/ppermute | solution.py:496
  43.6 2.2 %project.7.refs_0_ = bf16[3,1536,512]{2,1,0:T(8,128)(2,1)} custom-call(s32[1]{0:T(128)} %bitcast.6.side_ref, bf16[512,512]{1,0:T(8,128)(2,1)S(1)} %collective-permute-done.5.here_ref, bf16[512,512]{1,0:T(8,128)(2,1)S(1)} %collective-permute-done.6.there_ref, bf16[3,1024,512]{2,1,0:T(8,128)(2,1)S(1)} %copy-done.2, ...), custom_call_target="tpu_custom_call", output_to_operand_aliasing={{}: (4, {})} | custom-call | flops 1073741824 | bytes 4194304 | tf_op jit(solution)/shard_map/project/pallas_call | solution.py:264
  45.9 1.3 %collective-permute-done.4.there_ref = bf16[256,512]{1,0:T(8,128)(2,1)S(1)} collective-permute-done((bf16[256,512]{1,0:T(8,128)(2,1)S(1)}, bf16[256,512]{1,0:T(8,128)(2,1)S(1)}, u32[]{:S(2)}, u32[]{:S(2)}) %collective-permute-start.4) | collective-permute-done | bytes 262176 | tf_op jit(solution)/shard_map/ppermute | solution.py:496
  47.2 1.6 %project.8.refs_0_ = bf16[3,1536,512]{2,1,0:T(8,128)(2,1)} custom-call(s32[1]{0:T(128)} %bitcast.6.side_ref, bf16[256,512]{1,0:T(8,128)(2,1)S(1)} %collective-permute-done.1.here_ref, bf16[256,512]{1,0:T(8,128)(2,1)S(1)} %collective-permute-done.4.there_ref, bf16[3,1024,512]{2,1,0:T(8,128)(2,1)S(1)} %copy-done.2, ...), custom_call_target="tpu_custom_call", output_to_operand_aliasing={{}: (4, {})} | custom-call | flops 536870912 | bytes 3145728 | tf_op jit(solution)/shard_map/project/pallas_call | solution.py:264
  48.8 4.0 %collective-permute-done.3.there_ref = bf16[256,512]{1,0:T(8,128)(2,1)S(1)} collective-permute-done((bf16[256,512]{1,0:T(8,128)(2,1)S(1)}, bf16[256,512]{1,0:T(8,128)(2,1)S(1)}, u32[]{:S(2)}, u32[]{:S(2)}) %collective-permute-start.3) | collective-permute-done | bytes 262176 | tf_op jit(solution)/shard_map/ppermute | solution.py:496
  52.8 1.6 %project.9.q_ref.q_all_ref.k_ref.v_ref = bf16[3,1536,512]{2,1,0:T(8,128)(2,1)} custom-call(s32[1]{0:T(128)} %bitcast.6.side_ref, bf16[256,512]{1,0:T(8,128)(2,1)S(1)} %collective-permute-done.here_ref, bf16[256,512]{1,0:T(8,128)(2,1)S(1)} %collective-permute-done.3.there_ref, bf16[3,1024,512]{2,1,0:T(8,128)(2,1)S(1)} %copy-done.2, ...), custom_call_target="tpu_custom_call", output_to_operand_aliasing={{}: (4, {})} | custom-call | flops 536870912 | bytes 3145728 | tf_op jit(solution)/shard_map/project/pallas_call | solution.py:264
  54.4 10.6 %early_attention.1 = (f32[512,512]{1,0:T(8,128)S(1)}, f32[512,128]{1,0:T(8,128)S(1)}, f32[64,512]{1,0:T(8,128)S(1)}, f32[64,128]{1,0:T(8,128)S(1)}, bf16[64,512]{1,0:T(8,128)(2,1)S(1)}) custom-call(s32[24]{0:T(128)S(1)} %get-tuple-element.41.off_ref, s32[24]{0:T(128)S(1)} %get-tuple-element.32.pos_ref, s32[4]{0:T(128)S(1)} %bitcast.36, ...), custom_call_target="tpu_custom_call" | custom-call | flops 1610612736 | bytes 5242880 | tf_op jit(solution)/shard_map/early_attention/pallas_call | solution.py:581
  65.1 0.9 %project.10.refs_0_ = bf16[3,512,512]{2,1,0:T(8,128)(2,1)S(1)} custom-call(s32[1]{0:T(128)} %bitcast.6.side_ref, bf16[256,512]{1,0:T(8,128)(2,1)S(1)} %collective-permute-done.8.here_ref, bf16[256,512]{1,0:T(8,128)(2,1)S(1)} %collective-permute-done.10.there_ref, bf16[3,1024,512]{2,1,0:T(8,128)(2,1)S(1)} %copy-done.2), custom_call_target="tpu_custom_call" | custom-call | flops 536870912 | bytes 3145728 | tf_op jit(solution)/shard_map/project/pallas_call | solution.py:264
  67.2 7.3 %late_attention.1 = (bf16[512,512]{1,0:T(8,128)(2,1)S(1)}, bf16[512,512]{1,0:T(8,128)(2,1)S(1)}) custom-call(s32[5]{0:T(128)S(1)} %convert_element_type.37.valid_ref, s32[5]{0:T(128)S(1)} %get-tuple-element.31.block_ref, s32[5]{0:T(128)S(1)} %get-tuple-element.30.off_ref, s32[5]{0:T(128)S(1)} %get-tuple-element.29.pos_ref, s32[4]{0:T(128)S(1)} %bitcast.37, ...), custom_call_target="tpu_custom_call" | custom-call | flops 1073741824 | bytes 3145728 | tf_op jit(solution)/shard_map/late_attention/pallas_call | solution.py:618
  74.9 8.9 %collective-permute-done.11 = bf16[512,512]{1,0:T(8,128)(2,1)S(1)} collective-permute-done((bf16[512,512]{1,0:T(8,128)(2,1)S(1)}, bf16[512,512]{1,0:T(8,128)(2,1)S(1)}, u32[]{:S(2)}, u32[]{:S(2)}) %collective-permute-start.11) | collective-permute-done | bytes 524320 | tf_op jit(solution)/shard_map/ppermute | solution.py:496
  84.1 1.1 %collective-permute-start.12 = (f32[2,512]{1,0:T(2,128)S(1)}, f32[2,512]{1,0:T(2,128)S(1)}, u32[]{:S(2)}, u32[]{:S(2)}) collective-permute-start(f32[2,512]{1,0:T(2,128)S(1)} %pad_maximum_fusion), channel_id=1, source_target_pairs={{0,2},{2,0},{1,3},{3,1},{4,6},{6,4},{5,7},{7,5},{8,10},{10,8},{9,1... | collective-permute-start | bytes 12296 | tf_op jit(solution)/shard_map/ppermute | solution.py:496
  85.2 2.6 %collective-permute-done.12 = f32[2,512]{1,0:T(2,128)S(1)} collective-permute-done((f32[2,512]{1,0:T(2,128)S(1)}, f32[2,512]{1,0:T(2,128)S(1)}, u32[]{:S(2)}, u32[]{:S(2)}) %collective-permute-start.12) | collective-permute-done | bytes 4128 | tf_op jit(solution)/shard_map/ppermute | solution.py:496
  87.9 1.1 %fusion = bf16[1,512,512]{2,1,0:T(8,128)(2,1)} fusion(f32[512]{0:T(512)S(1)} %copy-done.6, f32[512]{0:T(512)S(1)} %copy-done.7, f32[512]{0:T(512)S(1)} %add_rsqrt_fusion, f32[512]{0:T(512)S(1)} %bitcast.43, bf16[512,512]{1,0:T(8,128)(2,1)S(1)} %collective-permute-done.11, bf16[512,512]{1,0:T(8,128)(2,1)S(1)} %get-tuple-element.25, ...), kind=kLoop, calls=%fused_computation.3 | loop fusion | flops 2621440 | bytes 2105344 | tf_op jit(solution)/shard_map/broadcast_in_dim | solution.py:662
  (66 shorter events, 8.9 us)
Async XLA Ops:
  0.0 9.4 %copy-start = (s32[1,16,8]{1,2,0:T(8,128)S(1)}, s32[1,16,8]{1,2,0:T(8,128)}, u32[]{:S(2)}) copy-start(s32[1,16,8]{1,2,0:T(8,128)} %param.16) | copy-start | bytes 1540
  0.0 31.0 %collective-permute-start.2 = (bf16[512,512]{1,0:T(8,128)(2,1)}, bf16[512,512]{1,0:T(8,128)(2,1)S(1)}, u32[]{:S(2)}, u32[]{:S(2)}) collective-permute-start(bf16[512,512]{1,0:T(8,128)(2,1)} %bitcast.31), channel_id=1, source_target_pairs={{0,2},{2,0},{1,3},{3,1},{4,6},{6,4},{5,7},{7,5},{8,10},{10,8},{9,1... | collective-permute-start | bytes 1572872 | tf_op jit(solution)/shard_map/ppermute | solution.py:496
  2.9 23.8 %collective-permute-start.5 = (bf16[512,512]{1,0:T(8,128)(2,1)}, bf16[512,512]{1,0:T(8,128)(2,1)S(1)}, u32[]{:S(2)}, u32[]{:S(2)}) collective-permute-start(bf16[512,512]{1,0:T(8,128)(2,1)} %bitcast.32), channel_id=1, source_target_pairs={{0,4},{4,0},{8,12},{12,8},{1,5},{5,1},{9,13},{13,9},{2,6},{6,2},{1... | collective-permute-start | bytes 1572872 | tf_op jit(solution)/shard_map/ppermute | solution.py:499
  5.6 22.0 %collective-permute-start = (bf16[256,512]{1,0:T(8,128)(2,1)S(1)}, bf16[256,512]{1,0:T(8,128)(2,1)S(1)}, u32[]{:S(2)}, u32[]{:S(2)}) collective-permute-start(bf16[256,512]{1,0:T(8,128)(2,1)S(1)} %get-tuple-element.38), channel_id=1, source_target_pairs={{0,8},{4,12},{8,0},{12,4},{1,9},{5,13},{9,1},{13,5},{2,10},{6,14},... | collective-permute-start | bytes 786440 | tf_op jit(solution)/shard_map/ppermute | solution.py:499
  8.2 22.8 %collective-permute-start.1 = (bf16[256,512]{1,0:T(8,128)(2,1)S(1)}, bf16[256,512]{1,0:T(8,128)(2,1)S(1)}, u32[]{:S(2)}, u32[]{:S(2)}) collective-permute-start(bf16[256,512]{1,0:T(8,128)(2,1)S(1)} %get-tuple-element.37), channel_id=1, source_target_pairs={{0,8},{4,12},{8,0},{12,4},{1,9},{5,13},{9,1},{13,5},{2,10},{6,14},... | collective-permute-start | bytes 786440 | tf_op jit(solution)/shard_map/ppermute | solution.py:499
  26.7 14.9 %collective-permute-start.6 = (bf16[512,512]{1,0:T(8,128)(2,1)S(1)}, bf16[512,512]{1,0:T(8,128)(2,1)S(1)}, u32[]{:S(2)}, u32[]{:S(2)}) collective-permute-start(bf16[512,512]{1,0:T(8,128)(2,1)S(1)} %collective-permute-done.5.here_ref), channel_id=1, source_target_pairs={{0,2},{2,0},{1,3},{3,1},{4,6},{6,4},{5,7},{7,5},{8,10},{10,8},{9,1... | collective-permute-start | bytes 1572872 | tf_op jit(solution)/shard_map/ppermute | solution.py:496
  27.6 11.7 %collective-permute-start.7 = (bf16[256,512]{1,0:T(8,128)(2,1)S(1)}, bf16[256,512]{1,0:T(8,128)(2,1)S(1)}, u32[]{:S(2)}, u32[]{:S(2)}) collective-permute-start(bf16[256,512]{1,0:T(8,128)(2,1)S(1)} %collective-permute-done.here_ref), channel_id=1, source_target_pairs={{0,4},{4,0},{8,12},{12,8},{1,5},{5,1},{9,13},{13,9},{2,6},{6,2},{1... | collective-permute-start | bytes 786440 | tf_op jit(solution)/shard_map/ppermute | solution.py:499
  31.0 10.1 %collective-permute-start.8 = (bf16[256,512]{1,0:T(8,128)(2,1)S(1)}, bf16[256,512]{1,0:T(8,128)(2,1)S(1)}, u32[]{:S(2)}, u32[]{:S(2)}) collective-permute-start(bf16[256,512]{1,0:T(8,128)(2,1)S(1)} %collective-permute-done.1.here_ref), channel_id=1, source_target_pairs={{0,4},{4,0},{8,12},{12,8},{1,5},{5,1},{9,13},{13,9},{2,6},{6,2},{1... | collective-permute-start | bytes 786440 | tf_op jit(solution)/shard_map/ppermute | solution.py:499
  31.0 16.2 %collective-permute-start.4 = (bf16[256,512]{1,0:T(8,128)(2,1)S(1)}, bf16[256,512]{1,0:T(8,128)(2,1)S(1)}, u32[]{:S(2)}, u32[]{:S(2)}) collective-permute-start(bf16[256,512]{1,0:T(8,128)(2,1)S(1)} %collective-permute-done.1.here_ref), channel_id=1, source_target_pairs={{0,2},{2,0},{1,3},{3,1},{4,6},{6,4},{5,7},{7,5},{8,10},{10,8},{9,1... | collective-permute-start | bytes 786440 | tf_op jit(solution)/shard_map/ppermute | solution.py:496
  31.7 21.1 %collective-permute-start.3 = (bf16[256,512]{1,0:T(8,128)(2,1)S(1)}, bf16[256,512]{1,0:T(8,128)(2,1)S(1)}, u32[]{:S(2)}, u32[]{:S(2)}) collective-permute-start(bf16[256,512]{1,0:T(8,128)(2,1)S(1)} %collective-permute-done.here_ref), channel_id=1, source_target_pairs={{0,2},{2,0},{1,3},{3,1},{4,6},{6,4},{5,7},{7,5},{8,10},{10,8},{9,1... | collective-permute-start | bytes 786440 | tf_op jit(solution)/shard_map/ppermute | solution.py:496
  33.3 1.9 %copy-start.1 = (bf16[3,1024,512]{2,1,0:T(8,128)(2,1)S(1)}, bf16[3,1024,512]{2,1,0:T(8,128)(2,1)}, u32[]{:S(2)}) copy-start(bf16[3,1024,512]{2,1,0:T(8,128)(2,1)} %w_ref.12) | copy-start | bytes 9437188
  35.2 1.0 %copy-start.3 = (bf16[1,512,512]{2,1,0:T(8,128)(2,1)S(1)}, bf16[1,512,512]{2,1,0:T(8,128)(2,1)}, u32[]{:S(2)}) copy-start(bf16[1,512,512]{2,1,0:T(8,128)(2,1)} %param.9) | copy-start | bytes 1572868
  36.2 7.4 %copy-start.2 = (bf16[3,1024,512]{2,1,0:T(8,128)(2,1)S(1)}, bf16[3,1024,512]{2,1,0:T(8,128)(2,1)}, u32[]{:S(2)}) copy-start(bf16[3,1024,512]{2,1,0:T(8,128)(2,1)} %w_ref.12) | copy-start | bytes 9437188
  41.6 23.4 %collective-permute-start.10 = (bf16[256,512]{1,0:T(8,128)(2,1)S(1)}, bf16[256,512]{1,0:T(8,128)(2,1)S(1)}, u32[]{:S(2)}, u32[]{:S(2)}) collective-permute-start(bf16[256,512]{1,0:T(8,128)(2,1)S(1)} %collective-permute-done.8.here_ref), channel_id=1, source_target_pairs={{0,2},{2,0},{1,3},{3,1},{4,6},{6,4},{5,7},{7,5},{8,10},{10,8},{9,1... | collective-permute-start | bytes 786440 | tf_op jit(solution)/shard_map/ppermute | solution.py:496
  42.5 23.5 %collective-permute-start.9 = (bf16[256,512]{1,0:T(8,128)(2,1)S(1)}, bf16[256,512]{1,0:T(8,128)(2,1)S(1)}, u32[]{:S(2)}, u32[]{:S(2)}) collective-permute-start(bf16[256,512]{1,0:T(8,128)(2,1)S(1)} %collective-permute-done.7.here_ref), channel_id=1, source_target_pairs={{0,2},{2,0},{1,3},{3,1},{4,6},{6,4},{5,7},{7,5},{8,10},{10,8},{9,1... | collective-permute-start | bytes 786440 | tf_op jit(solution)/shard_map/ppermute | solution.py:496
  66.0 1.2 %copy-start.5 = (bf16[512,1024]{1,0:T(8,128)(2,1)S(1)}, bf16[512,1024]{1,0:T(8,128)(2,1)}, u32[]{:S(2)}) copy-start(bf16[512,1024]{1,0:T(8,128)(2,1)} %w_ref.13) | copy-start | bytes 3145732
  67.2 16.6 %copy-start.4 = (bf16[1,512,512]{2,1,0:T(8,128)(2,1)S(1)}, bf16[1,512,512]{2,1,0:T(8,128)(2,1)}, u32[]{:S(2)}) copy-start(bf16[1,512,512]{2,1,0:T(8,128)(2,1)} %param.9) | copy-start | bytes 1572868
  67.2 20.6 %copy-start.6 = (f32[512]{0:T(512)S(1)}, f32[512]{0:T(512)}, u32[]{:S(2)}) copy-start(f32[512]{0:T(512)} %param.13) | copy-start | bytes 6148
  67.2 20.7 %copy-start.7 = (f32[512]{0:T(512)S(1)}, f32[512]{0:T(512)}, u32[]{:S(2)}) copy-start(f32[512]{0:T(512)} %param.12) | copy-start | bytes 6148
  74.5 9.3 %collective-permute-start.11 = (bf16[512,512]{1,0:T(8,128)(2,1)S(1)}, bf16[512,512]{1,0:T(8,128)(2,1)S(1)}, u32[]{:S(2)}, u32[]{:S(2)}) collective-permute-start(bf16[512,512]{1,0:T(8,128)(2,1)S(1)} %get-tuple-element.26), channel_id=1, source_target_pairs={{0,2},{2,0},{1,3},{3,1},{4,6},{6,4},{5,7},{7,5},{8,10},{10,8},{9,1... | collective-permute-start | bytes 1572872 | tf_op jit(solution)/shard_map/ppermute | solution.py:496
  84.1 3.7 %collective-permute-start.12 = (f32[2,512]{1,0:T(2,128)S(1)}, f32[2,512]{1,0:T(2,128)S(1)}, u32[]{:S(2)}, u32[]{:S(2)}) collective-permute-start(f32[2,512]{1,0:T(2,128)S(1)} %pad_maximum_fusion), channel_id=1, source_target_pairs={{0,2},{2,0},{1,3},{3,1},{4,6},{6,4},{5,7},{7,5},{8,10},{10,8},{9,1... | collective-permute-start | bytes 12296 | tf_op jit(solution)/shard_map/ppermute | solution.py:496

commit v3 on v0

--- a/solution.py
+++ b/solution.py
@@ -1,6 +1,9 @@
+import functools
 import jax
 import jax.numpy as jnp
 from jax import lax
+from jax.experimental import pallas as pl
+from jax.experimental.pallas import tpu as pltpu
 from jax.sharding import PartitionSpec as P
 
 HEAD = 64
@@ -66,7 +69,7 @@
     return jnp.concatenate(views, axis=axis_pos + 1)
 
 
-def shards(
+def requested(
     tokens, w_qkv, w_out, ln_gain, ln_bias, random_blocks, summary_pos, summary_blocks, pair_lengths
 ):
     tok_rows = tokens.shape[1]
@@ -214,6 +217,556 @@
     return normed.astype(jnp.bfloat16)[None]
 
 
+LANES = 128
+PAIR = LANES // HEAD
+VMEM_LIMIT = 14 * 1024 * 1024
+F32 = jnp.float32
+BF16 = jnp.bfloat16
+NT = (((1,), (1,)), ((), ()))
+
+
+def whole_block(shape):
+    return pl.BlockSpec(shape, lambda *_: (0,) * len(shape))
+
+
+def params(*semantics):
+    return pltpu.CompilerParams(
+        dimension_semantics=semantics or None, vmem_limit_bytes=VMEM_LIMIT
+    )
+
+
+def project_rows(side_ref, here_ref, there_ref, w_ref):
+    half = here_ref.shape[1]
+    low = pl.multiple_of(side_ref[0] * half, half)
+    high = pl.multiple_of((1 - side_ref[0]) * half, half)
+    product = jnp.dot(here_ref[...], w_ref[pl.ds(low, half), :], preferred_element_type=F32)
+    product += jnp.dot(there_ref[...], w_ref[pl.ds(high, half), :], preferred_element_type=F32)
+    return product.astype(BF16)
+
+
+def pair_up(refs):
+    return list(zip(refs[0::2], refs[1::2]))
+
+
+def first_kernel(side_ref, here_ref, there_ref, w_hbm, q_ref, kv_ref, w_kv_ref, w_q_ref, sem):
+    copies = [pltpu.make_async_copy(w_hbm.at[0], w_q_ref, sem.at[0])]
+    copies += [
+        pltpu.make_async_copy(w_hbm.at[j + 1], w_kv_ref.at[j], sem.at[j + 1]) for j in range(2)
+    ]
+    for copy in copies:
+        copy.start()
+    copies[0].wait()
+    q_ref[...] = project_rows(side_ref, here_ref, there_ref, w_q_ref)
+    for j in range(2):
+        copies[j + 1].wait()
+        kv_ref[j] = project_rows(side_ref, here_ref, there_ref, w_kv_ref.at[j])
+
+
+def pieces_kernel(side_ref, w_kv_ref, *refs):
+    count = len(refs) // 3
+    for piece, kv_ref in zip(pair_up(refs[: 2 * count]), refs[2 * count :]):
+        project_pieces(side_ref, [piece], w_kv_ref, kv_ref, 0)
+
+
+def segments_of(position, bounds_ref, pair_count):
+    segment = jnp.zeros(position.shape, jnp.int32)
+    for pair in range(pair_count):
+        segment += (position >= bounds_ref[pair]).astype(jnp.int32)
+    return segment
+
+
+def item_bias(query_seg, key_pos, bounds_ref, pair_count):
+    lane = lax.broadcasted_iota(jnp.int32, (1, BLOCK), 1)
+    key_seg = segments_of(key_pos + lane, bounds_ref, pair_count)
+    key_seg = jnp.where(key_pos >= 0, key_seg, -1)
+    return jnp.where(query_seg == key_seg, 0.0, MASKED)
+
+
+def split_heads(pair_queries):
+    lane = lax.broadcasted_iota(jnp.int32, pair_queries.shape, 1)
+    scaled = pair_queries.astype(F32) * HEAD ** (-0.5)
+    low = jnp.where(lane < HEAD, scaled, 0.0)
+    high = jnp.where(lane >= HEAD, scaled, 0.0)
+    return jnp.concatenate([low, high], axis=0).astype(BF16)
+
+
+def join_heads(stacked):
+    rows = stacked.shape[0] // PAIR
+    lane = lax.broadcasted_iota(jnp.int32, (rows, LANES), 1)
+    return jnp.where(lane < HEAD, stacked[:rows], stacked[rows:])
+
+
+def spread_pair(low, high):
+    lane = lax.broadcasted_iota(jnp.int32, (low.shape[0], LANES), 1)
+    return jnp.where(lane < HEAD, low, high)
+
+
+def summary_queries(rows_ref, q_ref, head_count):
+    tok_rows, cols = q_ref.shape
+    row = lax.broadcasted_iota(jnp.int32, (8, tok_rows), 0)
+    col = lax.broadcasted_iota(jnp.int32, (8, tok_rows), 1)
+    chosen = jnp.zeros((8, tok_rows), F32)
+    for u in range(rows_ref.shape[0]):
+        chosen = jnp.where((row == u) & (col == rows_ref[u]), 1.0, chosen)
+    picked = jnp.dot(chosen.astype(BF16), q_ref[...], preferred_element_type=F32)
+    picked = picked * HEAD ** (-0.5)
+    lane = lax.broadcasted_iota(jnp.int32, (8, cols), 1)
+    parts = [
+        jnp.where((lane >= h * HEAD) & (lane < (h + 1) * HEAD), picked, 0.0)
+        for h in range(head_count)
+    ]
+    return jnp.concatenate(parts, axis=0).astype(BF16)
+
+
+def attend_blocks(
+    first_block, block_total, off_ref, pos_ref, bounds_ref, base_ref, q_ref, kv_ref,
+    acc_ref, top_ref, sum_ref, bias_ref, score_ref, items, pair_count, head_count,
+):
+    row = lax.broadcasted_iota(jnp.int32, (BLOCK, 1), 0)
+
+    def block_step(step, carry):
+        place = pl.ds(pl.multiple_of(step * BLOCK, BLOCK), BLOCK)
+        first = pl.multiple_of((first_block + step) * BLOCK, BLOCK)
+        query_seg = segments_of(base_ref[0] + first + row, bounds_ref, pair_count)
+        offsets = []
+        for item in range(items):
+            at = (first_block + step) * items + item
+            offsets.append(pl.multiple_of(off_ref[at], BLOCK))
+            bias_ref[:, item * BLOCK : (item + 1) * BLOCK] = item_bias(
+                query_seg, pos_ref[at], bounds_ref, pair_count
+            )
+        tops = []
+        for pair in range(head_count // PAIR):
+            cols = slice(pair * LANES, (pair + 1) * LANES)
+            keys = jnp.concatenate([kv_ref[0, pl.ds(o, BLOCK), cols] for o in offsets], axis=0)
+            scores = lax.dot_general(
+                split_heads(q_ref[pl.ds(first, BLOCK), cols]), keys, NT, preferred_element_type=F32
+            )
+            for j in range(PAIR):
+                rows = slice(j * BLOCK, (j + 1) * BLOCK)
+                part = scores[rows] + bias_ref[...]
+                score_ref[pair, rows] = part
+                tops.append(jnp.max(part, axis=1, keepdims=True))
+        for pair in range(head_count // PAIR):
+            cols = slice(pair * LANES, (pair + 1) * LANES)
+            values = jnp.concatenate([kv_ref[1, pl.ds(o, BLOCK), cols] for o in offsets], axis=0)
+            values = jnp.concatenate([values, jnp.ones_like(values)], axis=1)
+            peaks = tops[pair * PAIR : (pair + 1) * PAIR]
+            weights = jnp.exp(score_ref[pair] - jnp.concatenate(peaks, axis=0)).astype(BF16)
+            product = jnp.dot(weights, values, preferred_element_type=F32)
+            acc_ref[place, cols] = join_heads(product[:, :LANES])
+            sum_ref[place, cols] = join_heads(product[:, LANES:])
+            top_ref[place, cols] = spread_pair(*peaks)
+        return carry
+
+    lax.fori_loop(0, block_total, block_step, 0)
+
+
+def project_pieces(side_ref, pieces, w_ref, kv_ref, row):
+    for here_ref, there_ref in pieces:
+        rows = here_ref.shape[0]
+        for j in range(2):
+            kv_ref[j, row : row + rows] = project_rows(side_ref, here_ref, there_ref, w_ref.at[j])
+        row += rows
+
+
+def early_kernel(
+    off_ref, pos_ref, bounds_ref, base_ref, q_ref, own_ref, *refs, items, pair_count, head_count
+):
+    *held, acc_ref, top_ref, sum_ref, kv_ref, bias_ref, score_ref, sem = refs
+    copies = []
+    row = 0
+    for i, part in enumerate([own_ref] + held):
+        rows = part.shape[1]
+        copies.append(pltpu.make_async_copy(part, kv_ref.at[:, pl.ds(row, rows)], sem.at[i]))
+        copies[-1].start()
+        row += rows
+    for copy in copies:
+        copy.wait()
+    attend_blocks(
+        0, acc_ref.shape[0] // BLOCK, off_ref, pos_ref, bounds_ref, base_ref, q_ref, kv_ref,
+        acc_ref, top_ref, sum_ref, bias_ref, score_ref, items, pair_count, head_count,
+    )
+
+
+def item_part(q_ref, kv_ref, first, offset, bias, head_count):
+    pairs = head_count // PAIR
+    scores, tops = [], []
+    for pair in range(pairs):
+        cols = slice(pair * LANES, (pair + 1) * LANES)
+        product = lax.dot_general(
+            split_heads(q_ref[pl.ds(first, BLOCK), cols]),
+            kv_ref[0, pl.ds(offset, BLOCK), cols],
+            NT,
+            preferred_element_type=F32,
+        )
+        product = product + jnp.concatenate([bias] * PAIR, axis=0)
+        scores.append(product)
+        tops.append(jnp.max(product, axis=1, keepdims=True))
+    peaks, totals, mixtures = [], [], []
+    for pair in range(pairs):
+        cols = slice(pair * LANES, (pair + 1) * LANES)
+        weights = jnp.exp(scores[pair] - tops[pair]).astype(BF16)
+        values = kv_ref[1, pl.ds(offset, BLOCK), cols]
+        values = jnp.concatenate([values, jnp.ones_like(values)], axis=1)
+        product = jnp.dot(weights, values, preferred_element_type=F32)
+        peaks.append(spread_pair(tops[pair][:BLOCK], tops[pair][BLOCK:]))
+        mixtures.append(join_heads(product[:, :LANES]))
+        totals.append(join_heads(product[:, LANES:]))
+    return peaks, totals, mixtures
+
+
+def add_items(
+    tables, bounds_ref, base_ref, q_ref, kv_ref, state, items, group, pair_count, head_count
+):
+    valid_ref, block_ref, off_ref, pos_ref = tables
+    peak_ref, total_ref, mix_ref = state
+    row = lax.broadcasted_iota(jnp.int32, (BLOCK, 1), 0)
+
+    def add_group(start):
+        parts = []
+        for item in range(start, min(start + group, items)):
+            offset = pl.multiple_of(off_ref[item], BLOCK)
+            first = pl.multiple_of(block_ref[item] * BLOCK, BLOCK)
+            query_seg = segments_of(base_ref[0] + first + row, bounds_ref, pair_count)
+            key_pos = jnp.where(valid_ref[item] == 1, pos_ref[item], -(2**30))
+            bias = item_bias(query_seg, key_pos, bounds_ref, pair_count)
+            parts.append((first, item_part(q_ref, kv_ref, first, offset, bias, head_count)))
+        for first, (peaks, totals, mixtures) in parts:
+            rows = pl.ds(first, BLOCK)
+            for pair in range(head_count // PAIR):
+                cols = slice(pair * LANES, (pair + 1) * LANES)
+                before = peak_ref[rows, cols]
+                top = jnp.maximum(before, peaks[pair])
+                fade = jnp.exp(before - top)
+                share = jnp.exp(peaks[pair] - top)
+                peak_ref[rows, cols] = top
+                total_ref[rows, cols] = total_ref[rows, cols] * fade + totals[pair] * share
+                mix_ref[rows, cols] = mix_ref[rows, cols] * fade + mixtures[pair] * share
+
+    for start in range(0, items, group):
+        pl.when(valid_ref[start] == 1)(functools.partial(add_group, start))
+
+
+def middle_kernel(
+    valid_ref, block_ref, off_ref, pos_ref, bounds_ref, base_ref, mine_ref, side_ref,
+    q_ref, w_kv_ref, kv_early_ref, sbias_ref, acc_in, top_in, sum_in,
+    here0_ref, there0_ref, here1_ref, there1_ref, w_out_hbm,
+    acc_ref, top_ref, sum_ref, sacc_ref, sml_ref, squery_ref, w_out_ref,
+    kv_ref, sem, *, items, group, pair_count, head_count,
+):
+    copy = pltpu.make_async_copy(w_out_hbm, w_out_ref, sem)
+    copy.start()
+    acc_ref[...] = acc_in[...]
+    top_ref[...] = top_in[...]
+    sum_ref[...] = sum_in[...]
+    pieces = [(here0_ref, there0_ref), (here1_ref, there1_ref)]
+    project_pieces(side_ref, pieces, w_kv_ref, kv_ref, 0)
+    add_items(
+        (valid_ref, block_ref, off_ref, pos_ref), bounds_ref, base_ref, q_ref, kv_ref,
+        (top_ref, sum_ref, acc_ref), items, group, pair_count, head_count,
+    )
+    queries = summary_queries(mine_ref, q_ref, head_count)
+    squery_ref[...] = queries
+    keys = kv_early_ref.shape[1]
+    scores = jnp.concatenate(
+        [
+            lax.dot_general(queries, part[0], NT, preferred_element_type=F32)
+            for part in (kv_early_ref, kv_ref)
+        ],
+        axis=1,
+    )
+    scores = scores + jnp.concatenate([sbias_ref[:, : scores.shape[1]]] * head_count, axis=0)
+    top = jnp.max(scores, axis=1, keepdims=True)
+    weights = jnp.exp(scores - top)
+    total = jnp.sum(weights, axis=1, keepdims=True)
+    weights = weights.astype(BF16)
+    sacc_ref[...] = jnp.dot(weights[:, :keys], kv_early_ref[1], preferred_element_type=F32) + jnp.dot(
+        weights[:, keys:], kv_ref[1], preferred_element_type=F32
+    )
+    slane = lax.broadcasted_iota(jnp.int32, sml_ref.shape, 1)
+    sml_ref[...] = jnp.where(slane == 0, top, total)
+    copy.wait()
+
+
+def late_kernel(
+    valid_ref, block_ref, off_ref, pos_ref, bounds_ref, base_ref, mine_ref, side_ref,
+    q_ref, w_kv_ref, w_ref, sbias_ref, acc_ref, top_ref, sum_ref,
+    sacc_ref, sml_ref, squery_ref, fresh_ref, here_ref, there_ref,
+    own_ref, other_ref, kv_ref, mix_ref, peak_ref, total_ref,
+    *, items, group, pair_count, head_count,
+):
+    tok_rows, cols_all = mix_ref.shape
+    fresh_rows = fresh_ref.shape[1]
+    mix_ref[...] = acc_ref[...]
+    peak_ref[...] = top_ref[...]
+    total_ref[...] = sum_ref[...]
+    kv_ref[:, :fresh_rows] = fresh_ref[...]
+    project_pieces(side_ref, [(here_ref, there_ref)], w_kv_ref, kv_ref, fresh_rows)
+    add_items(
+        (valid_ref, block_ref, off_ref, pos_ref), bounds_ref, base_ref, q_ref, kv_ref,
+        (peak_ref, total_ref, mix_ref), items, group, pair_count, head_count,
+    )
+
+    scores = lax.dot_general(squery_ref[...], kv_ref[0], NT, preferred_element_type=F32)
+    keys = scores.shape[1]
+    scores = scores + jnp.concatenate([sbias_ref[:, -keys:]] * head_count, axis=0)
+    before = sml_ref[:, 0:1]
+    top = jnp.maximum(before, jnp.max(scores, axis=1, keepdims=True))
+    weights = jnp.exp(scores - top)
+    fade = jnp.exp(before - top)
+    total = sml_ref[:, 1:2] * fade + jnp.sum(weights, axis=1, keepdims=True)
+    mixture = sacc_ref[...] * fade + jnp.dot(
+        weights.astype(BF16), kv_ref[1], preferred_element_type=F32
+    )
+    mixture = mixture / total
+    slane = lax.broadcasted_iota(jnp.int32, (8, cols_all), 1)
+    summary = jnp.zeros((8, cols_all), F32)
+    for h in range(head_count):
+        summary = jnp.where(
+            (slane >= h * HEAD) & (slane < (h + 1) * HEAD), mixture[h * 8 : (h + 1) * 8], summary
+        )
+
+    all_rows = lax.broadcasted_iota(jnp.int32, (tok_rows, 1), 0)
+    columns = []
+    for pair in range(head_count // PAIR):
+        cols = slice(pair * LANES, (pair + 1) * LANES)
+        part = mix_ref[:, cols] / total_ref[:, cols]
+        for u in range(mine_ref.shape[0]):
+            part = jnp.where(all_rows == mine_ref[u], summary[u : u + 1, cols], part)
+        columns.append(part.astype(BF16))
+    attention = jnp.concatenate(columns, axis=1)
+    half = w_ref.shape[1] // 2
+    low = pl.multiple_of(side_ref[0] * half, half)
+    high = pl.multiple_of((1 - side_ref[0]) * half, half)
+    other_ref[...] = jnp.dot(
+        attention, w_ref[:, pl.ds(high, half)], preferred_element_type=F32
+    ).astype(BF16)
+    own_ref[...] = jnp.dot(
+        attention, w_ref[:, pl.ds(low, half)], preferred_element_type=F32
+    ).astype(BF16)
+
+
+def gathered(
+    tokens, w_qkv, w_out, ln_gain, ln_bias, random_blocks, summary_pos, summary_blocks, pair_lengths
+):
+    tok_rows, half = tokens.shape[1:]
+    cols = w_qkv.shape[2]
+    head_count = cols // HEAD
+    full_width = w_out.shape[1]
+    ctx_count = lax.axis_size("ctx")
+    ctx_index = lax.axis_index("ctx")
+    side = lax.axis_index("heads").astype(jnp.int32).reshape(1)
+    block_count = tok_rows // BLOCK
+    total_blocks = block_count * ctx_count
+    pair_count = pair_lengths.shape[1]
+    own_tokens = tokens[0]
+    piece = tok_rows // 2
+    piece_blocks = block_count // 2
+    arrival = jnp.array([0, 1, 2, 4, 3, 5, 6, 7], jnp.int32)
+    place_of = jnp.array([0, 1, 2, 4, 3, 5, 6, 7], jnp.int32)
+    early_count, late_count, piece_count = 4, 6, 2 * ctx_count
+    early_rows, late_rows = early_count * piece, (piece_count - late_count) * piece
+
+    bounds = jnp.cumsum(pair_lengths[0]).astype(jnp.int32)
+    base = (ctx_index * tok_rows).astype(jnp.int32).reshape(1)
+    picks = random_blocks[0]
+    rand_count = picks.shape[1]
+    block_ids = ctx_index * block_count + jnp.arange(block_count, dtype=jnp.int32)
+    window = block_ids[:, None] + jnp.arange(-1, 2, dtype=jnp.int32)[None, :]
+    listed = jnp.concatenate([window, picks], axis=1)
+    items = listed.shape[1]
+    inside = (listed >= 0) & (listed < total_blocks)
+    slot_of = (listed // block_count) ^ ctx_index
+    within = listed % block_count
+    number = slot_of * 2 + within // piece_blocks
+    place = jnp.sum(
+        jnp.where(number[..., None] == jnp.arange(piece_count), place_of, 0), axis=-1
+    )
+    row = place * piece + (within % piece_blocks) * BLOCK
+    early = inside & (place < early_count)
+    early_off = jnp.where(early, row, 0).reshape(-1)
+    early_pos = jnp.where(early, listed * BLOCK, -(2**30)).reshape(-1)
+    capacity = max(2, -(-block_count * rand_count // ctx_count))
+
+    def item_list(first, last, count):
+        held = (inside & (place >= first) & (place < last)).reshape(-1)
+        rank = jnp.cumsum(held.astype(jnp.int32)) - 1
+        chosen = held[None, :] & (rank[None, :] == jnp.arange(count, dtype=jnp.int32)[:, None])
+
+        def compact(x):
+            return jnp.sum(jnp.where(chosen, x.reshape(-1)[None, :], 0), axis=1).astype(jnp.int32)
+
+        blocks = jnp.broadcast_to(jnp.arange(block_count, dtype=jnp.int32)[:, None], listed.shape)
+        valid = jnp.any(chosen, axis=1).astype(jnp.int32)
+        return valid, compact(blocks), compact(row - first * piece), compact(listed * BLOCK)
+
+    middle_items, late_items = 2 * capacity + 1, capacity + 1
+    middle_list = item_list(early_count, late_count, middle_items)
+    late_list = item_list(late_count, piece_count, late_items)
+    summaries = summary_pos.shape[1]
+    per_device = summaries // ctx_count
+    mine_pos = lax.dynamic_slice_in_dim(summary_pos[0], ctx_index * per_device, per_device, 0)
+    mine_lists = lax.dynamic_slice_in_dim(summary_blocks[0], ctx_index * per_device, per_device, 0)
+    mine = (mine_pos - ctx_index * tok_rows).astype(jnp.int32)
+    piece_first = ((arrival // 2) ^ ctx_index) * block_count + (arrival % 2) * piece_blocks
+    key_blocks = (piece_first[:, None] + jnp.arange(piece_blocks, dtype=jnp.int32)).reshape(-1)
+    in_list = jnp.any(mine_lists[:, :, None] == key_blocks[None, None, :], axis=1)
+    key_pos = (key_blocks[:, None] * BLOCK + jnp.arange(BLOCK, dtype=jnp.int32)).reshape(-1)
+    seen = jnp.repeat(in_list, BLOCK, axis=1) & (
+        segment_ids(key_pos, bounds)[None, :] == segment_ids(mine_pos, bounds)[:, None]
+    )
+    sbias = jnp.pad(jnp.where(seen, 0.0, MASKED), ((0, 8 - per_device), (0, 0)))
+    tables = (early_off, early_pos, middle_list, late_list, bounds, mine, base, sbias)
+
+    swap = [(0, 1), (1, 0)]
+
+    def other_half(x):
+        return lax.ppermute(x, "heads", swap)
+
+    def from_slot(x, slot):
+        return lax.ppermute(x, "ctx", [(i, i ^ slot) for i in range(ctx_count)])
+
+    def array(*shape, dtype=F32):
+        return jax.ShapeDtypeStruct(shape, dtype)
+
+    def like(arrays):
+        return [pltpu.VMEM(x.shape, x.dtype) for x in arrays]
+
+    def whole_call(kernel, scalars, args, far_args, outs, far_outs, scratch, work, name, **sizes):
+        far = pl.BlockSpec(memory_space=pltpu.HBM)
+        near = pl.BlockSpec(memory_space=pltpu.VMEM)
+        return pl.pallas_call(
+            functools.partial(kernel, **sizes),
+            in_specs=[pl.BlockSpec(memory_space=pltpu.SMEM)] * len(scalars)
+            + [near] * len(args)
+            + [far] * len(far_args),
+            out_specs=[far] * len(far_outs) + [near] * len(outs),
+            out_shape=far_outs + outs,
+            scratch_shapes=scratch,
+            compiler_params=params(),
+            cost_estimate=pl.CostEstimate(
+                flops=int(work * 1e9), bytes_accessed=int(work * 3.5e6), transcendentals=0
+            ),
+            name=name,
+        )(*scalars, *args, *far_args)
+
+    low, high = own_tokens[:piece], own_tokens[piece:]
+    own_there = other_half(own_tokens)
+    here2a = from_slot(low, 2)
+    here1a = from_slot(low, 1)
+    here2a, here1a, high, tables = lax.optimization_barrier((here2a, here1a, high, tables))
+    early_off, early_pos, middle_list, late_list, bounds, mine, base, sbias = tables
+    here2b = from_slot(high, 2)
+    here1b = from_slot(high, 1)
+    there1a, there2a = other_half(here1a), other_half(here2a)
+    queries, own_kv, w_kv = whole_call(
+        first_kernel,
+        [side],
+        [own_tokens, own_there],
+        [w_qkv],
+        [array(tok_rows, cols, dtype=BF16), array(2, tok_rows, cols, dtype=BF16)]
+        + [array(2, 2 * half, cols, dtype=BF16)],
+        [],
+        [pltpu.VMEM((2 * half, cols), BF16), pltpu.SemaphoreType.DMA((3,))],
+        2,
+        "own_projections",
+    )
+    here2b, here1b, w_kv = lax.optimization_barrier((here2b, here1b, w_kv))
+    here3b = from_slot(here2b, 1)
+    there1b, there2b = other_half(here1b), other_half(here2b)
+    piece_kv = array(2, piece, cols, dtype=BF16)
+    kv1a, kv2a = whole_call(
+        pieces_kernel,
+        [side],
+        [w_kv, here1a, there1a, here2a, there2a],
+        [],
+        [piece_kv, piece_kv],
+        [],
+        [],
+        1,
+        "piece_projections",
+    )
+    kv3a = from_slot(kv2a, 1)
+    there3b = other_half(here3b)
+
+    sizes = dict(pair_count=pair_count, head_count=head_count)
+    state = [array(tok_rows, cols)] * 3
+    *state, kv = whole_call(
+        early_kernel,
+        [early_off, early_pos, bounds, base],
+        [queries, own_kv, kv1a, kv2a],
+        [],
+        state + [array(2, early_rows, cols, dtype=BF16)],
+        [],
+        [
+            pltpu.VMEM((BLOCK, items * BLOCK), F32),
+            pltpu.VMEM((head_count // PAIR, PAIR * BLOCK, items * BLOCK), F32),
+            pltpu.SemaphoreType.DMA((3,)),
+        ],
+        7,
+        "early_attention",
+        items=items,
+        **sizes,
+    )
+    srows = 8 * head_count
+    *state, sacc, sml, squery, w_out_near = whole_call(
+        middle_kernel,
+        [*middle_list, bounds, base, mine, side],
+        [queries, w_kv, kv, sbias, *state, here1b, there1b, here2b, there2b],
+        [w_out],
+        [array(tok_rows, cols)] * 3
+        + [array(srows, cols), array(srows, LANES), array(srows, cols, dtype=BF16)]
+        + [array(*w_out.shape, dtype=BF16)],
+        [],
+        [pltpu.VMEM((2, 2 * piece, cols), BF16), pltpu.SemaphoreType.DMA],
+        5,
+        "middle_attention",
+        items=middle_items,
+        group=4,
+        **sizes,
+    )
+    own_term, other_term = whole_call(
+        late_kernel,
+        [*late_list, bounds, base, mine, side],
+        [queries, w_kv, w_out_near, sbias, *state, sacc, sml, squery, kv3a, here3b, there3b],
+        [],
+        [array(tok_rows, half, dtype=BF16)] * 2,
+        [],
+        [pltpu.VMEM((2, late_rows, cols), BF16)] + [pltpu.VMEM((tok_rows, cols), F32)] * 3,
+        4,
+        "late_attention",
+        items=late_items,
+        group=4,
+        **sizes,
+    )
+
+    received = other_half(other_term)
+    hidden = own_tokens.astype(F32) + (own_term.astype(F32) + received.astype(F32))
+    sums = jnp.stack([jnp.sum(hidden, axis=1), jnp.sum(hidden * hidden, axis=1)])
+    sums = sums + other_half(sums)
+    row_mean = sums[0] / full_width
+    row_var = sums[1] / full_width - row_mean * row_mean
+    normed = (hidden - row_mean[:, None]) * lax.rsqrt(row_var + 1e-05)[:, None] * ln_gain + ln_bias
+    return normed.astype(BF16)[None]
+
+
+def shards(*arrays):
+    tokens, w_qkv, random_blocks = arrays[0], arrays[1], arrays[5]
+    ctx_count = lax.axis_size("ctx")
+    picked = random_blocks.shape[1] * random_blocks.shape[2]
+    if (
+        lax.axis_size("heads") == 2
+        and ctx_count == 4
+        and picked >= ctx_count
+        and tokens.shape[1] % (2 * BLOCK) == 0
+        and w_qkv.shape[2] % LANES == 0
+        and arrays[6].shape[1] // ctx_count <= 8
+    ):
+        return gathered(*arrays)
+    return requested(*arrays)
+
+
 def solution(mesh):
     in_specs = (
         P(("groups", "dp"), "ctx", "heads"),

time: 257 us -> 74.1 us (0.29)
  blocking collectives: 97.2 us -> 0 us
  local copies, waits for them, and re-layouts: 43.4 us -> 6.81 us
  matrix products: 24.7 us -> 0 us
  Pallas kernels: 0 us -> 19.5 us
  other arithmetic: 25 us -> 6.32 us
  waiting for transfers between devices: 35 us -> 21 us
  between operations: 13.7 us -> 0.25 us
  starting transfers between devices: 17 us -> 20.1 us
    all_gather x1 -> x0, blocking collectives: 64.8 us -> none  [shards(): all_queries = lax.all_gather(summary_query, 'ctx', axis=0, tiled=True)]
    psum x2 -> x0, blocking collectives: 21.7 us -> none  [the longest x1 16.7 us: shards(): lax.psum(totals_all.astype(jnp.bfloat16), 'ctx').astype(jnp.float32)]
    ppermute x2 -> x14, waiting for transfers between devices: 0.01 us -> 21 us  [the longest x8 16.7 us: other_half(): return lax.ppermute(x, 'heads', swap)]
    pallas_call x0 -> x5, Pallas kernels: none -> 19.5 us  [whole_call(): pl.pallas_call(functools.partial(kernel, **sizes), in_specs=[pl.BlockSpec...]
    reduce_scatter x1 -> x0, waiting for transfers between devices: 18.7 us -> none  [shards(): lax.psum_scatter(partial_value.astype(jnp.bfloat16), 'heads', scatter_dim...]
    dot_general x5 -> x0, matrix products: 14.6 us -> none  [the longest x1 5.84 us: attend(): jnp.einsum('ghqk,gkhe->gqhe', weights.astype(jnp.bfloat16), value_heads,...]
    ppermute x2 -> x14, starting transfers between devices: 5.92 us -> 20.1 us  [the longest x6 10.1 us: from_slot(): return lax.ppermute(x, 'ctx', [(i, i ^ slot) for i in range(ctx_count)])]
    slice x8 -> x1, local copies, waits for them, and re-layouts: 14.6 us -> 1.08 us  [gathered(): low, high = (own_tokens[:piece], own_tokens[piece:])]
  transfers between devices with their start and end apart: 6 -> 14, of which waited for: 3 -> 8; matrix products, arithmetic and copies ran while one was open for 12% -> 10% of each run, Pallas kernels for 0% -> 20%
where the time goes in v3:
time: 74.1 us; the launch traced here: 73.9 us
  waiting for transfers between devices  21 us (28%)
  starting transfers between devices  20.1 us (27%)
  Pallas kernels  19.5 us (26%)
  local copies, waits for them, and re-layouts  6.81 us (9%)
  other arithmetic  6.32 us (9%)
    pallas_call x5, Pallas kernels, whole_call(): pl.pallas_call(functools.partial(kernel, **sizes), in_specs=[pl.BlockSpec...  19.5 us
    ppermute x8, waiting for transfers between devices, other_half(): return lax.ppermute(x, 'heads', swap)  16.7 us
    ppermute x6, starting transfers between devices, from_slot(): return lax.ppermute(x, 'ctx', [(i, i ^ slot) for i in range(ctx_count)])  10.1 us
    ppermute x8, starting transfers between devices, other_half(): return lax.ppermute(x, 'heads', swap)  9.99 us
    ppermute x6, waiting for transfers between devices, from_slot(): return lax.ppermute(x, 'ctx', [(i, i ^ slot) for i in range(ctx_count)])  4.3 us
    unnamed x15, local copies, waits for them, and re-layouts  3.04 us
  transfers between devices with their start and end apart: 14, of which 8 were waited for; matrix products, arithmetic and copies ran while one was open for 10% of the time, Pallas kernels for 20%

profile of v3, /device:TPU:0, one launch (start us, length us, event | category | flops | bytes accessed | tf_op | source)
XLA Modules:
  0.0 73.9 jit_solution(12278092348113793983)
XLA Ops:
  0.0 1.1 %slice_bitcast_fusion = (bf16[256,512]{1,0:T(8,128)(2,1)S(1)}, bf16[256,512]{1,0:T(8,128)(2,1)S(1)}) fusion(bf16[1,512,512]{2,1,0:T(8,128)(2,1)} %param.11), kind=kLoop, calls=%fused_computation.5 | loop fusion | bytes 1048576 | tf_op jit(solution)/shard_map/slice | solution.py:654
  1.1 4.1 %collective-permute-start = (bf16[256,512]{1,0:T(8,128)(2,1)S(1)}, bf16[256,512]{1,0:T(8,128)(2,1)S(1)}, u32[]{:S(2)}, u32[]{:S(2)}) collective-permute-start(bf16[256,512]{1,0:T(8,128)(2,1)S(1)} %get-tuple-element.102), channel_id=1, source_target_pairs={{0,8},{4,12},{8,0},{12,4},{1,9},{5,13},{9,1},{13,5},{2,10},{6,14},... | collective-permute-start | bytes 786440 | tf_op jit(solution)/shard_map/ppermute | solution.py:628
  5.2 1.6 %collective-permute-start.1 = (bf16[256,512]{1,0:T(8,128)(2,1)S(1)}, bf16[256,512]{1,0:T(8,128)(2,1)S(1)}, u32[]{:S(2)}, u32[]{:S(2)}) collective-permute-start(bf16[256,512]{1,0:T(8,128)(2,1)S(1)} %get-tuple-element.102), channel_id=1, source_target_pairs={{0,4},{4,0},{8,12},{12,8},{1,5},{5,1},{9,13},{13,9},{2,6},{6,2},{1... | collective-permute-start | bytes 786440 | tf_op jit(solution)/shard_map/ppermute | solution.py:628
  6.8 1.5 %collective-permute-start.2 = (bf16[512,512]{1,0:T(8,128)(2,1)}, bf16[512,512]{1,0:T(8,128)(2,1)S(1)}, u32[]{:S(2)}, u32[]{:S(2)}) collective-permute-start(bf16[512,512]{1,0:T(8,128)(2,1)} %bitcast.34), channel_id=1, source_target_pairs={{0,2},{2,0},{1,3},{3,1},{4,6},{6,4},{5,7},{7,5},{8,10},{10,8},{9,1... | collective-permute-start | bytes 1572872 | tf_op jit(solution)/shard_map/ppermute | solution.py:625
  15.9 1.3 %collective-permute-done.refs_2_ = bf16[256,512]{1,0:T(8,128)(2,1)S(1)} collective-permute-done((bf16[256,512]{1,0:T(8,128)(2,1)S(1)}, bf16[256,512]{1,0:T(8,128)(2,1)S(1)}, u32[]{:S(2)}, u32[]{:S(2)}) %collective-permute-start) | collective-permute-done | bytes 262176 | tf_op jit(solution)/shard_map/ppermute | solution.py:628
  17.4 1.4 %collective-permute-start.3 = (bf16[256,512]{1,0:T(8,128)(2,1)S(1)}, bf16[256,512]{1,0:T(8,128)(2,1)S(1)}, u32[]{:S(2)}, u32[]{:S(2)}) collective-permute-start(bf16[256,512]{1,0:T(8,128)(2,1)S(1)} %get-tuple-element.51), channel_id=1, source_target_pairs={{0,8},{4,12},{8,0},{12,4},{1,9},{5,13},{9,1},{13,5},{2,10},{6,14},... | collective-permute-start | bytes 786440 | tf_op jit(solution)/shard_map/ppermute | solution.py:628
  18.8 2.4 %collective-permute-start.4 = (bf16[256,512]{1,0:T(8,128)(2,1)S(1)}, bf16[256,512]{1,0:T(8,128)(2,1)S(1)}, u32[]{:S(2)}, u32[]{:S(2)}) collective-permute-start(bf16[256,512]{1,0:T(8,128)(2,1)S(1)} %get-tuple-element.51), channel_id=1, source_target_pairs={{0,4},{4,0},{8,12},{12,8},{1,5},{5,1},{9,13},{13,9},{2,6},{6,2},{1... | collective-permute-start | bytes 786440 | tf_op jit(solution)/shard_map/ppermute | solution.py:628
  21.2 1.5 %collective-permute-start.5 = (bf16[256,512]{1,0:T(8,128)(2,1)S(1)}, bf16[256,512]{1,0:T(8,128)(2,1)S(1)}, u32[]{:S(2)}, u32[]{:S(2)}) collective-permute-start(bf16[256,512]{1,0:T(8,128)(2,1)S(1)} %collective-permute-done.1.refs_0_), channel_id=1, source_target_pairs={{0,2},{2,0},{1,3},{3,1},{4,6},{6,4},{5,7},{7,5},{8,10},{10,8},{9,1... | collective-permute-start | bytes 786440 | tf_op jit(solution)/shard_map/ppermute | solution.py:625
  24.3 1.9 %copy-done.3 = bf16[3,1024,512]{2,1,0:T(8,128)(2,1)S(1)} copy-done((bf16[3,1024,512]{2,1,0:T(8,128)(2,1)S(1)}, bf16[3,1024,512]{2,1,0:T(8,128)(2,1)}, u32[]{:S(2)}) %copy-start.3) | copy-done | bytes 3145752
  26.2 2.4 %own_projections.1 = (bf16[512,512]{1,0:T(8,128)(2,1)S(1)}, bf16[2,512,512]{2,1,0:T(8,128)(2,1)S(1)}, bf16[2,1024,512]{2,1,0:T(8,128)(2,1)S(1)}) custom-call(s32[1]{0:T(128)} %bitcast.11.side_ref, bf16[512,512]{1,0:T(8,128)(2,1)S(1)} %bitcast.35, bf16[512,512]{1,0:T(8,128)(2,1)S(1)} %collective-permute-done.2.there_ref, bf16[3,1024,512]{2,1,0:T(8,128)(2,1)S(1)} %copy-done.3), custom_call_target="tpu_custom_call" | custom-call | flops 2000000000 | bytes 7000000 | tf_op jit(solution)/shard_map/own_projections/pallas_call | solution.py:639
  28.6 2.7 %collective-permute-done.3.here1_ref = bf16[256,512]{1,0:T(8,128)(2,1)S(1)} collective-permute-done((bf16[256,512]{1,0:T(8,128)(2,1)S(1)}, bf16[256,512]{1,0:T(8,128)(2,1)S(1)}, u32[]{:S(2)}, u32[]{:S(2)}) %collective-permute-start.3) | collective-permute-done | bytes 262176 | tf_op jit(solution)/shard_map/ppermute | solution.py:628
  31.3 1.2 %collective-permute-start.8 = (bf16[256,512]{1,0:T(8,128)(2,1)S(1)}, bf16[256,512]{1,0:T(8,128)(2,1)S(1)}, u32[]{:S(2)}, u32[]{:S(2)}) collective-permute-start(bf16[256,512]{1,0:T(8,128)(2,1)S(1)} %collective-permute-done.3.here1_ref), channel_id=1, source_target_pairs={{0,2},{2,0},{1,3},{3,1},{4,6},{6,4},{5,7},{7,5},{8,10},{10,8},{9,1... | collective-permute-start | bytes 786440 | tf_op jit(solution)/shard_map/ppermute | solution.py:625
  33.7 2.4 %collective-permute-done.6.refs_3_ = bf16[256,512]{1,0:T(8,128)(2,1)S(1)} collective-permute-done((bf16[256,512]{1,0:T(8,128)(2,1)S(1)}, bf16[256,512]{1,0:T(8,128)(2,1)S(1)}, u32[]{:S(2)}, u32[]{:S(2)}) %collective-permute-start.6) | collective-permute-done | bytes 262176 | tf_op jit(solution)/shard_map/ppermute | solution.py:625
  36.1 1.2 %piece_projections.1 = (bf16[2,256,512]{2,1,0:T(8,128)(2,1)S(1)}, bf16[2,256,512]{2,1,0:T(8,128)(2,1)S(1)}) custom-call(s32[1]{0:T(128)} %bitcast.11.side_ref, bf16[2,1024,512]{2,1,0:T(8,128)(2,1)S(1)} %get-tuple-element.53.w_kv_ref, bf16[256,512]{1,0:T(8,128)(2,1)S(1)} %collective-permute-done.1.refs_0_, ...), custom_call_target="tpu_custom_call" | custom-call | flops 1000000000 | bytes 3500000 | tf_op jit(solution)/shard_map/piece_projections/pallas_call | solution.py:639
  37.4 6.0 %early_attention.1 = (f32[512,512]{1,0:T(8,128)S(1)}, f32[512,512]{1,0:T(8,128)S(1)}, f32[512,512]{1,0:T(8,128)S(1)}, bf16[2,1024,512]{2,1,0:T(8,128)(2,1)S(1)}) custom-call(s32[24]{0:T(128)S(1)} %get-tuple-element.58.off_ref, s32[24]{0:T(128)S(1)} %get-tuple-element.59.pos_ref, s32[4]{0:T(128)S(1)} %bitcast.38, s32[1]{0:T(128)} %bitcast.8.base_ref, ...), custom_call_target="tpu_custom_call" | custom-call | flops 7000000000 | bytes 24500000 | tf_op jit(solution)/shard_map/early_attention/pallas_call | solution.py:639
  43.4 1.6 %collective-permute-start.11 = (bf16[256,512]{1,0:T(8,128)(2,1)S(1)}, bf16[256,512]{1,0:T(8,128)(2,1)S(1)}, u32[]{:S(2)}, u32[]{:S(2)}) collective-permute-start(bf16[256,512]{1,0:T(8,128)(2,1)S(1)} %collective-permute-done.10.here_ref), channel_id=1, source_target_pairs={{0,2},{2,0},{1,3},{3,1},{4,6},{6,4},{5,7},{7,5},{8,10},{10,8},{9,1... | collective-permute-start | bytes 786440 | tf_op jit(solution)/shard_map/ppermute | solution.py:625
  45.0 2.3 %collective-permute-done.7.there0_ref = bf16[256,512]{1,0:T(8,128)(2,1)S(1)} collective-permute-done((bf16[256,512]{1,0:T(8,128)(2,1)S(1)}, bf16[256,512]{1,0:T(8,128)(2,1)S(1)}, u32[]{:S(2)}, u32[]{:S(2)}) %collective-permute-start.7) | collective-permute-done | bytes 262176 | tf_op jit(solution)/shard_map/ppermute | solution.py:625
  47.3 5.0 %middle_attention.1 = (f32[512,512]{1,0:T(8,128)S(1)}, f32[512,512]{1,0:T(8,128)S(1)}, f32[512,512]{1,0:T(8,128)S(1)}, f32[64,512]{1,0:T(8,128)S(1)}, f32[64,128...) custom-call(s32[7]{0:T(128)S(1)} %convert_element_type.52.valid_ref, ...), custom_call_target="tpu_custom_call" | custom-call | flops 5000000000 | bytes 17500000 | tf_op jit(solution)/shard_map/middle_attention/pallas_call | solution.py:639
  52.4 4.8 %late_attention.1 = (bf16[512,512]{1,0:T(8,128)(2,1)S(1)}, bf16[512,512]{1,0:T(8,128)(2,1)S(1)}) custom-call(s32[4]{0:T(128)S(1)} %convert_element_type.54.valid_ref, s32[4]{0:T(128)S(1)} %get-tuple-element.44.block_ref, s32[4]{0:T(128)S(1)} %get-tuple-element.45.off_ref, s32[4]{0:T(128)S(1)} %get-tuple-element.46.pos_ref, s32[4]{0:T(128)S(1)} %bitcast.40, ...), custom_call_target="tpu_custom_call" | custom-call | flops 4000000000 | bytes 14000000 | tf_op jit(solution)/shard_map/late_attention/pallas_call | solution.py:639
  57.2 1.6 %collective-permute-start.12 = (bf16[512,512]{1,0:T(8,128)(2,1)S(1)}, bf16[512,512]{1,0:T(8,128)(2,1)S(1)}, u32[]{:S(2)}, u32[]{:S(2)}) collective-permute-start(bf16[512,512]{1,0:T(8,128)(2,1)S(1)} %get-tuple-element.80), channel_id=1, source_target_pairs={{0,2},{2,0},{1,3},{3,1},{4,6},{6,4},{5,7},{7,5},{8,10},{10,8},{9,1... | collective-permute-start | bytes 1572872 | tf_op jit(solution)/shard_map/ppermute | solution.py:625
  58.8 9.8 %collective-permute-done.12 = bf16[512,512]{1,0:T(8,128)(2,1)S(1)} collective-permute-done((bf16[512,512]{1,0:T(8,128)(2,1)S(1)}, bf16[512,512]{1,0:T(8,128)(2,1)S(1)}, u32[]{:S(2)}, u32[]{:S(2)}) %collective-permute-start.12) | collective-permute-done | bytes 524320 | tf_op jit(solution)/shard_map/ppermute | solution.py:625
  69.0 1.6 %collective-permute-start.13 = (f32[2,512]{1,0:T(2,128)S(1)}, f32[2,512]{1,0:T(2,128)S(1)}, u32[]{:S(2)}, u32[]{:S(2)}) collective-permute-start(f32[2,512]{1,0:T(2,128)S(1)} %pad_maximum_fusion), channel_id=1, source_target_pairs={{0,2},{2,0},{1,3},{3,1},{4,6},{6,4},{5,7},{7,5},{8,10},{10,8},{9,1... | collective-permute-start | bytes 12296 | tf_op jit(solution)/shard_map/ppermute | solution.py:625
  70.6 2.1 %collective-permute-done.13 = f32[2,512]{1,0:T(2,128)S(1)} collective-permute-done((f32[2,512]{1,0:T(2,128)S(1)}, f32[2,512]{1,0:T(2,128)S(1)}, u32[]{:S(2)}, u32[]{:S(2)}) %collective-permute-start.13) | collective-permute-done | bytes 4128 | tf_op jit(solution)/shard_map/ppermute | solution.py:625
  72.7 1.1 %fusion = bf16[1,512,512]{2,1,0:T(8,128)(2,1)} fusion(f32[512]{0:T(512)S(1)} %copy-done.5, f32[512]{0:T(512)S(1)} %copy-done.6, f32[512]{0:T(512)S(1)} %add_rsqrt_fusion, f32[512]{0:T(512)S(1)} %bitcast.48, bf16[512,512]{1,0:T(8,128)(2,1)S(1)} %collective-permute-done.12, bf16[512,512]{1,0:T(8,128)(2,1)S(1)} %get-tuple-element.79, ...), kind=kLoop, calls=%fused_computation.3 | loop fusion | flops 2621440 | bytes 2105344 | tf_op jit(solution)/shard_map/broadcast_in_dim | solution.py:751
  (87 shorter events, 11.0 us)
Async XLA Ops:
  0.0 13.8 %copy-start = (s32[1,16,8]{1,2,0:T(8,128)S(1)}, s32[1,16,8]{1,2,0:T(8,128)}, u32[]{:S(2)}) copy-start(s32[1,16,8]{1,2,0:T(8,128)} %param.18) | copy-start | bytes 1540
  1.1 16.1 %collective-permute-start = (bf16[256,512]{1,0:T(8,128)(2,1)S(1)}, bf16[256,512]{1,0:T(8,128)(2,1)S(1)}, u32[]{:S(2)}, u32[]{:S(2)}) collective-permute-start(bf16[256,512]{1,0:T(8,128)(2,1)S(1)} %get-tuple-element.102), channel_id=1, source_target_pairs={{0,8},{4,12},{8,0},{12,4},{1,9},{5,13},{9,1},{13,5},{2,10},{6,14},... | collective-permute-start | bytes 786440 | tf_op jit(solution)/shard_map/ppermute | solution.py:628
  5.2 12.2 %collective-permute-start.1 = (bf16[256,512]{1,0:T(8,128)(2,1)S(1)}, bf16[256,512]{1,0:T(8,128)(2,1)S(1)}, u32[]{:S(2)}, u32[]{:S(2)}) collective-permute-start(bf16[256,512]{1,0:T(8,128)(2,1)S(1)} %get-tuple-element.102), channel_id=1, source_target_pairs={{0,4},{4,0},{8,12},{12,8},{1,5},{5,1},{9,13},{13,9},{2,6},{6,2},{1... | collective-permute-start | bytes 786440 | tf_op jit(solution)/shard_map/ppermute | solution.py:628
  6.8 16.5 %collective-permute-start.2 = (bf16[512,512]{1,0:T(8,128)(2,1)}, bf16[512,512]{1,0:T(8,128)(2,1)S(1)}, u32[]{:S(2)}, u32[]{:S(2)}) collective-permute-start(bf16[512,512]{1,0:T(8,128)(2,1)} %bitcast.34), channel_id=1, source_target_pairs={{0,2},{2,0},{1,3},{3,1},{4,6},{6,4},{5,7},{7,5},{8,10},{10,8},{9,1... | collective-permute-start | bytes 1572872 | tf_op jit(solution)/shard_map/ppermute | solution.py:625
  17.4 13.9 %collective-permute-start.3 = (bf16[256,512]{1,0:T(8,128)(2,1)S(1)}, bf16[256,512]{1,0:T(8,128)(2,1)S(1)}, u32[]{:S(2)}, u32[]{:S(2)}) collective-permute-start(bf16[256,512]{1,0:T(8,128)(2,1)S(1)} %get-tuple-element.51), channel_id=1, source_target_pairs={{0,8},{4,12},{8,0},{12,4},{1,9},{5,13},{9,1},{13,5},{2,10},{6,14},... | collective-permute-start | bytes 786440 | tf_op jit(solution)/shard_map/ppermute | solution.py:628
  18.8 12.6 %collective-permute-start.4 = (bf16[256,512]{1,0:T(8,128)(2,1)S(1)}, bf16[256,512]{1,0:T(8,128)(2,1)S(1)}, u32[]{:S(2)}, u32[]{:S(2)}) collective-permute-start(bf16[256,512]{1,0:T(8,128)(2,1)S(1)} %get-tuple-element.51), channel_id=1, source_target_pairs={{0,4},{4,0},{8,12},{12,8},{1,5},{5,1},{9,13},{13,9},{2,6},{6,2},{1... | collective-permute-start | bytes 786440 | tf_op jit(solution)/shard_map/ppermute | solution.py:628
  21.2 12.5 %collective-permute-start.5 = (bf16[256,512]{1,0:T(8,128)(2,1)S(1)}, bf16[256,512]{1,0:T(8,128)(2,1)S(1)}, u32[]{:S(2)}, u32[]{:S(2)}) collective-permute-start(bf16[256,512]{1,0:T(8,128)(2,1)S(1)} %collective-permute-done.1.refs_0_), channel_id=1, source_target_pairs={{0,2},{2,0},{1,3},{3,1},{4,6},{6,4},{5,7},{7,5},{8,10},{10,8},{9,1... | collective-permute-start | bytes 786440 | tf_op jit(solution)/shard_map/ppermute | solution.py:625
  22.7 13.4 %collective-permute-start.6 = (bf16[256,512]{1,0:T(8,128)(2,1)S(1)}, bf16[256,512]{1,0:T(8,128)(2,1)S(1)}, u32[]{:S(2)}, u32[]{:S(2)}) collective-permute-start(bf16[256,512]{1,0:T(8,128)(2,1)S(1)} %collective-permute-done.refs_2_), channel_id=1, source_target_pairs={{0,2},{2,0},{1,3},{3,1},{4,6},{6,4},{5,7},{7,5},{8,10},{10,8},{9,1... | collective-permute-start | bytes 786440 | tf_op jit(solution)/shard_map/ppermute | solution.py:625
  23.2 1.0 %copy-start.1 = (bf16[1,512,512]{2,1,0:T(8,128)(2,1)S(1)}, bf16[1,512,512]{2,1,0:T(8,128)(2,1)}, u32[]{:S(2)}) copy-start(bf16[1,512,512]{2,1,0:T(8,128)(2,1)} %param.11) | copy-start | bytes 1572868
  24.3 1.9 %copy-start.3 = (bf16[3,1024,512]{2,1,0:T(8,128)(2,1)S(1)}, bf16[3,1024,512]{2,1,0:T(8,128)(2,1)}, u32[]{:S(2)}) copy-start(bf16[3,1024,512]{2,1,0:T(8,128)(2,1)} %w_hbm.1) | copy-start | bytes 9437188
  31.3 16.0 %collective-permute-start.8 = (bf16[256,512]{1,0:T(8,128)(2,1)S(1)}, bf16[256,512]{1,0:T(8,128)(2,1)S(1)}, u32[]{:S(2)}, u32[]{:S(2)}) collective-permute-start(bf16[256,512]{1,0:T(8,128)(2,1)S(1)} %collective-permute-done.3.here1_ref), channel_id=1, source_target_pairs={{0,2},{2,0},{1,3},{3,1},{4,6},{6,4},{5,7},{7,5},{8,10},{10,8},{9,1... | collective-permute-start | bytes 786440 | tf_op jit(solution)/shard_map/ppermute | solution.py:625
  32.6 10.8 %collective-permute-start.10 = (bf16[256,512]{1,0:T(8,128)(2,1)S(1)}, bf16[256,512]{1,0:T(8,128)(2,1)S(1)}, u32[]{:S(2)}, u32[]{:S(2)}) collective-permute-start(bf16[256,512]{1,0:T(8,128)(2,1)S(1)} %collective-permute-done.3.here1_ref), channel_id=1, source_target_pairs={{0,4},{4,0},{8,12},{12,8},{1,5},{5,1},{9,13},{13,9},{2,6},{6,2},{1... | collective-permute-start | bytes 786440 | tf_op jit(solution)/shard_map/ppermute | solution.py:628
  33.1 14.2 %collective-permute-start.7 = (bf16[256,512]{1,0:T(8,128)(2,1)S(1)}, bf16[256,512]{1,0:T(8,128)(2,1)S(1)}, u32[]{:S(2)}, u32[]{:S(2)}) collective-permute-start(bf16[256,512]{1,0:T(8,128)(2,1)S(1)} %collective-permute-done.4.here0_ref), channel_id=1, source_target_pairs={{0,2},{2,0},{1,3},{3,1},{4,6},{6,4},{5,7},{7,5},{8,10},{10,8},{9,1... | collective-permute-start | bytes 786440 | tf_op jit(solution)/shard_map/ppermute | solution.py:625
  37.3 15.0 %collective-permute-start.9 = (bf16[2,256,512]{2,1,0:T(8,128)(2,1)S(1)}, bf16[2,256,512]{2,1,0:T(8,128)(2,1)S(1)}, u32[]{:S(2)}, u32[]{:S(2)}) collective-permute-start(bf16[2,256,512]{2,1,0:T(8,128)(2,1)S(1)} %get-tuple-element.64.refs_1_), channel_id=1, source_target_pairs={{0,4},{4,0},{8,12},{12,8},{1,5},{5,1},{9,13},{13,9},{2,6},{6,2},{1... | collective-permute-start | bytes 1572872 | tf_op jit(solution)/shard_map/ppermute | solution.py:628
  37.4 9.9 %copy-start.4 = (bf16[512,1024]{1,0:T(8,128)(2,1)S(1)}, bf16[512,1024]{1,0:T(8,128)(2,1)}, u32[]{:S(2)}) copy-start(bf16[512,1024]{1,0:T(8,128)(2,1)} %w_out_hbm.1) | copy-start | bytes 3145732
  43.4 8.9 %collective-permute-start.11 = (bf16[256,512]{1,0:T(8,128)(2,1)S(1)}, bf16[256,512]{1,0:T(8,128)(2,1)S(1)}, u32[]{:S(2)}, u32[]{:S(2)}) collective-permute-start(bf16[256,512]{1,0:T(8,128)(2,1)S(1)} %collective-permute-done.10.here_ref), channel_id=1, source_target_pairs={{0,2},{2,0},{1,3},{3,1},{4,6},{6,4},{5,7},{7,5},{8,10},{10,8},{9,1... | collective-permute-start | bytes 786440 | tf_op jit(solution)/shard_map/ppermute | solution.py:625
  52.4 16.2 %copy-start.2 = (bf16[1,512,512]{2,1,0:T(8,128)(2,1)S(1)}, bf16[1,512,512]{2,1,0:T(8,128)(2,1)}, u32[]{:S(2)}) copy-start(bf16[1,512,512]{2,1,0:T(8,128)(2,1)} %param.11) | copy-start | bytes 1572868
  52.4 20.3 %copy-start.5 = (f32[512]{0:T(512)S(1)}, f32[512]{0:T(512)}, u32[]{:S(2)}) copy-start(f32[512]{0:T(512)} %param.15) | copy-start | bytes 6148
  52.4 20.3 %copy-start.6 = (f32[512]{0:T(512)S(1)}, f32[512]{0:T(512)}, u32[]{:S(2)}) copy-start(f32[512]{0:T(512)} %param.14) | copy-start | bytes 6148
  57.2 11.4 %collective-permute-start.12 = (bf16[512,512]{1,0:T(8,128)(2,1)S(1)}, bf16[512,512]{1,0:T(8,128)(2,1)S(1)}, u32[]{:S(2)}, u32[]{:S(2)}) collective-permute-start(bf16[512,512]{1,0:T(8,128)(2,1)S(1)} %get-tuple-element.80), channel_id=1, source_target_pairs={{0,2},{2,0},{1,3},{3,1},{4,6},{6,4},{5,7},{7,5},{8,10},{10,8},{9,1... | collective-permute-start | bytes 1572872 | tf_op jit(solution)/shard_map/ppermute | solution.py:625
  69.0 3.7 %collective-permute-start.13 = (f32[2,512]{1,0:T(2,128)S(1)}, f32[2,512]{1,0:T(2,128)S(1)}, u32[]{:S(2)}, u32[]{:S(2)}) collective-permute-start(f32[2,512]{1,0:T(2,128)S(1)} %pad_maximum_fusion), channel_id=1, source_target_pairs={{0,2},{2,0},{1,3},{3,1},{4,6},{6,4},{5,7},{7,5},{8,10},{10,8},{9,1... | collective-permute-start | bytes 12296 | tf_op jit(solution)/shard_map/ppermute | solution.py:625

commit v4 on v3

--- a/solution.py
+++ b/solution.py
@@ -248,17 +248,21 @@
     return list(zip(refs[0::2], refs[1::2]))
 
 
-def first_kernel(side_ref, here_ref, there_ref, w_hbm, q_ref, kv_ref, w_kv_ref, w_q_ref, sem):
-    copies = [pltpu.make_async_copy(w_hbm.at[0], w_q_ref, sem.at[0])]
-    copies += [
-        pltpu.make_async_copy(w_hbm.at[j + 1], w_kv_ref.at[j], sem.at[j + 1]) for j in range(2)
+def weights_kernel(w_hbm, w_q_ref, w_kv_ref, mark_ref, sem):
+    mark_ref[...] = jnp.zeros(mark_ref.shape, F32)
+    copies = [
+        pltpu.make_async_copy(w_hbm.at[0], w_q_ref, sem.at[0]),
+        pltpu.make_async_copy(w_hbm.at[pl.ds(1, 2)], w_kv_ref, sem.at[1]),
     ]
     for copy in copies:
         copy.start()
-    copies[0].wait()
+    for copy in copies:
+        copy.wait()
+
+
+def first_kernel(side_ref, here_ref, there_ref, w_q_ref, w_kv_ref, mark_ref, q_ref, kv_ref):
     q_ref[...] = project_rows(side_ref, here_ref, there_ref, w_q_ref)
     for j in range(2):
-        copies[j + 1].wait()
         kv_ref[j] = project_rows(side_ref, here_ref, there_ref, w_kv_ref.at[j])
 
 
@@ -370,10 +374,39 @@
         row += rows
 
 
+def add_summary(queries, keys, values, bias, before, head_count):
+    scores = lax.dot_general(queries, keys, NT, preferred_element_type=F32)
+    scores = scores + jnp.concatenate([bias] * head_count, axis=0)
+    top = jnp.max(scores, axis=1, keepdims=True)
+    if before is not None:
+        top = jnp.maximum(top, before[1])
+    weights = jnp.exp(scores - top)
+    total = jnp.sum(weights, axis=1, keepdims=True)
+    mixture = jnp.dot(weights.astype(BF16), values, preferred_element_type=F32)
+    if before is not None:
+        fade = jnp.exp(before[1] - top)
+        mixture = mixture + before[0] * fade
+        total = total + before[2] * fade
+    return mixture, top, total
+
+
+def store_summary(state, sacc_ref, sml_ref):
+    mixture, top, total = state
+    sacc_ref[...] = mixture
+    lane = lax.broadcasted_iota(jnp.int32, sml_ref.shape, 1)
+    sml_ref[...] = jnp.where(lane == 0, top, total)
+
+
+def load_summary(sacc_ref, sml_ref):
+    return sacc_ref[...], sml_ref[:, 0:1], sml_ref[:, 1:2]
+
+
 def early_kernel(
-    off_ref, pos_ref, bounds_ref, base_ref, q_ref, own_ref, *refs, items, pair_count, head_count
+    off_ref, pos_ref, bounds_ref, base_ref, mine_ref, q_ref, sbias_ref, own_ref, *refs,
+    items, pair_count, head_count,
 ):
-    *held, acc_ref, top_ref, sum_ref, kv_ref, bias_ref, score_ref, sem = refs
+    *held, acc_ref, top_ref, sum_ref, kv_ref, sacc_ref, sml_ref, squery_ref = refs[:-3]
+    bias_ref, score_ref, sem = refs[-3:]
     copies = []
     row = 0
     for i, part in enumerate([own_ref] + held):
@@ -387,6 +420,10 @@
         0, acc_ref.shape[0] // BLOCK, off_ref, pos_ref, bounds_ref, base_ref, q_ref, kv_ref,
         acc_ref, top_ref, sum_ref, bias_ref, score_ref, items, pair_count, head_count,
     )
+    squery_ref[...] = summary_queries(mine_ref, q_ref, head_count)
+    bias = sbias_ref[:, : kv_ref.shape[1]]
+    state = add_summary(squery_ref[...], kv_ref[0], kv_ref[1], bias, None, head_count)
+    store_summary(state, sacc_ref, sml_ref)
 
 
 def item_part(q_ref, kv_ref, first, offset, bias, head_count):
@@ -449,11 +486,11 @@
 
 
 def middle_kernel(
-    valid_ref, block_ref, off_ref, pos_ref, bounds_ref, base_ref, mine_ref, side_ref,
-    q_ref, w_kv_ref, kv_early_ref, sbias_ref, acc_in, top_in, sum_in,
+    valid_ref, block_ref, off_ref, pos_ref, bounds_ref, base_ref, side_ref,
+    q_ref, w_kv_ref, sbias_ref, acc_in, top_in, sum_in, sacc_in, sml_in, squery_ref,
     here0_ref, there0_ref, here1_ref, there1_ref, w_out_hbm,
-    acc_ref, top_ref, sum_ref, sacc_ref, sml_ref, squery_ref, w_out_ref,
-    kv_ref, sem, *, items, group, pair_count, head_count,
+    acc_ref, top_ref, sum_ref, sacc_ref, sml_ref, w_out_ref,
+    kv_ref, sem, *, items, group, pair_count, head_count, first_key,
 ):
     copy = pltpu.make_async_copy(w_out_hbm, w_out_ref, sem)
     copy.start()
@@ -466,26 +503,10 @@
         (valid_ref, block_ref, off_ref, pos_ref), bounds_ref, base_ref, q_ref, kv_ref,
         (top_ref, sum_ref, acc_ref), items, group, pair_count, head_count,
     )
-    queries = summary_queries(mine_ref, q_ref, head_count)
-    squery_ref[...] = queries
-    keys = kv_early_ref.shape[1]
-    scores = jnp.concatenate(
-        [
-            lax.dot_general(queries, part[0], NT, preferred_element_type=F32)
-            for part in (kv_early_ref, kv_ref)
-        ],
-        axis=1,
-    )
-    scores = scores + jnp.concatenate([sbias_ref[:, : scores.shape[1]]] * head_count, axis=0)
-    top = jnp.max(scores, axis=1, keepdims=True)
-    weights = jnp.exp(scores - top)
-    total = jnp.sum(weights, axis=1, keepdims=True)
-    weights = weights.astype(BF16)
-    sacc_ref[...] = jnp.dot(weights[:, :keys], kv_early_ref[1], preferred_element_type=F32) + jnp.dot(
-        weights[:, keys:], kv_ref[1], preferred_element_type=F32
-    )
-    slane = lax.broadcasted_iota(jnp.int32, sml_ref.shape, 1)
-    sml_ref[...] = jnp.where(slane == 0, top, total)
+    bias = sbias_ref[:, first_key : first_key + kv_ref.shape[1]]
+    state = load_summary(sacc_in, sml_in)
+    state = add_summary(squery_ref[...], kv_ref[0], kv_ref[1], bias, state, head_count)
+    store_summary(state, sacc_ref, sml_ref)
     copy.wait()
 
 
@@ -508,18 +529,10 @@
         (peak_ref, total_ref, mix_ref), items, group, pair_count, head_count,
     )
 
-    scores = lax.dot_general(squery_ref[...], kv_ref[0], NT, preferred_element_type=F32)
-    keys = scores.shape[1]
-    scores = scores + jnp.concatenate([sbias_ref[:, -keys:]] * head_count, axis=0)
-    before = sml_ref[:, 0:1]
-    top = jnp.maximum(before, jnp.max(scores, axis=1, keepdims=True))
-    weights = jnp.exp(scores - top)
-    fade = jnp.exp(before - top)
-    total = sml_ref[:, 1:2] * fade + jnp.sum(weights, axis=1, keepdims=True)
-    mixture = sacc_ref[...] * fade + jnp.dot(
-        weights.astype(BF16), kv_ref[1], preferred_element_type=F32
-    )
-    mixture = mixture / total
+    bias = sbias_ref[:, -kv_ref.shape[1] :]
+    state = load_summary(sacc_ref, sml_ref)
+    state = add_summary(squery_ref[...], kv_ref[0], kv_ref[1], bias, state, head_count)
+    mixture = state[0] / state[2]
     slane = lax.broadcasted_iota(jnp.int32, (8, cols_all), 1)
     summary = jnp.zeros((8, cols_all), F32)
     for h in range(head_count):
@@ -617,7 +630,7 @@
         segment_ids(key_pos, bounds)[None, :] == segment_ids(mine_pos, bounds)[:, None]
     )
     sbias = jnp.pad(jnp.where(seen, 0.0, MASKED), ((0, 8 - per_device), (0, 0)))
-    tables = (early_off, early_pos, middle_list, late_list, bounds, mine, base, sbias)
+    tables = (early_off, early_pos, middle_list, late_list, bounds, mine, base, sbias, side)
 
     swap = [(0, 1), (1, 0)]
 
@@ -655,24 +668,35 @@
     own_there = other_half(own_tokens)
     here2a = from_slot(low, 2)
     here1a = from_slot(low, 1)
-    here2a, here1a, high, tables = lax.optimization_barrier((here2a, here1a, high, tables))
-    early_off, early_pos, middle_list, late_list, bounds, mine, base, sbias = tables
+    high, tables = lax.optimization_barrier((high, tables))
+    early_off, early_pos, middle_list, late_list, bounds, mine, base, sbias, side = tables
     here2b = from_slot(high, 2)
     here1b = from_slot(high, 1)
+    w_q, w_kv, mark = whole_call(
+        weights_kernel,
+        [],
+        [],
+        [w_qkv],
+        [array(2 * half, cols, dtype=BF16), array(2, 2 * half, cols, dtype=BF16), array(8, LANES)],
+        [],
+        [pltpu.SemaphoreType.DMA((2,))],
+        1,
+        "near_weights",
+    )
+    here2a, mark = lax.optimization_barrier((here2a, mark))
     there1a, there2a = other_half(here1a), other_half(here2a)
-    queries, own_kv, w_kv = whole_call(
+    queries, own_kv = whole_call(
         first_kernel,
         [side],
-        [own_tokens, own_there],
-        [w_qkv],
-        [array(tok_rows, cols, dtype=BF16), array(2, tok_rows, cols, dtype=BF16)]
-        + [array(2, 2 * half, cols, dtype=BF16)],
-        [],
-        [pltpu.VMEM((2 * half, cols), BF16), pltpu.SemaphoreType.DMA((3,))],
+        [own_tokens, own_there, w_q, w_kv, mark],
+        [],
+        [array(tok_rows, cols, dtype=BF16), array(2, tok_rows, cols, dtype=BF16)],
+        [],
+        [],
         2,
         "own_projections",
     )
-    here2b, here1b, w_kv = lax.optimization_barrier((here2b, here1b, w_kv))
+    here2b, here1b, own_kv = lax.optimization_barrier((here2b, here1b, own_kv))
     here3b = from_slot(here2b, 1)
     there1b, there2b = other_half(here1b), other_half(here2b)
     piece_kv = array(2, piece, cols, dtype=BF16)
@@ -692,12 +716,17 @@
 
     sizes = dict(pair_count=pair_count, head_count=head_count)
     state = [array(tok_rows, cols)] * 3
-    *state, kv = whole_call(
+    srows = 8 * head_count
+    summary_state = [array(srows, cols), array(srows, LANES)]
+    *state, kv, sacc, sml, squery = whole_call(
         early_kernel,
-        [early_off, early_pos, bounds, base],
-        [queries, own_kv, kv1a, kv2a],
-        [],
-        state + [array(2, early_rows, cols, dtype=BF16)],
+        [early_off, early_pos, bounds, base, mine],
+        [queries, sbias, own_kv, kv1a, kv2a],
+        [],
+        state
+        + [array(2, early_rows, cols, dtype=BF16)]
+        + summary_state
+        + [array(srows, cols, dtype=BF16)],
         [],
         [
             pltpu.VMEM((BLOCK, items * BLOCK), F32),
@@ -709,21 +738,19 @@
         items=items,
         **sizes,
     )
-    srows = 8 * head_count
-    *state, sacc, sml, squery, w_out_near = whole_call(
+    *state, sacc, sml, w_out_near = whole_call(
         middle_kernel,
-        [*middle_list, bounds, base, mine, side],
-        [queries, w_kv, kv, sbias, *state, here1b, there1b, here2b, there2b],
+        [*middle_list, bounds, base, side],
+        [queries, w_kv, sbias, *state, sacc, sml, squery, here1b, there1b, here2b, there2b],
         [w_out],
-        [array(tok_rows, cols)] * 3
-        + [array(srows, cols), array(srows, LANES), array(srows, cols, dtype=BF16)]
-        + [array(*w_out.shape, dtype=BF16)],
+        [array(tok_rows, cols)] * 3 + summary_state + [array(*w_out.shape, dtype=BF16)],
         [],
         [pltpu.VMEM((2, 2 * piece, cols), BF16), pltpu.SemaphoreType.DMA],
         5,
         "middle_attention",
         items=middle_items,
         group=4,
+        first_key=early_rows,
         **sizes,
     )
     own_term, other_term = whole_call(

time: 74.1 us -> 72.1 us (0.973)
  starting transfers between devices: 20.1 us -> 18.1 us
  local copies, waits for them, and re-layouts: 6.81 us -> 5.76 us
    ppermute x6, waiting for transfers between devices: 4.3 us -> 7.93 us  [from_slot(): return lax.ppermute(x, 'ctx', [(i, i ^ slot) for i in range(ctx_count)])]
    ppermute x8, waiting for transfers between devices: 16.7 us -> 13.7 us  [other_half(): return lax.ppermute(x, 'heads', swap)]
    ppermute x8, starting transfers between devices: 9.99 us -> 8.43 us  [other_half(): return lax.ppermute(x, 'heads', swap)]
    unnamed x15 -> x13, local copies, waits for them, and re-layouts: 3.04 us -> 1.99 us
    pallas_call x5 -> x6, Pallas kernels: 19.5 us -> 19.8 us  [whole_call(): pl.pallas_call(functools.partial(kernel, **sizes), in_specs=[pl.BlockSpec...]
  transfers between devices with their start and end apart: 14 -> 14, of which waited for: 8 -> 6; matrix products, arithmetic and copies ran while one was open for 10% -> 11% of each run, Pallas kernels for 20% -> 21%
where the time goes in v4:
time: 72.1 us; the launch traced here: 71.8 us
  waiting for transfers between devices  21.6 us (30%)
  Pallas kernels  19.8 us (27%)
  starting transfers between devices  18.1 us (25%)
  other arithmetic  6.34 us (9%)
  local copies, waits for them, and re-layouts  5.76 us (8%)
    pallas_call x6, Pallas kernels, whole_call(): pl.pallas_call(functools.partial(kernel, **sizes), in_specs=[pl.BlockSpec...  19.8 us
    ppermute x8, waiting for transfers between devices, other_half(): return lax.ppermute(x, 'heads', swap)  13.7 us
    ppermute x6, starting transfers between devices, from_slot(): return lax.ppermute(x, 'ctx', [(i, i ^ slot) for i in range(ctx_count)])  9.66 us
    ppermute x8, starting transfers between devices, other_half(): return lax.ppermute(x, 'heads', swap)  8.43 us
    ppermute x6, waiting for transfers between devices, from_slot(): return lax.ppermute(x, 'ctx', [(i, i ^ slot) for i in range(ctx_count)])  7.93 us
    unnamed x13, local copies, waits for them, and re-layouts  1.99 us
  transfers between devices with their start and end apart: 14, of which 6 were waited for; matrix products, arithmetic and copies ran while one was open for 11% of the time, Pallas kernels for 21%

profile of v4, /device:TPU:0, one launch (start us, length us, event | category | flops | bytes accessed | tf_op | source)
XLA Modules:
  0.0 71.8 jit_solution(11162513240380800043)
XLA Ops:
  0.0 1.1 %slice_bitcast_fusion = (bf16[256,512]{1,0:T(8,128)(2,1)S(1)}, bf16[256,512]{1,0:T(8,128)(2,1)S(1)}) fusion(bf16[1,512,512]{2,1,0:T(8,128)(2,1)} %param.11), kind=kLoop, calls=%fused_computation.5 | loop fusion | bytes 1048576 | tf_op jit(solution)/shard_map/slice | solution.py:667
  1.1 4.1 %collective-permute-start.1 = (bf16[256,512]{1,0:T(8,128)(2,1)S(1)}, bf16[256,512]{1,0:T(8,128)(2,1)S(1)}, u32[]{:S(2)}, u32[]{:S(2)}) collective-permute-start(bf16[256,512]{1,0:T(8,128)(2,1)S(1)} %get-tuple-element.109), channel_id=1, source_target_pairs={{0,8},{4,12},{8,0},{12,4},{1,9},{5,13},{9,1},{13,5},{2,10},{6,14},... | collective-permute-start | bytes 786440 | tf_op jit(solution)/shard_map/ppermute | solution.py:641
  5.2 1.6 %collective-permute-start.4 = (bf16[256,512]{1,0:T(8,128)(2,1)S(1)}, bf16[256,512]{1,0:T(8,128)(2,1)S(1)}, u32[]{:S(2)}, u32[]{:S(2)}) collective-permute-start(bf16[256,512]{1,0:T(8,128)(2,1)S(1)} %get-tuple-element.109), channel_id=1, source_target_pairs={{0,4},{4,0},{8,12},{12,8},{1,5},{5,1},{9,13},{13,9},{2,6},{6,2},{1... | collective-permute-start | bytes 786440 | tf_op jit(solution)/shard_map/ppermute | solution.py:641
  6.8 1.5 %collective-permute-start = (bf16[512,512]{1,0:T(8,128)(2,1)}, bf16[512,512]{1,0:T(8,128)(2,1)S(1)}, u32[]{:S(2)}, u32[]{:S(2)}) collective-permute-start(bf16[512,512]{1,0:T(8,128)(2,1)} %bitcast.34), channel_id=1, source_target_pairs={{0,2},{2,0},{1,3},{3,1},{4,6},{6,4},{5,7},{7,5},{8,10},{10,8},{9,1... | collective-permute-start | bytes 1572872 | tf_op jit(solution)/shard_map/ppermute | solution.py:638
  8.3 0.7 copy.38
  9.0 0.9 %select_reduce_fusion = s32[4,6]{0,1:T(8,128)S(1)} fusion(s32[8]{0:T(128)} %constant.133.clone, s32[4,6]{0,1:T(8,128)S(1)} %get-tuple-element.115), kind=kLoop, calls=%fused_computation.14 | loop fusion | flops 552 | bytes 224 | tf_op jit(solution)/shard_map/reduce_sum | solution.py:596
  11.8 0.8 %reduce-window.26 = s32[4,1]{0,1:T(1,128)S(1)} reduce-window(s32[4,1]{0,1:T(1,128)} %bitcast.51, s32[]{:T(128)} %constant.114.clone.1), window={size=4x1 pad=3_0x0_0}, to_apply=%region_11.12 | reduce-window | flops 12 | bytes 36 | tf_op jit(solution)/shard_map/reduce-window.11
  13.9 0.7 %broadcast_subtract_fusion = (s32[4]{0:T(128)S(1)}, s32[4]{0:T(128)S(1)}) fusion(s32[]{:T(128)} %mul.97, s32[1,16]{1,0:T(1,128)} %param.17, s32[]{:T(128)S(6)} %select_n.115), kind=kLoop, calls=%fused_computation.83 | loop fusion | flops 4 | bytes 56 | tf_op jit(solution)/shard_map/sub | solution.py:624
  16.8 1.9 %copy-done.2 = bf16[3,1024,512]{2,1,0:T(8,128)(2,1)S(1)} copy-done((bf16[3,1024,512]{2,1,0:T(8,128)(2,1)S(1)}, bf16[3,1024,512]{2,1,0:T(8,128)(2,1)}, u32[]{:S(2)}) %copy-start.2) | copy-done | bytes 3145752
  19.3 1.7 %collective-permute-start.6 = (bf16[256,512]{1,0:T(8,128)(2,1)S(1)}, bf16[256,512]{1,0:T(8,128)(2,1)S(1)}, u32[]{:S(2)}, u32[]{:S(2)}) collective-permute-start(bf16[256,512]{1,0:T(8,128)(2,1)S(1)} %collective-permute-done.1.refs_2_), channel_id=1, source_target_pairs={{0,2},{2,0},{1,3},{3,1},{4,6},{6,4},{5,7},{7,5},{8,10},{10,8},{9,1... | collective-permute-start | bytes 786440 | tf_op jit(solution)/shard_map/ppermute | solution.py:638
  21.0 1.8 %own_projections.1 = (bf16[512,512]{1,0:T(8,128)(2,1)S(1)}, bf16[2,512,512]{2,1,0:T(8,128)(2,1)S(1)}) custom-call(s32[1]{0:T(128)} %bitcast.10.side_ref, bf16[512,512]{1,0:T(8,128)(2,1)S(1)} %bitcast.35, bf16[512,512]{1,0:T(8,128)(2,1)S(1)} %collective-permute-done.there_ref, bf16[1024,512]{1,0:T(8,128)(2,1)S(1)} %get-tuple-element.55.w_q_ref, ...), custom_call_target="tpu_custom_call" | custom-call | flops 2000000000 | bytes 7000000 | tf_op jit(solution)/shard_map/own_projections/pallas_call | solution.py:652
  22.8 6.8 %collective-permute-done.2.here1_ref = bf16[256,512]{1,0:T(8,128)(2,1)S(1)} collective-permute-done((bf16[256,512]{1,0:T(8,128)(2,1)S(1)}, bf16[256,512]{1,0:T(8,128)(2,1)S(1)}, u32[]{:S(2)}, u32[]{:S(2)}) %collective-permute-start.2) | collective-permute-done | bytes 262176 | tf_op jit(solution)/shard_map/ppermute | solution.py:641
  30.2 1.4 %collective-permute-start.10 = (bf16[256,512]{1,0:T(8,128)(2,1)S(1)}, bf16[256,512]{1,0:T(8,128)(2,1)S(1)}, u32[]{:S(2)}, u32[]{:S(2)}) collective-permute-start(bf16[256,512]{1,0:T(8,128)(2,1)S(1)} %collective-permute-done.2.here1_ref), channel_id=1, source_target_pairs={{0,4},{4,0},{8,12},{12,8},{1,5},{5,1},{9,13},{13,9},{2,6},{6,2},{1... | collective-permute-start | bytes 786440 | tf_op jit(solution)/shard_map/ppermute | solution.py:641
  32.2 1.3 %piece_projections.1 = (bf16[2,256,512]{2,1,0:T(8,128)(2,1)S(1)}, bf16[2,256,512]{2,1,0:T(8,128)(2,1)S(1)}) custom-call(s32[1]{0:T(128)} %bitcast.10.side_ref, bf16[2,1024,512]{2,1,0:T(8,128)(2,1)S(1)} %get-tuple-element.56.w_kv_ref, bf16[256,512]{1,0:T(8,128)(2,1)S(1)} %collective-permute-done.4.refs_0_, ...), custom_call_target="tpu_custom_call" | custom-call | flops 1000000000 | bytes 3500000 | tf_op jit(solution)/shard_map/piece_projections/pallas_call | solution.py:652
  33.5 1.7 %collective-permute-start.9 = (bf16[2,256,512]{2,1,0:T(8,128)(2,1)S(1)}, bf16[2,256,512]{2,1,0:T(8,128)(2,1)S(1)}, u32[]{:S(2)}, u32[]{:S(2)}) collective-permute-start(bf16[2,256,512]{2,1,0:T(8,128)(2,1)S(1)} %get-tuple-element.72.refs_1_), channel_id=1, source_target_pairs={{0,4},{4,0},{8,12},{12,8},{1,5},{5,1},{9,13},{13,9},{2,6},{6,2},{1... | collective-permute-start | bytes 1572872 | tf_op jit(solution)/shard_map/ppermute | solution.py:641
  35.2 7.4 %early_attention.1 = (f32[512,512]{1,0:T(8,128)S(1)}, f32[512,512]{1,0:T(8,128)S(1)}, f32[512,512]{1,0:T(8,128)S(1)}, bf16[2,1024,512]{2,1,0:T(8,128)(2,1)}, f32...) custom-call(s32[24]{0:T(128)S(1)} %get-tuple-element.65.off_ref, ...), custom_call_target="tpu_custom_call" | custom-call | flops 7000000000 | bytes 24500000 | tf_op jit(solution)/shard_map/early_attention/pallas_call | solution.py:652
  43.5 4.5 %middle_attention.1 = (f32[512,512]{1,0:T(8,128)S(1)}, f32[512,512]{1,0:T(8,128)S(1)}, f32[512,512]{1,0:T(8,128)S(1)}, f32[64,512]{1,0:T(8,128)S(1)}, f32[64,128...) custom-call(s32[7]{0:T(128)S(1)} %convert_element_type.52.valid_ref, s32[7]{0:T(128)S(1)} %get-tuple-element.61.block_ref, ...), custom_call_target="tpu_custom_call" | custom-call | flops 5000000000 | bytes 17500000 | tf_op jit(solution)/shard_map/middle_attention/pallas_call | solution.py:652
  47.9 1.1 %collective-permute-done.9.fresh_ref = bf16[2,256,512]{2,1,0:T(8,128)(2,1)S(1)} collective-permute-done((bf16[2,256,512]{2,1,0:T(8,128)(2,1)S(1)}, bf16[2,256,512]{2,1,0:T(8,128)(2,1)S(1)}, u32[]{:S(2)}, u32[]{:S(2)}) %collective-permute-start.9) | collective-permute-done | bytes 524320 | tf_op jit(solution)/shard_map/ppermute | solution.py:641
  49.5 4.7 %late_attention.1 = (bf16[512,512]{1,0:T(8,128)(2,1)S(1)}, bf16[512,512]{1,0:T(8,128)(2,1)S(1)}) custom-call(s32[4]{0:T(128)S(1)} %convert_element_type.54.valid_ref, s32[4]{0:T(128)S(1)} %get-tuple-element.48.block_ref, s32[4]{0:T(128)S(1)} %get-tuple-element.49.off_ref, s32[4]{0:T(128)S(1)} %get-tuple-element.50.pos_ref, s32[4]{0:T(128)S(1)} %bitcast.40, ...), custom_call_target="tpu_custom_call" | custom-call | flops 4000000000 | bytes 14000000 | tf_op jit(solution)/shard_map/late_attention/pallas_call | solution.py:652
  54.3 1.4 %collective-permute-start.12 = (bf16[512,512]{1,0:T(8,128)(2,1)S(1)}, bf16[512,512]{1,0:T(8,128)(2,1)S(1)}, u32[]{:S(2)}, u32[]{:S(2)}) collective-permute-start(bf16[512,512]{1,0:T(8,128)(2,1)S(1)} %get-tuple-element.88), channel_id=1, source_target_pairs={{0,2},{2,0},{1,3},{3,1},{4,6},{6,4},{5,7},{7,5},{8,10},{10,8},{9,1... | collective-permute-start | bytes 1572872 | tf_op jit(solution)/shard_map/ppermute | solution.py:638
  55.7 10.9 %collective-permute-done.12 = bf16[512,512]{1,0:T(8,128)(2,1)S(1)} collective-permute-done((bf16[512,512]{1,0:T(8,128)(2,1)S(1)}, bf16[512,512]{1,0:T(8,128)(2,1)S(1)}, u32[]{:S(2)}, u32[]{:S(2)}) %collective-permute-start.12) | collective-permute-done | bytes 524320 | tf_op jit(solution)/shard_map/ppermute | solution.py:638
  67.0 1.8 %collective-permute-start.13 = (f32[2,512]{1,0:T(2,128)S(1)}, f32[2,512]{1,0:T(2,128)S(1)}, u32[]{:S(2)}, u32[]{:S(2)}) collective-permute-start(f32[2,512]{1,0:T(2,128)S(1)} %pad_maximum_fusion), channel_id=1, source_target_pairs={{0,2},{2,0},{1,3},{3,1},{4,6},{6,4},{5,7},{7,5},{8,10},{10,8},{9,1... | collective-permute-start | bytes 12296 | tf_op jit(solution)/shard_map/ppermute | solution.py:638
  68.8 1.9 %collective-permute-done.13 = f32[2,512]{1,0:T(2,128)S(1)} collective-permute-done((f32[2,512]{1,0:T(2,128)S(1)}, f32[2,512]{1,0:T(2,128)S(1)}, u32[]{:S(2)}, u32[]{:S(2)}) %collective-permute-start.13) | collective-permute-done | bytes 4128 | tf_op jit(solution)/shard_map/ppermute | solution.py:638
  70.7 1.1 %fusion = bf16[1,512,512]{2,1,0:T(8,128)(2,1)} fusion(f32[512]{0:T(512)S(1)} %copy-done.4, f32[512]{0:T(512)S(1)} %copy-done.5, f32[512]{0:T(512)S(1)} %add_rsqrt_fusion, f32[512]{0:T(512)S(1)} %bitcast.48, bf16[512,512]{1,0:T(8,128)(2,1)S(1)} %collective-permute-done.12, bf16[512,512]{1,0:T(8,128)(2,1)S(1)} %get-tuple-element.87, ...), kind=kLoop, calls=%fused_computation.3 | loop fusion | flops 2621440 | bytes 2105344 | tf_op jit(solution)/shard_map/broadcast_in_dim | solution.py:778
  (86 shorter events, 8.8 us)
Async XLA Ops:
  0.0 13.5 %copy-start = (s32[1,16,8]{1,2,0:T(8,128)S(1)}, s32[1,16,8]{1,2,0:T(8,128)}, u32[]{:S(2)}) copy-start(s32[1,16,8]{1,2,0:T(8,128)} %param.18) | copy-start | bytes 1540
  1.1 17.8 %collective-permute-start.1 = (bf16[256,512]{1,0:T(8,128)(2,1)S(1)}, bf16[256,512]{1,0:T(8,128)(2,1)S(1)}, u32[]{:S(2)}, u32[]{:S(2)}) collective-permute-start(bf16[256,512]{1,0:T(8,128)(2,1)S(1)} %get-tuple-element.109), channel_id=1, source_target_pairs={{0,8},{4,12},{8,0},{12,4},{1,9},{5,13},{9,1},{13,5},{2,10},{6,14},... | collective-permute-start | bytes 786440 | tf_op jit(solution)/shard_map/ppermute | solution.py:641
  5.2 13.7 %collective-permute-start.4 = (bf16[256,512]{1,0:T(8,128)(2,1)S(1)}, bf16[256,512]{1,0:T(8,128)(2,1)S(1)}, u32[]{:S(2)}, u32[]{:S(2)}) collective-permute-start(bf16[256,512]{1,0:T(8,128)(2,1)S(1)} %get-tuple-element.109), channel_id=1, source_target_pairs={{0,4},{4,0},{8,12},{12,8},{1,5},{5,1},{9,13},{13,9},{2,6},{6,2},{1... | collective-permute-start | bytes 786440 | tf_op jit(solution)/shard_map/ppermute | solution.py:641
  6.8 14.3 %collective-permute-start = (bf16[512,512]{1,0:T(8,128)(2,1)}, bf16[512,512]{1,0:T(8,128)(2,1)S(1)}, u32[]{:S(2)}, u32[]{:S(2)}) collective-permute-start(bf16[512,512]{1,0:T(8,128)(2,1)} %bitcast.34), channel_id=1, source_target_pairs={{0,2},{2,0},{1,3},{3,1},{4,6},{6,4},{5,7},{7,5},{8,10},{10,8},{9,1... | collective-permute-start | bytes 1572872 | tf_op jit(solution)/shard_map/ppermute | solution.py:638
  10.0 11.0 %copy-start.1 = (bf16[1,512,512]{2,1,0:T(8,128)(2,1)S(1)}, bf16[1,512,512]{2,1,0:T(8,128)(2,1)}, u32[]{:S(2)}) copy-start(bf16[1,512,512]{2,1,0:T(8,128)(2,1)} %param.11) | copy-start | bytes 1572868
  15.9 13.7 %collective-permute-start.2 = (bf16[256,512]{1,0:T(8,128)(2,1)S(1)}, bf16[256,512]{1,0:T(8,128)(2,1)S(1)}, u32[]{:S(2)}, u32[]{:S(2)}) collective-permute-start(bf16[256,512]{1,0:T(8,128)(2,1)S(1)} %get-tuple-element.67), channel_id=1, source_target_pairs={{0,8},{4,12},{8,0},{12,4},{1,9},{5,13},{9,1},{13,5},{2,10},{6,14},... | collective-permute-start | bytes 786440 | tf_op jit(solution)/shard_map/ppermute | solution.py:641
  16.3 13.3 %collective-permute-start.3 = (bf16[256,512]{1,0:T(8,128)(2,1)S(1)}, bf16[256,512]{1,0:T(8,128)(2,1)S(1)}, u32[]{:S(2)}, u32[]{:S(2)}) collective-permute-start(bf16[256,512]{1,0:T(8,128)(2,1)S(1)} %get-tuple-element.67), channel_id=1, source_target_pairs={{0,4},{4,0},{8,12},{12,8},{1,5},{5,1},{9,13},{13,9},{2,6},{6,2},{1... | collective-permute-start | bytes 786440 | tf_op jit(solution)/shard_map/ppermute | solution.py:641
  16.8 1.9 %copy-start.2 = (bf16[3,1024,512]{2,1,0:T(8,128)(2,1)S(1)}, bf16[3,1024,512]{2,1,0:T(8,128)(2,1)}, u32[]{:S(2)}) copy-start(bf16[3,1024,512]{2,1,0:T(8,128)(2,1)} %w_hbm.1) | copy-start | bytes 9437188
  18.9 13.3 %collective-permute-start.5 = (bf16[256,512]{1,0:T(8,128)(2,1)S(1)}, bf16[256,512]{1,0:T(8,128)(2,1)S(1)}, u32[]{:S(2)}, u32[]{:S(2)}) collective-permute-start(bf16[256,512]{1,0:T(8,128)(2,1)S(1)} %collective-permute-done.4.refs_0_), channel_id=1, source_target_pairs={{0,2},{2,0},{1,3},{3,1},{4,6},{6,4},{5,7},{7,5},{8,10},{10,8},{9,1... | collective-permute-start | bytes 786440 | tf_op jit(solution)/shard_map/ppermute | solution.py:638
  19.3 12.9 %collective-permute-start.6 = (bf16[256,512]{1,0:T(8,128)(2,1)S(1)}, bf16[256,512]{1,0:T(8,128)(2,1)S(1)}, u32[]{:S(2)}, u32[]{:S(2)}) collective-permute-start(bf16[256,512]{1,0:T(8,128)(2,1)S(1)} %collective-permute-done.1.refs_2_), channel_id=1, source_target_pairs={{0,2},{2,0},{1,3},{3,1},{4,6},{6,4},{5,7},{7,5},{8,10},{10,8},{9,1... | collective-permute-start | bytes 786440 | tf_op jit(solution)/shard_map/ppermute | solution.py:638
  29.6 13.8 %collective-permute-start.8 = (bf16[256,512]{1,0:T(8,128)(2,1)S(1)}, bf16[256,512]{1,0:T(8,128)(2,1)S(1)}, u32[]{:S(2)}, u32[]{:S(2)}) collective-permute-start(bf16[256,512]{1,0:T(8,128)(2,1)S(1)} %collective-permute-done.2.here1_ref), channel_id=1, source_target_pairs={{0,2},{2,0},{1,3},{3,1},{4,6},{6,4},{5,7},{7,5},{8,10},{10,8},{9,1... | collective-permute-start | bytes 786440 | tf_op jit(solution)/shard_map/ppermute | solution.py:638
  30.2 12.3 %collective-permute-start.10 = (bf16[256,512]{1,0:T(8,128)(2,1)S(1)}, bf16[256,512]{1,0:T(8,128)(2,1)S(1)}, u32[]{:S(2)}, u32[]{:S(2)}) collective-permute-start(bf16[256,512]{1,0:T(8,128)(2,1)S(1)} %collective-permute-done.2.here1_ref), channel_id=1, source_target_pairs={{0,4},{4,0},{8,12},{12,8},{1,5},{5,1},{9,13},{13,9},{2,6},{6,2},{1... | collective-permute-start | bytes 786440 | tf_op jit(solution)/shard_map/ppermute | solution.py:641
  31.7 11.8 %collective-permute-start.7 = (bf16[256,512]{1,0:T(8,128)(2,1)S(1)}, bf16[256,512]{1,0:T(8,128)(2,1)S(1)}, u32[]{:S(2)}, u32[]{:S(2)}) collective-permute-start(bf16[256,512]{1,0:T(8,128)(2,1)S(1)} %collective-permute-done.3.here0_ref), channel_id=1, source_target_pairs={{0,2},{2,0},{1,3},{3,1},{4,6},{6,4},{5,7},{7,5},{8,10},{10,8},{9,1... | collective-permute-start | bytes 786440 | tf_op jit(solution)/shard_map/ppermute | solution.py:638
  33.5 15.6 %collective-permute-start.9 = (bf16[2,256,512]{2,1,0:T(8,128)(2,1)S(1)}, bf16[2,256,512]{2,1,0:T(8,128)(2,1)S(1)}, u32[]{:S(2)}, u32[]{:S(2)}) collective-permute-start(bf16[2,256,512]{2,1,0:T(8,128)(2,1)S(1)} %get-tuple-element.72.refs_1_), channel_id=1, source_target_pairs={{0,4},{4,0},{8,12},{12,8},{1,5},{5,1},{9,13},{13,9},{2,6},{6,2},{1... | collective-permute-start | bytes 1572872 | tf_op jit(solution)/shard_map/ppermute | solution.py:641
  35.2 8.3 %copy-start.3 = (bf16[512,1024]{1,0:T(8,128)(2,1)S(1)}, bf16[512,1024]{1,0:T(8,128)(2,1)}, u32[]{:S(2)}) copy-start(bf16[512,1024]{1,0:T(8,128)(2,1)} %w_out_hbm.1) | copy-start | bytes 3145732
  42.5 7.0 %collective-permute-start.11 = (bf16[256,512]{1,0:T(8,128)(2,1)S(1)}, bf16[256,512]{1,0:T(8,128)(2,1)S(1)}, u32[]{:S(2)}, u32[]{:S(2)}) collective-permute-start(bf16[256,512]{1,0:T(8,128)(2,1)S(1)} %collective-permute-done.10.here_ref), channel_id=1, source_target_pairs={{0,2},{2,0},{1,3},{3,1},{4,6},{6,4},{5,7},{7,5},{8,10},{10,8},{9,1... | collective-permute-start | bytes 786440 | tf_op jit(solution)/shard_map/ppermute | solution.py:638
  49.5 21.1 %copy-start.4 = (f32[512]{0:T(512)S(1)}, f32[512]{0:T(512)}, u32[]{:S(2)}) copy-start(f32[512]{0:T(512)} %param.15) | copy-start | bytes 6148
  49.5 21.1 %copy-start.5 = (f32[512]{0:T(512)S(1)}, f32[512]{0:T(512)}, u32[]{:S(2)}) copy-start(f32[512]{0:T(512)} %param.14) | copy-start | bytes 6148
  54.3 12.3 %collective-permute-start.12 = (bf16[512,512]{1,0:T(8,128)(2,1)S(1)}, bf16[512,512]{1,0:T(8,128)(2,1)S(1)}, u32[]{:S(2)}, u32[]{:S(2)}) collective-permute-start(bf16[512,512]{1,0:T(8,128)(2,1)S(1)} %get-tuple-element.88), channel_id=1, source_target_pairs={{0,2},{2,0},{1,3},{3,1},{4,6},{6,4},{5,7},{7,5},{8,10},{10,8},{9,1... | collective-permute-start | bytes 1572872 | tf_op jit(solution)/shard_map/ppermute | solution.py:638
  67.0 3.7 %collective-permute-start.13 = (f32[2,512]{1,0:T(2,128)S(1)}, f32[2,512]{1,0:T(2,128)S(1)}, u32[]{:S(2)}, u32[]{:S(2)}) collective-permute-start(f32[2,512]{1,0:T(2,128)S(1)} %pad_maximum_fusion), channel_id=1, source_target_pairs={{0,2},{2,0},{1,3},{3,1},{4,6},{6,4},{5,7},{7,5},{8,10},{10,8},{9,1... | collective-permute-start | bytes 12296 | tf_op jit(solution)/shard_map/ppermute | solution.py:638

commit v5 on v4

--- a/solution.py
+++ b/solution.py
@@ -494,9 +494,6 @@
 ):
     copy = pltpu.make_async_copy(w_out_hbm, w_out_ref, sem)
     copy.start()
-    acc_ref[...] = acc_in[...]
-    top_ref[...] = top_in[...]
-    sum_ref[...] = sum_in[...]
     pieces = [(here0_ref, there0_ref), (here1_ref, there1_ref)]
     project_pieces(side_ref, pieces, w_kv_ref, kv_ref, 0)
     add_items(
@@ -514,14 +511,11 @@
     valid_ref, block_ref, off_ref, pos_ref, bounds_ref, base_ref, mine_ref, side_ref,
     q_ref, w_kv_ref, w_ref, sbias_ref, acc_ref, top_ref, sum_ref,
     sacc_ref, sml_ref, squery_ref, fresh_ref, here_ref, there_ref,
-    own_ref, other_ref, kv_ref, mix_ref, peak_ref, total_ref,
+    own_ref, other_ref, mix_ref, peak_ref, total_ref, kv_ref,
     *, items, group, pair_count, head_count,
 ):
     tok_rows, cols_all = mix_ref.shape
     fresh_rows = fresh_ref.shape[1]
-    mix_ref[...] = acc_ref[...]
-    peak_ref[...] = top_ref[...]
-    total_ref[...] = sum_ref[...]
     kv_ref[:, :fresh_rows] = fresh_ref[...]
     project_pieces(side_ref, [(here_ref, there_ref)], w_kv_ref, kv_ref, fresh_rows)
     add_items(
@@ -558,6 +552,11 @@
     own_ref[...] = jnp.dot(
         attention, w_ref[:, pl.ds(low, half)], preferred_element_type=F32
     ).astype(BF16)
+
+
+def running_sum(values):
+    order = jnp.arange(values.shape[0], dtype=jnp.int32)
+    return jnp.sum(jnp.where(order[None, :] <= order[:, None], values[None, :], 0), axis=1)
 
 
 def gathered(
@@ -581,7 +580,7 @@
     early_count, late_count, piece_count = 4, 6, 2 * ctx_count
     early_rows, late_rows = early_count * piece, (piece_count - late_count) * piece
 
-    bounds = jnp.cumsum(pair_lengths[0]).astype(jnp.int32)
+    bounds = running_sum(pair_lengths[0])
     base = (ctx_index * tok_rows).astype(jnp.int32).reshape(1)
     picks = random_blocks[0]
     rand_count = picks.shape[1]
@@ -604,7 +603,7 @@
 
     def item_list(first, last, count):
         held = (inside & (place >= first) & (place < last)).reshape(-1)
-        rank = jnp.cumsum(held.astype(jnp.int32)) - 1
+        rank = running_sum(held.astype(jnp.int32)) - 1
         chosen = held[None, :] & (rank[None, :] == jnp.arange(count, dtype=jnp.int32)[:, None])
 
         def compact(x):
@@ -646,7 +645,7 @@
     def like(arrays):
         return [pltpu.VMEM(x.shape, x.dtype) for x in arrays]
 
-    def whole_call(kernel, scalars, args, far_args, outs, far_outs, scratch, work, name, **sizes):
+    def whole_call(kernel, scalars, args, far_args, outs, far_outs, scratch, work, name, aliases=None, **sizes):
         far = pl.BlockSpec(memory_space=pltpu.HBM)
         near = pl.BlockSpec(memory_space=pltpu.VMEM)
         return pl.pallas_call(
@@ -657,6 +656,7 @@
             out_specs=[far] * len(far_outs) + [near] * len(outs),
             out_shape=far_outs + outs,
             scratch_shapes=scratch,
+            input_output_aliases=aliases or {},
             compiler_params=params(),
             cost_estimate=pl.CostEstimate(
                 flops=int(work * 1e9), bytes_accessed=int(work * 3.5e6), transcendentals=0
@@ -700,18 +700,23 @@
     here3b = from_slot(here2b, 1)
     there1b, there2b = other_half(here1b), other_half(here2b)
     piece_kv = array(2, piece, cols, dtype=BF16)
-    kv1a, kv2a = whole_call(
-        pieces_kernel,
-        [side],
-        [w_kv, here1a, there1a, here2a, there2a],
-        [],
-        [piece_kv, piece_kv],
-        [],
-        [],
-        1,
-        "piece_projections",
-    )
+
+    def piece_projections(here, there):
+        return whole_call(
+            pieces_kernel,
+            [side],
+            [w_kv, here, there],
+            [],
+            [piece_kv],
+            [],
+            [],
+            1,
+            "piece_projections",
+        )[0]
+
+    kv2a = piece_projections(here2a, there2a)
     kv3a = from_slot(kv2a, 1)
+    kv1a = piece_projections(here1a, there1a)
     there3b = other_half(here3b)
 
     sizes = dict(pair_count=pair_count, head_count=head_count)
@@ -748,21 +753,23 @@
         [pltpu.VMEM((2, 2 * piece, cols), BF16), pltpu.SemaphoreType.DMA],
         5,
         "middle_attention",
+        aliases={len(middle_list) + 3 + 3 + i: i for i in range(3)},
         items=middle_items,
         group=4,
         first_key=early_rows,
         **sizes,
     )
-    own_term, other_term = whole_call(
+    own_term, other_term, *state = whole_call(
         late_kernel,
         [*late_list, bounds, base, mine, side],
         [queries, w_kv, w_out_near, sbias, *state, sacc, sml, squery, kv3a, here3b, there3b],
         [],
-        [array(tok_rows, half, dtype=BF16)] * 2,
-        [],
-        [pltpu.VMEM((2, late_rows, cols), BF16)] + [pltpu.VMEM((tok_rows, cols), F32)] * 3,
+        [array(tok_rows, half, dtype=BF16)] * 2 + [array(tok_rows, cols)] * 3,
+        [],
+        [pltpu.VMEM((2, late_rows, cols), BF16)],
         4,
         "late_attention",
+        aliases={len(late_list) + 4 + 4 + i: 2 + i for i in range(3)},
         items=late_items,
         group=4,
         **sizes,

time: 72.1 us -> 70.5 us (0.978)
  waiting for transfers between devices: 21.6 us -> 20.4 us
    ppermute x8, starting transfers between devices: 8.43 us -> 9.4 us  [other_half(): return lax.ppermute(x, 'heads', swap)]
    another operation x3 -> x0, other arithmetic: 0.94 us -> none
    reduce_sum x0 -> x2, other arithmetic: none -> 0.89 us  [running_sum(): jnp.sum(jnp.where(order[None, :] <= order[:, None], values[None, :], 0),...]
    ppermute x8, waiting for transfers between devices: 13.7 us -> 12.9 us  [other_half(): return lax.ppermute(x, 'heads', swap)]
    pallas_call x6 -> x7, Pallas kernels: 19.8 us -> 19.7 us  [whole_call(): pl.pallas_call(functools.partial(kernel, **sizes), in_specs=[pl.BlockSpec...]
  transfers between devices with their start and end apart: 14 -> 14, of which waited for: 6 -> 6; matrix products, arithmetic and copies ran while one was open for 11% -> 10% of each run, Pallas kernels for 21% -> 22%
where the time goes in v5:
time: 70.5 us; the launch traced here: 70.2 us
  waiting for transfers between devices  20.4 us (29%)
  Pallas kernels  19.7 us (28%)
  starting transfers between devices  18.4 us (26%)
  other arithmetic  6.06 us (9%)
  local copies, waits for them, and re-layouts  5.42 us (8%)
    pallas_call x7, Pallas kernels, whole_call(): pl.pallas_call(functools.partial(kernel, **sizes), in_specs=[pl.BlockSpec...  19.7 us
    ppermute x8, waiting for transfers between devices, other_half(): return lax.ppermute(x, 'heads', swap)  12.9 us
    ppermute x8, starting transfers between devices, other_half(): return lax.ppermute(x, 'heads', swap)  9.4 us
    ppermute x6, starting transfers between devices, from_slot(): return lax.ppermute(x, 'ctx', [(i, i ^ slot) for i in range(ctx_count)])  8.99 us
    ppermute x6, waiting for transfers between devices, from_slot(): return lax.ppermute(x, 'ctx', [(i, i ^ slot) for i in range(ctx_count)])  7.47 us
    unnamed x13, local copies, waits for them, and re-layouts  1.99 us
  transfers between devices with their start and end apart: 14, of which 6 were waited for; matrix products, arithmetic and copies ran while one was open for 10% of the time, Pallas kernels for 22%

profile of v5, /device:TPU:0, one launch (start us, length us, event | category | flops | bytes accessed | tf_op | source)
XLA Modules:
  0.0 70.2 jit_solution(7750722980833981325)
XLA Ops:
  0.0 1.1 %slice_bitcast_fusion = (bf16[256,512]{1,0:T(8,128)(2,1)S(1)}, bf16[256,512]{1,0:T(8,128)(2,1)S(1)}) fusion(bf16[1,512,512]{2,1,0:T(8,128)(2,1)} %param.11), kind=kLoop, calls=%fused_computation.5 | loop fusion | bytes 1048576 | tf_op jit(solution)/shard_map/slice | solution.py:667
  1.1 4.1 %collective-permute-start.1 = (bf16[256,512]{1,0:T(8,128)(2,1)S(1)}, bf16[256,512]{1,0:T(8,128)(2,1)S(1)}, u32[]{:S(2)}, u32[]{:S(2)}) collective-permute-start(bf16[256,512]{1,0:T(8,128)(2,1)S(1)} %get-tuple-element.102), channel_id=1, source_target_pairs={{0,8},{4,12},{8,0},{12,4},{1,9},{5,13},{9,1},{13,5},{2,10},{6,14},... | collective-permute-start | bytes 786440 | tf_op jit(solution)/shard_map/ppermute | solution.py:640
  5.2 1.6 %collective-permute-start.4 = (bf16[256,512]{1,0:T(8,128)(2,1)S(1)}, bf16[256,512]{1,0:T(8,128)(2,1)S(1)}, u32[]{:S(2)}, u32[]{:S(2)}) collective-permute-start(bf16[256,512]{1,0:T(8,128)(2,1)S(1)} %get-tuple-element.102), channel_id=1, source_target_pairs={{0,4},{4,0},{8,12},{12,8},{1,5},{5,1},{9,13},{13,9},{2,6},{6,2},{1... | collective-permute-start | bytes 786440 | tf_op jit(solution)/shard_map/ppermute | solution.py:640
  6.8 1.5 %collective-permute-start = (bf16[512,512]{1,0:T(8,128)(2,1)}, bf16[512,512]{1,0:T(8,128)(2,1)S(1)}, u32[]{:S(2)}, u32[]{:S(2)}) collective-permute-start(bf16[512,512]{1,0:T(8,128)(2,1)} %bitcast.33), channel_id=1, source_target_pairs={{0,2},{2,0},{1,3},{3,1},{4,6},{6,4},{5,7},{7,5},{8,10},{10,8},{9,1... | collective-permute-start | bytes 1572872 | tf_op jit(solution)/shard_map/ppermute | solution.py:637
  9.1 0.9 %select_reduce_fusion.2 = s32[4,6]{0,1:T(8,128)S(1)} fusion(s32[8]{0:T(128)} %constant.126.clone, s32[4,6]{0,1:T(8,128)S(1)} %get-tuple-element.112), kind=kLoop, calls=%fused_computation.15 | loop fusion | flops 552 | bytes 224 | tf_op jit(solution)/shard_map/reduce_sum | solution.py:595
  11.6 0.8 %select_reduce_fusion.6.bounds_ref = s32[4]{0:T(128)S(1)} fusion(s32[4]{0:T(128)} %bitcast.44), kind=kLoop, calls=%fused_computation.54 | loop fusion | flops 44 | bytes 32 | tf_op jit(solution)/shard_map/reduce_sum | solution.py:559
  16.2 1.9 %copy-done.2 = bf16[3,1024,512]{2,1,0:T(8,128)(2,1)S(1)} copy-done((bf16[3,1024,512]{2,1,0:T(8,128)(2,1)S(1)}, bf16[3,1024,512]{2,1,0:T(8,128)(2,1)}, u32[]{:S(2)}) %copy-start.2) | copy-done | bytes 3145752
  18.3 1.0 %collective-permute-start.6 = (bf16[256,512]{1,0:T(8,128)(2,1)S(1)}, bf16[256,512]{1,0:T(8,128)(2,1)S(1)}, u32[]{:S(2)}, u32[]{:S(2)}) collective-permute-start(bf16[256,512]{1,0:T(8,128)(2,1)S(1)} %collective-permute-done.1.refs_0_), channel_id=1, source_target_pairs={{0,2},{2,0},{1,3},{3,1},{4,6},{6,4},{5,7},{7,5},{8,10},{10,8},{9,1... | collective-permute-start | bytes 786440 | tf_op jit(solution)/shard_map/ppermute | solution.py:637
  19.3 1.1 %collective-permute-start.5 = (bf16[256,512]{1,0:T(8,128)(2,1)S(1)}, bf16[256,512]{1,0:T(8,128)(2,1)S(1)}, u32[]{:S(2)}, u32[]{:S(2)}) collective-permute-start(bf16[256,512]{1,0:T(8,128)(2,1)S(1)} %collective-permute-done.4.refs_0_), channel_id=1, source_target_pairs={{0,2},{2,0},{1,3},{3,1},{4,6},{6,4},{5,7},{7,5},{8,10},{10,8},{9,1... | collective-permute-start | bytes 786440 | tf_op jit(solution)/shard_map/ppermute | solution.py:637
  20.7 1.8 %own_projections.1 = (bf16[512,512]{1,0:T(8,128)(2,1)S(1)}, bf16[2,512,512]{2,1,0:T(8,128)(2,1)S(1)}) custom-call(s32[1]{0:T(128)} %bitcast.9.side_ref, bf16[512,512]{1,0:T(8,128)(2,1)S(1)} %bitcast.34, bf16[512,512]{1,0:T(8,128)(2,1)S(1)} %collective-permute-done.there_ref, bf16[1024,512]{1,0:T(8,128)(2,1)S(1)} %get-tuple-element.53.w_q_ref, ...), custom_call_target="tpu_custom_call" | custom-call | flops 2000000000 | bytes 7000000 | tf_op jit(solution)/shard_map/own_projections/pallas_call | solution.py:651
  22.5 6.6 %collective-permute-done.2.here1_ref = bf16[256,512]{1,0:T(8,128)(2,1)S(1)} collective-permute-done((bf16[256,512]{1,0:T(8,128)(2,1)S(1)}, bf16[256,512]{1,0:T(8,128)(2,1)S(1)}, u32[]{:S(2)}, u32[]{:S(2)}) %collective-permute-start.2) | collective-permute-done | bytes 262176 | tf_op jit(solution)/shard_map/ppermute | solution.py:640
  29.1 1.1 %collective-permute-start.8 = (bf16[256,512]{1,0:T(8,128)(2,1)S(1)}, bf16[256,512]{1,0:T(8,128)(2,1)S(1)}, u32[]{:S(2)}, u32[]{:S(2)}) collective-permute-start(bf16[256,512]{1,0:T(8,128)(2,1)S(1)} %collective-permute-done.2.here1_ref), channel_id=1, source_target_pairs={{0,2},{2,0},{1,3},{3,1},{4,6},{6,4},{5,7},{7,5},{8,10},{10,8},{9,1... | collective-permute-start | bytes 786440 | tf_op jit(solution)/shard_map/ppermute | solution.py:637
  30.2 1.5 %collective-permute-start.10 = (bf16[256,512]{1,0:T(8,128)(2,1)S(1)}, bf16[256,512]{1,0:T(8,128)(2,1)S(1)}, u32[]{:S(2)}, u32[]{:S(2)}) collective-permute-start(bf16[256,512]{1,0:T(8,128)(2,1)S(1)} %collective-permute-done.2.here1_ref), channel_id=1, source_target_pairs={{0,4},{4,0},{8,12},{12,8},{1,5},{5,1},{9,13},{13,9},{2,6},{6,2},{1... | collective-permute-start | bytes 786440 | tf_op jit(solution)/shard_map/ppermute | solution.py:640
  32.9 1.0 %collective-permute-start.9 = (bf16[2,256,512]{2,1,0:T(8,128)(2,1)S(1)}, bf16[2,256,512]{2,1,0:T(8,128)(2,1)S(1)}, u32[]{:S(2)}, u32[]{:S(2)}) collective-permute-start(bf16[2,256,512]{2,1,0:T(8,128)(2,1)S(1)} %piece_projections.3.refs_1_), channel_id=1, source_target_pairs={{0,4},{4,0},{8,12},{12,8},{1,5},{5,1},{9,13},{13,9},{2,6},{6,2},{1... | collective-permute-start | bytes 1572872 | tf_op jit(solution)/shard_map/ppermute | solution.py:640
  34.6 7.4 %early_attention.1 = (f32[512,512]{1,0:T(8,128)S(1)}, f32[512,512]{1,0:T(8,128)S(1)}, f32[512,512]{1,0:T(8,128)S(1)}, bf16[2,1024,512]{2,1,0:T(8,128)(2,1)}, f32...) custom-call(s32[24]{0:T(128)S(1)} %get-tuple-element.63.off_ref, ...), custom_call_target="tpu_custom_call" | custom-call | flops 7000000000 | bytes 24500000 | tf_op jit(solution)/shard_map/early_attention/pallas_call | solution.py:651
  42.0 1.2 %collective-permute-start.11 = (bf16[256,512]{1,0:T(8,128)(2,1)S(1)}, bf16[256,512]{1,0:T(8,128)(2,1)S(1)}, u32[]{:S(2)}, u32[]{:S(2)}) collective-permute-start(bf16[256,512]{1,0:T(8,128)(2,1)S(1)} %collective-permute-done.10.here_ref), channel_id=1, source_target_pairs={{0,2},{2,0},{1,3},{3,1},{4,6},{6,4},{5,7},{7,5},{8,10},{10,8},{9,1... | collective-permute-start | bytes 786440 | tf_op jit(solution)/shard_map/ppermute | solution.py:637
  43.2 4.3 %middle_attention.1 = (f32[512,512]{1,0:T(8,128)S(1)}, f32[512,512]{1,0:T(8,128)S(1)}, f32[512,512]{1,0:T(8,128)S(1)}, f32[64,512]{1,0:T(8,128)S(1)}, f32[64,128...) custom-call(s32[7]{0:T(128)S(1)} %convert_element_type.42.valid_ref, ...), custom_call_target="tpu_custom_call", output_to_operand_aliasing={{0}: (10, {}), {1}: (11, {}), {2}: (12, {})} | custom-call | flops 5000000000 | bytes 17500000 | tf_op jit(solution)/shard_map/middle_attention/pallas_call | solution.py:651
  47.5 0.9 %collective-permute-done.9.fresh_ref = bf16[2,256,512]{2,1,0:T(8,128)(2,1)S(1)} collective-permute-done((bf16[2,256,512]{2,1,0:T(8,128)(2,1)S(1)}, bf16[2,256,512]{2,1,0:T(8,128)(2,1)S(1)}, u32[]{:S(2)}, u32[]{:S(2)}) %collective-permute-start.9) | collective-permute-done | bytes 524320 | tf_op jit(solution)/shard_map/ppermute | solution.py:640
  48.7 4.6 %late_attention.1 = (bf16[512,512]{1,0:T(8,128)(2,1)S(1)}, bf16[512,512]{1,0:T(8,128)(2,1)S(1)}, f32[512,512]{1,0:T(8,128)S(1)}, f32[512,512]{1,0:T(8,128)S(1)}, f32[512,512]{1,0:T(8,128)S(1)}) custom-call(s32[4]{0:T(128)S(1)} %convert_element_type.44.valid_ref, ...), custom_call_target="tpu_custom_call", output_to_operand_aliasing={{2}: (12, {}), {3}: (13, {}), {4}: (14, {})} | custom-call | flops 4000000000 | bytes 14000000 | tf_op jit(solution)/shard_map/late_attention/pallas_call | solution.py:651
  53.3 1.2 %collective-permute-start.12 = (bf16[512,512]{1,0:T(8,128)(2,1)S(1)}, bf16[512,512]{1,0:T(8,128)(2,1)S(1)}, u32[]{:S(2)}, u32[]{:S(2)}) collective-permute-start(bf16[512,512]{1,0:T(8,128)(2,1)S(1)} %get-tuple-element.84), channel_id=1, source_target_pairs={{0,2},{2,0},{1,3},{3,1},{4,6},{6,4},{5,7},{7,5},{8,10},{10,8},{9,1... | collective-permute-start | bytes 1572872 | tf_op jit(solution)/shard_map/ppermute | solution.py:637
  54.5 10.4 %collective-permute-done.12 = bf16[512,512]{1,0:T(8,128)(2,1)S(1)} collective-permute-done((bf16[512,512]{1,0:T(8,128)(2,1)S(1)}, bf16[512,512]{1,0:T(8,128)(2,1)S(1)}, u32[]{:S(2)}, u32[]{:S(2)}) %collective-permute-start.12) | collective-permute-done | bytes 524320 | tf_op jit(solution)/shard_map/ppermute | solution.py:637
  65.3 1.8 %collective-permute-start.13 = (f32[2,512]{1,0:T(2,128)S(1)}, f32[2,512]{1,0:T(2,128)S(1)}, u32[]{:S(2)}, u32[]{:S(2)}) collective-permute-start(f32[2,512]{1,0:T(2,128)S(1)} %pad_maximum_fusion), channel_id=1, source_target_pairs={{0,2},{2,0},{1,3},{3,1},{4,6},{6,4},{5,7},{7,5},{8,10},{10,8},{9,1... | collective-permute-start | bytes 12296 | tf_op jit(solution)/shard_map/ppermute | solution.py:637
  67.1 1.9 %collective-permute-done.13 = f32[2,512]{1,0:T(2,128)S(1)} collective-permute-done((f32[2,512]{1,0:T(2,128)S(1)}, f32[2,512]{1,0:T(2,128)S(1)}, u32[]{:S(2)}, u32[]{:S(2)}) %collective-permute-start.13) | collective-permute-done | bytes 4128 | tf_op jit(solution)/shard_map/ppermute | solution.py:637
  69.0 1.1 %fusion = bf16[1,512,512]{2,1,0:T(8,128)(2,1)} fusion(f32[512]{0:T(512)S(1)} %copy-done.4, f32[512]{0:T(512)S(1)} %copy-done.5, f32[512]{0:T(512)S(1)} %add_rsqrt_fusion, f32[512]{0:T(512)S(1)} %bitcast.40, bf16[512,512]{1,0:T(8,128)(2,1)S(1)} %collective-permute-done.12, bf16[512,512]{1,0:T(8,128)(2,1)S(1)} %get-tuple-element.83, ...), kind=kLoop, calls=%fused_computation.3 | loop fusion | flops 2621440 | bytes 2105344 | tf_op jit(solution)/shard_map/broadcast_in_dim | solution.py:785
  (81 shorter events, 9.3 us)
Async XLA Ops:
  0.0 12.4 %copy-start = (s32[1,16,8]{1,2,0:T(8,128)S(1)}, s32[1,16,8]{1,2,0:T(8,128)}, u32[]{:S(2)}) copy-start(s32[1,16,8]{1,2,0:T(8,128)} %param.18) | copy-start | bytes 1540
  1.1 19.6 %copy-start.1 = (bf16[1,512,512]{2,1,0:T(8,128)(2,1)S(1)}, bf16[1,512,512]{2,1,0:T(8,128)(2,1)}, u32[]{:S(2)}) copy-start(bf16[1,512,512]{2,1,0:T(8,128)(2,1)} %param.11) | copy-start | bytes 1572868
  1.1 17.2 %collective-permute-start.1 = (bf16[256,512]{1,0:T(8,128)(2,1)S(1)}, bf16[256,512]{1,0:T(8,128)(2,1)S(1)}, u32[]{:S(2)}, u32[]{:S(2)}) collective-permute-start(bf16[256,512]{1,0:T(8,128)(2,1)S(1)} %get-tuple-element.102), channel_id=1, source_target_pairs={{0,8},{4,12},{8,0},{12,4},{1,9},{5,13},{9,1},{13,5},{2,10},{6,14},... | collective-permute-start | bytes 786440 | tf_op jit(solution)/shard_map/ppermute | solution.py:640
  5.2 14.1 %collective-permute-start.4 = (bf16[256,512]{1,0:T(8,128)(2,1)S(1)}, bf16[256,512]{1,0:T(8,128)(2,1)S(1)}, u32[]{:S(2)}, u32[]{:S(2)}) collective-permute-start(bf16[256,512]{1,0:T(8,128)(2,1)S(1)} %get-tuple-element.102), channel_id=1, source_target_pairs={{0,4},{4,0},{8,12},{12,8},{1,5},{5,1},{9,13},{13,9},{2,6},{6,2},{1... | collective-permute-start | bytes 786440 | tf_op jit(solution)/shard_map/ppermute | solution.py:640
  6.8 13.9 %collective-permute-start = (bf16[512,512]{1,0:T(8,128)(2,1)}, bf16[512,512]{1,0:T(8,128)(2,1)S(1)}, u32[]{:S(2)}, u32[]{:S(2)}) collective-permute-start(bf16[512,512]{1,0:T(8,128)(2,1)} %bitcast.33), channel_id=1, source_target_pairs={{0,2},{2,0},{1,3},{3,1},{4,6},{6,4},{5,7},{7,5},{8,10},{10,8},{9,1... | collective-permute-start | bytes 1572872 | tf_op jit(solution)/shard_map/ppermute | solution.py:637
  15.3 13.8 %collective-permute-start.2 = (bf16[256,512]{1,0:T(8,128)(2,1)S(1)}, bf16[256,512]{1,0:T(8,128)(2,1)S(1)}, u32[]{:S(2)}, u32[]{:S(2)}) collective-permute-start(bf16[256,512]{1,0:T(8,128)(2,1)S(1)} %get-tuple-element.65), channel_id=1, source_target_pairs={{0,8},{4,12},{8,0},{12,4},{1,9},{5,13},{9,1},{13,5},{2,10},{6,14},... | collective-permute-start | bytes 786440 | tf_op jit(solution)/shard_map/ppermute | solution.py:640
  15.7 13.4 %collective-permute-start.3 = (bf16[256,512]{1,0:T(8,128)(2,1)S(1)}, bf16[256,512]{1,0:T(8,128)(2,1)S(1)}, u32[]{:S(2)}, u32[]{:S(2)}) collective-permute-start(bf16[256,512]{1,0:T(8,128)(2,1)S(1)} %get-tuple-element.65), channel_id=1, source_target_pairs={{0,4},{4,0},{8,12},{12,8},{1,5},{5,1},{9,13},{13,9},{2,6},{6,2},{1... | collective-permute-start | bytes 786440 | tf_op jit(solution)/shard_map/ppermute | solution.py:640
  16.2 1.9 %copy-start.2 = (bf16[3,1024,512]{2,1,0:T(8,128)(2,1)S(1)}, bf16[3,1024,512]{2,1,0:T(8,128)(2,1)}, u32[]{:S(2)}) copy-start(bf16[3,1024,512]{2,1,0:T(8,128)(2,1)} %w_hbm.1) | copy-start | bytes 9437188
  18.3 13.9 %collective-permute-start.6 = (bf16[256,512]{1,0:T(8,128)(2,1)S(1)}, bf16[256,512]{1,0:T(8,128)(2,1)S(1)}, u32[]{:S(2)}, u32[]{:S(2)}) collective-permute-start(bf16[256,512]{1,0:T(8,128)(2,1)S(1)} %collective-permute-done.1.refs_0_), channel_id=1, source_target_pairs={{0,2},{2,0},{1,3},{3,1},{4,6},{6,4},{5,7},{7,5},{8,10},{10,8},{9,1... | collective-permute-start | bytes 786440 | tf_op jit(solution)/shard_map/ppermute | solution.py:637
  19.3 14.6 %collective-permute-start.5 = (bf16[256,512]{1,0:T(8,128)(2,1)S(1)}, bf16[256,512]{1,0:T(8,128)(2,1)S(1)}, u32[]{:S(2)}, u32[]{:S(2)}) collective-permute-start(bf16[256,512]{1,0:T(8,128)(2,1)S(1)} %collective-permute-done.4.refs_0_), channel_id=1, source_target_pairs={{0,2},{2,0},{1,3},{3,1},{4,6},{6,4},{5,7},{7,5},{8,10},{10,8},{9,1... | collective-permute-start | bytes 786440 | tf_op jit(solution)/shard_map/ppermute | solution.py:637
  29.1 14.1 %collective-permute-start.8 = (bf16[256,512]{1,0:T(8,128)(2,1)S(1)}, bf16[256,512]{1,0:T(8,128)(2,1)S(1)}, u32[]{:S(2)}, u32[]{:S(2)}) collective-permute-start(bf16[256,512]{1,0:T(8,128)(2,1)S(1)} %collective-permute-done.2.here1_ref), channel_id=1, source_target_pairs={{0,2},{2,0},{1,3},{3,1},{4,6},{6,4},{5,7},{7,5},{8,10},{10,8},{9,1... | collective-permute-start | bytes 786440 | tf_op jit(solution)/shard_map/ppermute | solution.py:637
  30.2 11.8 %collective-permute-start.10 = (bf16[256,512]{1,0:T(8,128)(2,1)S(1)}, bf16[256,512]{1,0:T(8,128)(2,1)S(1)}, u32[]{:S(2)}, u32[]{:S(2)}) collective-permute-start(bf16[256,512]{1,0:T(8,128)(2,1)S(1)} %collective-permute-done.2.here1_ref), channel_id=1, source_target_pairs={{0,4},{4,0},{8,12},{12,8},{1,5},{5,1},{9,13},{13,9},{2,6},{6,2},{1... | collective-permute-start | bytes 786440 | tf_op jit(solution)/shard_map/ppermute | solution.py:640
  31.7 11.5 %collective-permute-start.7 = (bf16[256,512]{1,0:T(8,128)(2,1)S(1)}, bf16[256,512]{1,0:T(8,128)(2,1)S(1)}, u32[]{:S(2)}, u32[]{:S(2)}) collective-permute-start(bf16[256,512]{1,0:T(8,128)(2,1)S(1)} %collective-permute-done.3.here0_ref), channel_id=1, source_target_pairs={{0,2},{2,0},{1,3},{3,1},{4,6},{6,4},{5,7},{7,5},{8,10},{10,8},{9,1... | collective-permute-start | bytes 786440 | tf_op jit(solution)/shard_map/ppermute | solution.py:637
  32.9 15.5 %collective-permute-start.9 = (bf16[2,256,512]{2,1,0:T(8,128)(2,1)S(1)}, bf16[2,256,512]{2,1,0:T(8,128)(2,1)S(1)}, u32[]{:S(2)}, u32[]{:S(2)}) collective-permute-start(bf16[2,256,512]{2,1,0:T(8,128)(2,1)S(1)} %piece_projections.3.refs_1_), channel_id=1, source_target_pairs={{0,4},{4,0},{8,12},{12,8},{1,5},{5,1},{9,13},{13,9},{2,6},{6,2},{1... | collective-permute-start | bytes 1572872 | tf_op jit(solution)/shard_map/ppermute | solution.py:640
  34.6 8.6 %copy-start.3 = (bf16[512,1024]{1,0:T(8,128)(2,1)S(1)}, bf16[512,1024]{1,0:T(8,128)(2,1)}, u32[]{:S(2)}) copy-start(bf16[512,1024]{1,0:T(8,128)(2,1)} %w_out_hbm.1) | copy-start | bytes 3145732
  42.0 6.7 %collective-permute-start.11 = (bf16[256,512]{1,0:T(8,128)(2,1)S(1)}, bf16[256,512]{1,0:T(8,128)(2,1)S(1)}, u32[]{:S(2)}, u32[]{:S(2)}) collective-permute-start(bf16[256,512]{1,0:T(8,128)(2,1)S(1)} %collective-permute-done.10.here_ref), channel_id=1, source_target_pairs={{0,2},{2,0},{1,3},{3,1},{4,6},{6,4},{5,7},{7,5},{8,10},{10,8},{9,1... | collective-permute-start | bytes 786440 | tf_op jit(solution)/shard_map/ppermute | solution.py:637
  48.7 20.3 %copy-start.4 = (f32[512]{0:T(512)S(1)}, f32[512]{0:T(512)}, u32[]{:S(2)}) copy-start(f32[512]{0:T(512)} %param.15) | copy-start | bytes 6148
  48.7 20.3 %copy-start.5 = (f32[512]{0:T(512)S(1)}, f32[512]{0:T(512)}, u32[]{:S(2)}) copy-start(f32[512]{0:T(512)} %param.14) | copy-start | bytes 6148
  53.3 11.6 %collective-permute-start.12 = (bf16[512,512]{1,0:T(8,128)(2,1)S(1)}, bf16[512,512]{1,0:T(8,128)(2,1)S(1)}, u32[]{:S(2)}, u32[]{:S(2)}) collective-permute-start(bf16[512,512]{1,0:T(8,128)(2,1)S(1)} %get-tuple-element.84), channel_id=1, source_target_pairs={{0,2},{2,0},{1,3},{3,1},{4,6},{6,4},{5,7},{7,5},{8,10},{10,8},{9,1... | collective-permute-start | bytes 1572872 | tf_op jit(solution)/shard_map/ppermute | solution.py:637
  65.3 3.7 %collective-permute-start.13 = (f32[2,512]{1,0:T(2,128)S(1)}, f32[2,512]{1,0:T(2,128)S(1)}, u32[]{:S(2)}, u32[]{:S(2)}) collective-permute-start(f32[2,512]{1,0:T(2,128)S(1)} %pad_maximum_fusion), channel_id=1, source_target_pairs={{0,2},{2,0},{1,3},{3,1},{4,6},{6,4},{5,7},{7,5},{8,10},{10,8},{9,1... | collective-permute-start | bytes 12296 | tf_op jit(solution)/shard_map/ppermute | solution.py:637

commit v6 on v5

--- a/solution.py
+++ b/solution.py
@@ -248,7 +248,7 @@
     return list(zip(refs[0::2], refs[1::2]))
 
 
-def weights_kernel(w_hbm, w_q_ref, w_kv_ref, mark_ref, sem):
+def weights_kernel(w_hbm, unused_hbm, other_hbm, w_q_ref, w_kv_ref, mark_ref, sem):
     mark_ref[...] = jnp.zeros(mark_ref.shape, F32)
     copies = [
         pltpu.make_async_copy(w_hbm.at[0], w_q_ref, sem.at[0]),
@@ -676,15 +676,16 @@
         weights_kernel,
         [],
         [],
-        [w_qkv],
+        [w_qkv, here1a, sbias],
         [array(2 * half, cols, dtype=BF16), array(2, 2 * half, cols, dtype=BF16), array(8, LANES)],
         [],
         [pltpu.SemaphoreType.DMA((2,))],
         1,
         "near_weights",
     )
-    here2a, mark = lax.optimization_barrier((here2a, mark))
-    there1a, there2a = other_half(here1a), other_half(here2a)
+    there2a = other_half(here2a)
+    here1a, own_there = lax.optimization_barrier((here1a, own_there))
+    there1a = other_half(here1a)
     queries, own_kv = whole_call(
         first_kernel,
         [side],
@@ -696,9 +697,6 @@
         2,
         "own_projections",
     )
-    here2b, here1b, own_kv = lax.optimization_barrier((here2b, here1b, own_kv))
-    here3b = from_slot(here2b, 1)
-    there1b, there2b = other_half(here1b), other_half(here2b)
     piece_kv = array(2, piece, cols, dtype=BF16)
 
     def piece_projections(here, there):
@@ -715,6 +713,9 @@
         )[0]
 
     kv2a = piece_projections(here2a, there2a)
+    here2b, here1b, own_kv, kv2a = lax.optimization_barrier((here2b, here1b, own_kv, kv2a))
+    here3b = from_slot(here2b, 1)
+    there1b, there2b = other_half(here1b), other_half(here2b)
     kv3a = from_slot(kv2a, 1)
     kv1a = piece_projections(here1a, there1a)
     there3b = other_half(here3b)

time: 70.5 us -> 70.2 us (level)
    ppermute x6, waiting for transfers between devices: 7.47 us -> 5.51 us  [from_slot(): return lax.ppermute(x, 'ctx', [(i, i ^ slot) for i in range(ctx_count)])]
    ppermute x6, starting transfers between devices: 8.99 us -> 10.8 us  [from_slot(): return lax.ppermute(x, 'ctx', [(i, i ^ slot) for i in range(ctx_count)])]
    ppermute x8, waiting for transfers between devices: 12.9 us -> 14.6 us  [other_half(): return lax.ppermute(x, 'heads', swap)]
    ppermute x8, starting transfers between devices: 9.4 us -> 7.76 us  [other_half(): return lax.ppermute(x, 'heads', swap)]
where the time goes in v6:
time: 70.2 us; the launch traced here: 70 us
  waiting for transfers between devices  20.1 us (29%)
  Pallas kernels  19.6 us (28%)
  starting transfers between devices  18.6 us (26%)
  other arithmetic  6.07 us (9%)
  local copies, waits for them, and re-layouts  5.42 us (8%)
    pallas_call x7, Pallas kernels, whole_call(): pl.pallas_call(functools.partial(kernel, **sizes), in_specs=[pl.BlockSpec...  19.6 us
    ppermute x8, waiting for transfers between devices, other_half(): return lax.ppermute(x, 'heads', swap)  14.6 us
    ppermute x6, starting transfers between devices, from_slot(): return lax.ppermute(x, 'ctx', [(i, i ^ slot) for i in range(ctx_count)])  10.8 us
    ppermute x8, starting transfers between devices, other_half(): return lax.ppermute(x, 'heads', swap)  7.76 us
    ppermute x6, waiting for transfers between devices, from_slot(): return lax.ppermute(x, 'ctx', [(i, i ^ slot) for i in range(ctx_count)])  5.51 us
    unnamed x13, local copies, waits for them, and re-layouts  1.99 us
  transfers between devices with their start and end apart: 14, of which 6 were waited for; matrix products, arithmetic and copies ran while one was open for 10% of the time, Pallas kernels for 22%

profile of v6, /device:TPU:0, one launch (start us, length us, event | category | flops | bytes accessed | tf_op | source)
XLA Modules:
  0.0 70.0 jit_solution(326085634499843406)
XLA Ops:
  0.0 1.1 %slice_bitcast_fusion = (bf16[256,512]{1,0:T(8,128)(2,1)S(1)}, bf16[256,512]{1,0:T(8,128)(2,1)S(1)}) fusion(bf16[1,512,512]{2,1,0:T(8,128)(2,1)} %param.11), kind=kLoop, calls=%fused_computation.5 | loop fusion | bytes 1048576 | tf_op jit(solution)/shard_map/slice | solution.py:667
  1.1 3.1 %collective-permute-start = (bf16[256,512]{1,0:T(8,128)(2,1)S(1)}, bf16[256,512]{1,0:T(8,128)(2,1)S(1)}, u32[]{:S(2)}, u32[]{:S(2)}) collective-permute-start(bf16[256,512]{1,0:T(8,128)(2,1)S(1)} %get-tuple-element.104), channel_id=1, source_target_pairs={{0,4},{4,0},{8,12},{12,8},{1,5},{5,1},{9,13},{13,9},{2,6},{6,2},{1... | collective-permute-start | bytes 786440 | tf_op jit(solution)/shard_map/ppermute | solution.py:640
  4.2 2.6 %collective-permute-start.4 = (bf16[256,512]{1,0:T(8,128)(2,1)S(1)}, bf16[256,512]{1,0:T(8,128)(2,1)S(1)}, u32[]{:S(2)}, u32[]{:S(2)}) collective-permute-start(bf16[256,512]{1,0:T(8,128)(2,1)S(1)} %get-tuple-element.104), channel_id=1, source_target_pairs={{0,8},{4,12},{8,0},{12,4},{1,9},{5,13},{9,1},{13,5},{2,10},{6,14},... | collective-permute-start | bytes 786440 | tf_op jit(solution)/shard_map/ppermute | solution.py:640
  6.8 1.5 %collective-permute-start.1 = (bf16[512,512]{1,0:T(8,128)(2,1)}, bf16[512,512]{1,0:T(8,128)(2,1)S(1)}, u32[]{:S(2)}, u32[]{:S(2)}) collective-permute-start(bf16[512,512]{1,0:T(8,128)(2,1)} %bitcast.33), channel_id=1, source_target_pairs={{0,2},{2,0},{1,3},{3,1},{4,6},{6,4},{5,7},{7,5},{8,10},{10,8},{9,1... | collective-permute-start | bytes 1572872 | tf_op jit(solution)/shard_map/ppermute | solution.py:637
  9.0 0.9 %select_reduce_fusion.2 = s32[4,6]{0,1:T(8,128)S(1)} fusion(s32[8]{0:T(128)} %constant.126.clone, s32[4,6]{0,1:T(8,128)S(1)} %get-tuple-element.114), kind=kLoop, calls=%fused_computation.15 | loop fusion | flops 552 | bytes 224 | tf_op jit(solution)/shard_map/reduce_sum | solution.py:595
  11.6 0.8 %select_reduce_fusion.6.bounds_ref = s32[4]{0:T(128)S(1)} fusion(s32[4]{0:T(128)} %bitcast.44), kind=kLoop, calls=%fused_computation.54 | loop fusion | flops 44 | bytes 32 | tf_op jit(solution)/shard_map/reduce_sum | solution.py:559
  13.6 0.7 %broadcast_subtract_fusion = (s32[4]{0:T(128)S(1)}, s32[4]{0:T(128)S(1)}) fusion(s32[]{:T(128)} %mul.97, s32[1,16]{1,0:T(1,128)} %param.17, s32[]{:T(128)S(6)} %select_n.129), kind=kLoop, calls=%fused_computation.83 | loop fusion | flops 4 | bytes 56 | tf_op jit(solution)/shard_map/sub | solution.py:623
  14.9 3.6 %collective-permute-done.4.refs_0_ = bf16[256,512]{1,0:T(8,128)(2,1)S(1)} collective-permute-done((bf16[256,512]{1,0:T(8,128)(2,1)S(1)}, bf16[256,512]{1,0:T(8,128)(2,1)S(1)}, u32[]{:S(2)}, u32[]{:S(2)}) %collective-permute-start.4) | collective-permute-done | bytes 262176 | tf_op jit(solution)/shard_map/ppermute | solution.py:640
  18.5 1.5 %collective-permute-start.5 = (bf16[256,512]{1,0:T(8,128)(2,1)S(1)}, bf16[256,512]{1,0:T(8,128)(2,1)S(1)}, u32[]{:S(2)}, u32[]{:S(2)}) collective-permute-start(bf16[256,512]{1,0:T(8,128)(2,1)S(1)} %collective-permute-done.4.refs_0_), channel_id=1, source_target_pairs={{0,2},{2,0},{1,3},{3,1},{4,6},{6,4},{5,7},{7,5},{8,10},{10,8},{9,1... | collective-permute-start | bytes 786440 | tf_op jit(solution)/shard_map/ppermute | solution.py:637
  20.8 2.7 %collective-permute-start.3 = (bf16[256,512]{1,0:T(8,128)(2,1)S(1)}, bf16[256,512]{1,0:T(8,128)(2,1)S(1)}, u32[]{:S(2)}, u32[]{:S(2)}) collective-permute-start(bf16[256,512]{1,0:T(8,128)(2,1)S(1)} %get-tuple-element.66), channel_id=1, source_target_pairs={{0,4},{4,0},{8,12},{12,8},{1,5},{5,1},{9,13},{13,9},{2,6},{6,2},{1... | collective-permute-start | bytes 786440 | tf_op jit(solution)/shard_map/ppermute | solution.py:640
  23.5 1.9 %copy-done.2 = bf16[3,1024,512]{2,1,0:T(8,128)(2,1)S(1)} copy-done((bf16[3,1024,512]{2,1,0:T(8,128)(2,1)S(1)}, bf16[3,1024,512]{2,1,0:T(8,128)(2,1)}, u32[]{:S(2)}) %copy-start.2) | copy-done | bytes 3145752
  26.3 0.9 %collective-permute-done.5.refs_1_ = bf16[256,512]{1,0:T(8,128)(2,1)S(1)} collective-permute-done((bf16[256,512]{1,0:T(8,128)(2,1)S(1)}, bf16[256,512]{1,0:T(8,128)(2,1)S(1)}, u32[]{:S(2)}, u32[]{:S(2)}) %collective-permute-start.5) | collective-permute-done | bytes 262176 | tf_op jit(solution)/shard_map/ppermute | solution.py:637
  27.9 1.8 %own_projections.1 = (bf16[512,512]{1,0:T(8,128)(2,1)S(1)}, bf16[2,512,512]{2,1,0:T(8,128)(2,1)S(1)}) custom-call(s32[1]{0:T(128)} %bitcast.9.side_ref, bf16[512,512]{1,0:T(8,128)(2,1)S(1)} %bitcast.34, bf16[512,512]{1,0:T(8,128)(2,1)S(1)} %collective-permute-done.1.there_ref, bf16[1024,512]{1,0:T(8,128)(2,1)S(1)} %get-tuple-element.56.w_q_ref, ...), custom_call_target="tpu_custom_call" | custom-call | flops 2000000000 | bytes 7000000 | tf_op jit(solution)/shard_map/own_projections/pallas_call | solution.py:651
  29.7 1.9 %collective-permute-done.2.here1_ref = bf16[256,512]{1,0:T(8,128)(2,1)S(1)} collective-permute-done((bf16[256,512]{1,0:T(8,128)(2,1)S(1)}, bf16[256,512]{1,0:T(8,128)(2,1)S(1)}, u32[]{:S(2)}, u32[]{:S(2)}) %collective-permute-start.2) | collective-permute-done | bytes 262176 | tf_op jit(solution)/shard_map/ppermute | solution.py:640
  32.1 1.8 %collective-permute-start.10 = (bf16[256,512]{1,0:T(8,128)(2,1)S(1)}, bf16[256,512]{1,0:T(8,128)(2,1)S(1)}, u32[]{:S(2)}, u32[]{:S(2)}) collective-permute-start(bf16[256,512]{1,0:T(8,128)(2,1)S(1)} %collective-permute-done.2.here1_ref), channel_id=1, source_target_pairs={{0,4},{4,0},{8,12},{12,8},{1,5},{5,1},{9,13},{13,9},{2,6},{6,2},{1... | collective-permute-start | bytes 786440 | tf_op jit(solution)/shard_map/ppermute | solution.py:640
  33.9 1.5 %collective-permute-start.7 = (bf16[256,512]{1,0:T(8,128)(2,1)S(1)}, bf16[256,512]{1,0:T(8,128)(2,1)S(1)}, u32[]{:S(2)}, u32[]{:S(2)}) collective-permute-start(bf16[256,512]{1,0:T(8,128)(2,1)S(1)} %collective-permute-done.3.here0_ref), channel_id=1, source_target_pairs={{0,2},{2,0},{1,3},{3,1},{4,6},{6,4},{5,7},{7,5},{8,10},{10,8},{9,1... | collective-permute-start | bytes 786440 | tf_op jit(solution)/shard_map/ppermute | solution.py:637
  36.3 7.4 %early_attention.1 = (f32[512,512]{1,0:T(8,128)S(1)}, f32[512,512]{1,0:T(8,128)S(1)}, f32[512,512]{1,0:T(8,128)S(1)}, bf16[2,1024,512]{2,1,0:T(8,128)(2,1)}, f32...) custom-call(s32[24]{0:T(128)S(1)} %get-tuple-element.64.off_ref, ...), custom_call_target="tpu_custom_call" | custom-call | flops 7000000000 | bytes 24500000 | tf_op jit(solution)/shard_map/early_attention/pallas_call | solution.py:651
  44.3 4.3 %middle_attention.1 = (f32[512,512]{1,0:T(8,128)S(1)}, f32[512,512]{1,0:T(8,128)S(1)}, f32[512,512]{1,0:T(8,128)S(1)}, f32[64,512]{1,0:T(8,128)S(1)}, f32[64,128...) custom-call(s32[7]{0:T(128)S(1)} %convert_element_type.42.valid_ref, ...), custom_call_target="tpu_custom_call", output_to_operand_aliasing={{0}: (10, {}), {1}: (11, {}), {2}: (12, {})} | custom-call | flops 5000000000 | bytes 17500000 | tf_op jit(solution)/shard_map/middle_attention/pallas_call | solution.py:651
  48.6 1.5 %collective-permute-done.11.there_ref = bf16[256,512]{1,0:T(8,128)(2,1)S(1)} collective-permute-done((bf16[256,512]{1,0:T(8,128)(2,1)S(1)}, bf16[256,512]{1,0:T(8,128)(2,1)S(1)}, u32[]{:S(2)}, u32[]{:S(2)}) %collective-permute-start.11) | collective-permute-done | bytes 262176 | tf_op jit(solution)/shard_map/ppermute | solution.py:637
  50.1 4.5 %late_attention.1 = (bf16[512,512]{1,0:T(8,128)(2,1)S(1)}, bf16[512,512]{1,0:T(8,128)(2,1)S(1)}, f32[512,512]{1,0:T(8,128)S(1)}, f32[512,512]{1,0:T(8,128)S(1)}, f32[512,512]{1,0:T(8,128)S(1)}) custom-call(s32[4]{0:T(128)S(1)} %convert_element_type.44.valid_ref, ...), custom_call_target="tpu_custom_call", output_to_operand_aliasing={{2}: (12, {}), {3}: (13, {}), {4}: (14, {})} | custom-call | flops 4000000000 | bytes 14000000 | tf_op jit(solution)/shard_map/late_attention/pallas_call | solution.py:651
  55.3 9.4 %collective-permute-done.12 = bf16[512,512]{1,0:T(8,128)(2,1)S(1)} collective-permute-done((bf16[512,512]{1,0:T(8,128)(2,1)S(1)}, bf16[512,512]{1,0:T(8,128)(2,1)S(1)}, u32[]{:S(2)}, u32[]{:S(2)}) %collective-permute-start.12) | collective-permute-done | bytes 524320 | tf_op jit(solution)/shard_map/ppermute | solution.py:637
  65.1 0.9 %collective-permute-start.13 = (f32[2,512]{1,0:T(2,128)S(1)}, f32[2,512]{1,0:T(2,128)S(1)}, u32[]{:S(2)}, u32[]{:S(2)}) collective-permute-start(f32[2,512]{1,0:T(2,128)S(1)} %pad_maximum_fusion), channel_id=1, source_target_pairs={{0,2},{2,0},{1,3},{3,1},{4,6},{6,4},{5,7},{7,5},{8,10},{10,8},{9,1... | collective-permute-start | bytes 12296 | tf_op jit(solution)/shard_map/ppermute | solution.py:637
  66.0 2.8 %collective-permute-done.13 = f32[2,512]{1,0:T(2,128)S(1)} collective-permute-done((f32[2,512]{1,0:T(2,128)S(1)}, f32[2,512]{1,0:T(2,128)S(1)}, u32[]{:S(2)}, u32[]{:S(2)}) %collective-permute-start.13) | collective-permute-done | bytes 4128 | tf_op jit(solution)/shard_map/ppermute | solution.py:637
  68.9 1.2 %fusion = bf16[1,512,512]{2,1,0:T(8,128)(2,1)} fusion(f32[512]{0:T(512)S(1)} %copy-done.4, f32[512]{0:T(512)S(1)} %copy-done.5, f32[512]{0:T(512)S(1)} %add_rsqrt_fusion, f32[512]{0:T(512)S(1)} %bitcast.40, bf16[512,512]{1,0:T(8,128)(2,1)S(1)} %collective-permute-done.12, bf16[512,512]{1,0:T(8,128)(2,1)S(1)} %get-tuple-element.85, ...), kind=kLoop, calls=%fused_computation.3 | loop fusion | flops 2621440 | bytes 2105344 | tf_op jit(solution)/shard_map/broadcast_in_dim | solution.py:786
  (81 shorter events, 9.7 us)
Async XLA Ops:
  0.0 12.3 %copy-start = (s32[1,16,8]{1,2,0:T(8,128)S(1)}, s32[1,16,8]{1,2,0:T(8,128)}, u32[]{:S(2)}) copy-start(s32[1,16,8]{1,2,0:T(8,128)} %param.18) | copy-start | bytes 1540
  1.1 22.4 %collective-permute-start = (bf16[256,512]{1,0:T(8,128)(2,1)S(1)}, bf16[256,512]{1,0:T(8,128)(2,1)S(1)}, u32[]{:S(2)}, u32[]{:S(2)}) collective-permute-start(bf16[256,512]{1,0:T(8,128)(2,1)S(1)} %get-tuple-element.104), channel_id=1, source_target_pairs={{0,4},{4,0},{8,12},{12,8},{1,5},{5,1},{9,13},{13,9},{2,6},{6,2},{1... | collective-permute-start | bytes 786440 | tf_op jit(solution)/shard_map/ppermute | solution.py:640
  4.2 14.3 %collective-permute-start.4 = (bf16[256,512]{1,0:T(8,128)(2,1)S(1)}, bf16[256,512]{1,0:T(8,128)(2,1)S(1)}, u32[]{:S(2)}, u32[]{:S(2)}) collective-permute-start(bf16[256,512]{1,0:T(8,128)(2,1)S(1)} %get-tuple-element.104), channel_id=1, source_target_pairs={{0,8},{4,12},{8,0},{12,4},{1,9},{5,13},{9,1},{13,5},{2,10},{6,14},... | collective-permute-start | bytes 786440 | tf_op jit(solution)/shard_map/ppermute | solution.py:640
  6.8 18.9 %collective-permute-start.1 = (bf16[512,512]{1,0:T(8,128)(2,1)}, bf16[512,512]{1,0:T(8,128)(2,1)S(1)}, u32[]{:S(2)}, u32[]{:S(2)}) collective-permute-start(bf16[512,512]{1,0:T(8,128)(2,1)} %bitcast.33), channel_id=1, source_target_pairs={{0,2},{2,0},{1,3},{3,1},{4,6},{6,4},{5,7},{7,5},{8,10},{10,8},{9,1... | collective-permute-start | bytes 1572872 | tf_op jit(solution)/shard_map/ppermute | solution.py:637
  18.5 8.6 %collective-permute-start.5 = (bf16[256,512]{1,0:T(8,128)(2,1)S(1)}, bf16[256,512]{1,0:T(8,128)(2,1)S(1)}, u32[]{:S(2)}, u32[]{:S(2)}) collective-permute-start(bf16[256,512]{1,0:T(8,128)(2,1)S(1)} %collective-permute-done.4.refs_0_), channel_id=1, source_target_pairs={{0,2},{2,0},{1,3},{3,1},{4,6},{6,4},{5,7},{7,5},{8,10},{10,8},{9,1... | collective-permute-start | bytes 786440 | tf_op jit(solution)/shard_map/ppermute | solution.py:637
  20.4 11.1 %collective-permute-start.2 = (bf16[256,512]{1,0:T(8,128)(2,1)S(1)}, bf16[256,512]{1,0:T(8,128)(2,1)S(1)}, u32[]{:S(2)}, u32[]{:S(2)}) collective-permute-start(bf16[256,512]{1,0:T(8,128)(2,1)S(1)} %get-tuple-element.66), channel_id=1, source_target_pairs={{0,8},{4,12},{8,0},{12,4},{1,9},{5,13},{9,1},{13,5},{2,10},{6,14},... | collective-permute-start | bytes 786440 | tf_op jit(solution)/shard_map/ppermute | solution.py:640
  20.8 10.7 %collective-permute-start.3 = (bf16[256,512]{1,0:T(8,128)(2,1)S(1)}, bf16[256,512]{1,0:T(8,128)(2,1)S(1)}, u32[]{:S(2)}, u32[]{:S(2)}) collective-permute-start(bf16[256,512]{1,0:T(8,128)(2,1)S(1)} %get-tuple-element.66), channel_id=1, source_target_pairs={{0,4},{4,0},{8,12},{12,8},{1,5},{5,1},{9,13},{13,9},{2,6},{6,2},{1... | collective-permute-start | bytes 786440 | tf_op jit(solution)/shard_map/ppermute | solution.py:640
  23.5 1.9 %copy-start.2 = (bf16[3,1024,512]{2,1,0:T(8,128)(2,1)S(1)}, bf16[3,1024,512]{2,1,0:T(8,128)(2,1)}, u32[]{:S(2)}) copy-start(bf16[3,1024,512]{2,1,0:T(8,128)(2,1)} %w_hbm.1) | copy-start | bytes 9437188
  25.7 2.2 %copy-start.1 = (bf16[1,512,512]{2,1,0:T(8,128)(2,1)S(1)}, bf16[1,512,512]{2,1,0:T(8,128)(2,1)}, u32[]{:S(2)}) copy-start(bf16[1,512,512]{2,1,0:T(8,128)(2,1)} %param.11) | copy-start | bytes 1572868
  25.7 9.9 %collective-permute-start.6 = (bf16[256,512]{1,0:T(8,128)(2,1)S(1)}, bf16[256,512]{1,0:T(8,128)(2,1)S(1)}, u32[]{:S(2)}, u32[]{:S(2)}) collective-permute-start(bf16[256,512]{1,0:T(8,128)(2,1)S(1)} %collective-permute-done.unused_hbm.refs_0_), channel_id=1, source_target_pairs={{0,2},{2,0},{1,3},{3,1},{4,6},{6,4},{5,7},{7,5},{8,10},{10,8},{9,1... | collective-permute-start | bytes 786440 | tf_op jit(solution)/shard_map/ppermute | solution.py:637
  31.5 12.8 %collective-permute-start.8 = (bf16[256,512]{1,0:T(8,128)(2,1)S(1)}, bf16[256,512]{1,0:T(8,128)(2,1)S(1)}, u32[]{:S(2)}, u32[]{:S(2)}) collective-permute-start(bf16[256,512]{1,0:T(8,128)(2,1)S(1)} %collective-permute-done.2.here1_ref), channel_id=1, source_target_pairs={{0,2},{2,0},{1,3},{3,1},{4,6},{6,4},{5,7},{7,5},{8,10},{10,8},{9,1... | collective-permute-start | bytes 786440 | tf_op jit(solution)/shard_map/ppermute | solution.py:637
  32.1 11.6 %collective-permute-start.10 = (bf16[256,512]{1,0:T(8,128)(2,1)S(1)}, bf16[256,512]{1,0:T(8,128)(2,1)S(1)}, u32[]{:S(2)}, u32[]{:S(2)}) collective-permute-start(bf16[256,512]{1,0:T(8,128)(2,1)S(1)} %collective-permute-done.2.here1_ref), channel_id=1, source_target_pairs={{0,4},{4,0},{8,12},{12,8},{1,5},{5,1},{9,13},{13,9},{2,6},{6,2},{1... | collective-permute-start | bytes 786440 | tf_op jit(solution)/shard_map/ppermute | solution.py:640
  33.9 10.4 %collective-permute-start.7 = (bf16[256,512]{1,0:T(8,128)(2,1)S(1)}, bf16[256,512]{1,0:T(8,128)(2,1)S(1)}, u32[]{:S(2)}, u32[]{:S(2)}) collective-permute-start(bf16[256,512]{1,0:T(8,128)(2,1)S(1)} %collective-permute-done.3.here0_ref), channel_id=1, source_target_pairs={{0,2},{2,0},{1,3},{3,1},{4,6},{6,4},{5,7},{7,5},{8,10},{10,8},{9,1... | collective-permute-start | bytes 786440 | tf_op jit(solution)/shard_map/ppermute | solution.py:637
  35.3 14.8 %collective-permute-start.9 = (bf16[2,256,512]{2,1,0:T(8,128)(2,1)S(1)}, bf16[2,256,512]{2,1,0:T(8,128)(2,1)S(1)}, u32[]{:S(2)}, u32[]{:S(2)}) collective-permute-start(bf16[2,256,512]{2,1,0:T(8,128)(2,1)S(1)} %piece_projections.2.refs_1_), channel_id=1, source_target_pairs={{0,4},{4,0},{8,12},{12,8},{1,5},{5,1},{9,13},{13,9},{2,6},{6,2},{1... | collective-permute-start | bytes 1572872 | tf_op jit(solution)/shard_map/ppermute | solution.py:640
  36.3 8.0 %copy-start.3 = (bf16[512,1024]{1,0:T(8,128)(2,1)S(1)}, bf16[512,1024]{1,0:T(8,128)(2,1)}, u32[]{:S(2)}) copy-start(bf16[512,1024]{1,0:T(8,128)(2,1)} %w_out_hbm.1) | copy-start | bytes 3145732
  43.7 6.4 %collective-permute-start.11 = (bf16[256,512]{1,0:T(8,128)(2,1)S(1)}, bf16[256,512]{1,0:T(8,128)(2,1)S(1)}, u32[]{:S(2)}, u32[]{:S(2)}) collective-permute-start(bf16[256,512]{1,0:T(8,128)(2,1)S(1)} %collective-permute-done.10.here_ref), channel_id=1, source_target_pairs={{0,2},{2,0},{1,3},{3,1},{4,6},{6,4},{5,7},{7,5},{8,10},{10,8},{9,1... | collective-permute-start | bytes 786440 | tf_op jit(solution)/shard_map/ppermute | solution.py:637
  50.1 18.7 %copy-start.4 = (f32[512]{0:T(512)S(1)}, f32[512]{0:T(512)}, u32[]{:S(2)}) copy-start(f32[512]{0:T(512)} %param.15) | copy-start | bytes 6148
  50.1 18.7 %copy-start.5 = (f32[512]{0:T(512)S(1)}, f32[512]{0:T(512)}, u32[]{:S(2)}) copy-start(f32[512]{0:T(512)} %param.14) | copy-start | bytes 6148
  54.7 10.1 %collective-permute-start.12 = (bf16[512,512]{1,0:T(8,128)(2,1)S(1)}, bf16[512,512]{1,0:T(8,128)(2,1)S(1)}, u32[]{:S(2)}, u32[]{:S(2)}) collective-permute-start(bf16[512,512]{1,0:T(8,128)(2,1)S(1)} %get-tuple-element.86), channel_id=1, source_target_pairs={{0,2},{2,0},{1,3},{3,1},{4,6},{6,4},{5,7},{7,5},{8,10},{10,8},{9,1... | collective-permute-start | bytes 1572872 | tf_op jit(solution)/shard_map/ppermute | solution.py:637
  65.1 3.7 %collective-permute-start.13 = (f32[2,512]{1,0:T(2,128)S(1)}, f32[2,512]{1,0:T(2,128)S(1)}, u32[]{:S(2)}, u32[]{:S(2)}) collective-permute-start(f32[2,512]{1,0:T(2,128)S(1)} %pad_maximum_fusion), channel_id=1, source_target_pairs={{0,2},{2,0},{1,3},{3,1},{4,6},{6,4},{5,7},{7,5},{8,10},{10,8},{9,1... | collective-permute-start | bytes 12296 | tf_op jit(solution)/shard_map/ppermute | solution.py:637

commit v7 on v6

--- a/solution.py
+++ b/solution.py
@@ -402,10 +402,10 @@
 
 
 def early_kernel(
-    off_ref, pos_ref, bounds_ref, base_ref, mine_ref, q_ref, sbias_ref, own_ref, *refs,
+    off_ref, pos_ref, bounds_ref, base_ref, q_ref, own_ref, *refs,
     items, pair_count, head_count,
 ):
-    *held, acc_ref, top_ref, sum_ref, kv_ref, sacc_ref, sml_ref, squery_ref = refs[:-3]
+    *held, acc_ref, top_ref, sum_ref, kv_ref = refs[:-3]
     bias_ref, score_ref, sem = refs[-3:]
     copies = []
     row = 0
@@ -417,8 +417,23 @@
     for copy in copies:
         copy.wait()
     attend_blocks(
-        0, acc_ref.shape[0] // BLOCK, off_ref, pos_ref, bounds_ref, base_ref, q_ref, kv_ref,
+        0, acc_ref.shape[0] // BLOCK // 2, off_ref, pos_ref, bounds_ref, base_ref, q_ref, kv_ref,
         acc_ref, top_ref, sum_ref, bias_ref, score_ref, items, pair_count, head_count,
+    )
+
+
+def second_kernel(
+    off_ref, pos_ref, bounds_ref, base_ref, mine_ref,
+    q_ref, sbias_ref, kv_ref, acc_in, top_in, sum_in,
+    acc_ref, top_ref, sum_ref, sacc_ref, sml_ref, squery_ref, bias_ref, score_ref,
+    *, items, pair_count, head_count,
+):
+    rows = acc_ref.shape[0] // 2
+    rest = pl.ds(rows, rows)
+    attend_blocks(
+        rows // BLOCK, rows // BLOCK, off_ref, pos_ref, bounds_ref, base_ref, q_ref, kv_ref,
+        acc_ref.at[rest], top_ref.at[rest], sum_ref.at[rest], bias_ref, score_ref,
+        items, pair_count, head_count,
     )
     squery_ref[...] = summary_queries(mine_ref, q_ref, head_count)
     bias = sbias_ref[:, : kv_ref.shape[1]]
@@ -724,23 +739,34 @@
     state = [array(tok_rows, cols)] * 3
     srows = 8 * head_count
     summary_state = [array(srows, cols), array(srows, LANES)]
-    *state, kv, sacc, sml, squery = whole_call(
+    score_scratch = [
+        pltpu.VMEM((BLOCK, items * BLOCK), F32),
+        pltpu.VMEM((head_count // PAIR, PAIR * BLOCK, items * BLOCK), F32),
+    ]
+    *state, kv = whole_call(
         early_kernel,
+        [early_off, early_pos, bounds, base],
+        [queries, own_kv, kv1a, kv2a],
+        [],
+        state + [array(2, early_rows, cols, dtype=BF16)],
+        [],
+        score_scratch + [pltpu.SemaphoreType.DMA((3,))],
+        4,
+        "early_attention",
+        items=items,
+        **sizes,
+    )
+    *state, sacc, sml, squery = whole_call(
+        second_kernel,
         [early_off, early_pos, bounds, base, mine],
-        [queries, sbias, own_kv, kv1a, kv2a],
-        [],
-        state
-        + [array(2, early_rows, cols, dtype=BF16)]
-        + summary_state
-        + [array(srows, cols, dtype=BF16)],
-        [],
-        [
-            pltpu.VMEM((BLOCK, items * BLOCK), F32),
-            pltpu.VMEM((head_count // PAIR, PAIR * BLOCK, items * BLOCK), F32),
-            pltpu.SemaphoreType.DMA((3,)),
-        ],
-        7,
-        "early_attention",
+        [queries, sbias, kv, *state],
+        [],
+        [array(tok_rows, cols)] * 3 + summary_state + [array(srows, cols, dtype=BF16)],
+        [],
+        score_scratch,
+        4,
+        "second_attention",
+        aliases={8 + i: i for i in range(3)},
         items=items,
         **sizes,
     )

time: 70.2 us -> 70.5 us (level)
    pallas_call x7 -> x8, Pallas kernels: 19.6 us -> 20 us  [whole_call(): pl.pallas_call(functools.partial(kernel, **sizes), in_specs=[pl.BlockSpec...]
  transfers between devices with their start and end apart: 14 -> 14, of which waited for: 6 -> 7; matrix products, arithmetic and copies ran while one was open for 10% -> 10% of each run, Pallas kernels for 22% -> 22%
where the time goes in v7:
time: 70.5 us; the launch traced here: 70.3 us
  waiting for transfers between devices  20 us (28%)
  Pallas kernels  20 us (28%)
  starting transfers between devices  18.5 us (26%)
  other arithmetic  6.07 us (9%)
  local copies, waits for them, and re-layouts  5.42 us (8%)
    pallas_call x8, Pallas kernels, whole_call(): pl.pallas_call(functools.partial(kernel, **sizes), in_specs=[pl.BlockSpec...  20 us
    ppermute x8, waiting for transfers between devices, other_half(): return lax.ppermute(x, 'heads', swap)  14.2 us
    ppermute x6, starting transfers between devices, from_slot(): return lax.ppermute(x, 'ctx', [(i, i ^ slot) for i in range(ctx_count)])  10.8 us
    ppermute x8, starting transfers between devices, other_half(): return lax.ppermute(x, 'heads', swap)  7.72 us
    ppermute x6, waiting for transfers between devices, from_slot(): return lax.ppermute(x, 'ctx', [(i, i ^ slot) for i in range(ctx_count)])  5.78 us
    unnamed x13, local copies, waits for them, and re-layouts  1.99 us
  transfers between devices with their start and end apart: 14, of which 7 were waited for; matrix products, arithmetic and copies ran while one was open for 10% of the time, Pallas kernels for 22%

profile of v7, /device:TPU:0, one launch (start us, length us, event | category | flops | bytes accessed | tf_op | source)
XLA Modules:
  0.0 70.3 jit_solution(14732833848931993798)
XLA Ops:
  0.0 1.1 %slice_bitcast_fusion = (bf16[256,512]{1,0:T(8,128)(2,1)S(1)}, bf16[256,512]{1,0:T(8,128)(2,1)S(1)}) fusion(bf16[1,512,512]{2,1,0:T(8,128)(2,1)} %param.11), kind=kLoop, calls=%fused_computation.5 | loop fusion | bytes 1048576 | tf_op jit(solution)/shard_map/slice | solution.py:682
  1.1 3.1 %collective-permute-start = (bf16[256,512]{1,0:T(8,128)(2,1)S(1)}, bf16[256,512]{1,0:T(8,128)(2,1)S(1)}, u32[]{:S(2)}, u32[]{:S(2)}) collective-permute-start(bf16[256,512]{1,0:T(8,128)(2,1)S(1)} %get-tuple-element.112), channel_id=1, source_target_pairs={{0,4},{4,0},{8,12},{12,8},{1,5},{5,1},{9,13},{13,9},{2,6},{6,2},{1... | collective-permute-start | bytes 786440 | tf_op jit(solution)/shard_map/ppermute | solution.py:655
  4.2 2.6 %collective-permute-start.4 = (bf16[256,512]{1,0:T(8,128)(2,1)S(1)}, bf16[256,512]{1,0:T(8,128)(2,1)S(1)}, u32[]{:S(2)}, u32[]{:S(2)}) collective-permute-start(bf16[256,512]{1,0:T(8,128)(2,1)S(1)} %get-tuple-element.112), channel_id=1, source_target_pairs={{0,8},{4,12},{8,0},{12,4},{1,9},{5,13},{9,1},{13,5},{2,10},{6,14},... | collective-permute-start | bytes 786440 | tf_op jit(solution)/shard_map/ppermute | solution.py:655
  6.8 1.5 %collective-permute-start.1 = (bf16[512,512]{1,0:T(8,128)(2,1)}, bf16[512,512]{1,0:T(8,128)(2,1)S(1)}, u32[]{:S(2)}, u32[]{:S(2)}) collective-permute-start(bf16[512,512]{1,0:T(8,128)(2,1)} %bitcast.33), channel_id=1, source_target_pairs={{0,2},{2,0},{1,3},{3,1},{4,6},{6,4},{5,7},{7,5},{8,10},{10,8},{9,1... | collective-permute-start | bytes 1572872 | tf_op jit(solution)/shard_map/ppermute | solution.py:652
  9.0 0.9 %select_reduce_fusion.2 = s32[4,6]{0,1:T(8,128)S(1)} fusion(s32[8]{0:T(128)} %constant.126.clone, s32[4,6]{0,1:T(8,128)S(1)} %get-tuple-element.122), kind=kLoop, calls=%fused_computation.15 | loop fusion | flops 552 | bytes 224 | tf_op jit(solution)/shard_map/reduce_sum | solution.py:610
  11.6 0.8 %select_reduce_fusion.6.bounds_ref = s32[4]{0:T(128)S(1)} fusion(s32[4]{0:T(128)} %bitcast.44), kind=kLoop, calls=%fused_computation.54 | loop fusion | flops 44 | bytes 32 | tf_op jit(solution)/shard_map/reduce_sum | solution.py:574
  14.9 3.6 %collective-permute-done.4.refs_0_ = bf16[256,512]{1,0:T(8,128)(2,1)S(1)} collective-permute-done((bf16[256,512]{1,0:T(8,128)(2,1)S(1)}, bf16[256,512]{1,0:T(8,128)(2,1)S(1)}, u32[]{:S(2)}, u32[]{:S(2)}) %collective-permute-start.4) | collective-permute-done | bytes 262176 | tf_op jit(solution)/shard_map/ppermute | solution.py:655
  18.5 1.5 %collective-permute-start.5 = (bf16[256,512]{1,0:T(8,128)(2,1)S(1)}, bf16[256,512]{1,0:T(8,128)(2,1)S(1)}, u32[]{:S(2)}, u32[]{:S(2)}) collective-permute-start(bf16[256,512]{1,0:T(8,128)(2,1)S(1)} %collective-permute-done.4.refs_0_), channel_id=1, source_target_pairs={{0,2},{2,0},{1,3},{3,1},{4,6},{6,4},{5,7},{7,5},{8,10},{10,8},{9,1... | collective-permute-start | bytes 786440 | tf_op jit(solution)/shard_map/ppermute | solution.py:652
  20.8 2.7 %collective-permute-start.3 = (bf16[256,512]{1,0:T(8,128)(2,1)S(1)}, bf16[256,512]{1,0:T(8,128)(2,1)S(1)}, u32[]{:S(2)}, u32[]{:S(2)}) collective-permute-start(bf16[256,512]{1,0:T(8,128)(2,1)S(1)} %get-tuple-element.70), channel_id=1, source_target_pairs={{0,4},{4,0},{8,12},{12,8},{1,5},{5,1},{9,13},{13,9},{2,6},{6,2},{1... | collective-permute-start | bytes 786440 | tf_op jit(solution)/shard_map/ppermute | solution.py:655
  23.5 1.9 %copy-done.2 = bf16[3,1024,512]{2,1,0:T(8,128)(2,1)S(1)} copy-done((bf16[3,1024,512]{2,1,0:T(8,128)(2,1)S(1)}, bf16[3,1024,512]{2,1,0:T(8,128)(2,1)}, u32[]{:S(2)}) %copy-start.2) | copy-done | bytes 3145752
  26.3 0.9 %collective-permute-done.5.refs_1_ = bf16[256,512]{1,0:T(8,128)(2,1)S(1)} collective-permute-done((bf16[256,512]{1,0:T(8,128)(2,1)S(1)}, bf16[256,512]{1,0:T(8,128)(2,1)S(1)}, u32[]{:S(2)}, u32[]{:S(2)}) %collective-permute-start.5) | collective-permute-done | bytes 262176 | tf_op jit(solution)/shard_map/ppermute | solution.py:652
  27.9 1.8 %own_projections.1 = (bf16[512,512]{1,0:T(8,128)(2,1)S(1)}, bf16[2,512,512]{2,1,0:T(8,128)(2,1)S(1)}) custom-call(s32[1]{0:T(128)} %bitcast.9.side_ref, bf16[512,512]{1,0:T(8,128)(2,1)S(1)} %bitcast.34, bf16[512,512]{1,0:T(8,128)(2,1)S(1)} %collective-permute-done.1.there_ref, bf16[1024,512]{1,0:T(8,128)(2,1)S(1)} %get-tuple-element.60.w_q_ref, ...), custom_call_target="tpu_custom_call" | custom-call | flops 2000000000 | bytes 7000000 | tf_op jit(solution)/shard_map/own_projections/pallas_call | solution.py:666
  29.7 1.9 %collective-permute-done.2.here1_ref = bf16[256,512]{1,0:T(8,128)(2,1)S(1)} collective-permute-done((bf16[256,512]{1,0:T(8,128)(2,1)S(1)}, bf16[256,512]{1,0:T(8,128)(2,1)S(1)}, u32[]{:S(2)}, u32[]{:S(2)}) %collective-permute-start.2) | collective-permute-done | bytes 262176 | tf_op jit(solution)/shard_map/ppermute | solution.py:655
  32.1 1.8 %collective-permute-start.10 = (bf16[256,512]{1,0:T(8,128)(2,1)S(1)}, bf16[256,512]{1,0:T(8,128)(2,1)S(1)}, u32[]{:S(2)}, u32[]{:S(2)}) collective-permute-start(bf16[256,512]{1,0:T(8,128)(2,1)S(1)} %collective-permute-done.2.here1_ref), channel_id=1, source_target_pairs={{0,4},{4,0},{8,12},{12,8},{1,5},{5,1},{9,13},{13,9},{2,6},{6,2},{1... | collective-permute-start | bytes 786440 | tf_op jit(solution)/shard_map/ppermute | solution.py:655
  33.9 1.5 %collective-permute-start.7 = (bf16[256,512]{1,0:T(8,128)(2,1)S(1)}, bf16[256,512]{1,0:T(8,128)(2,1)S(1)}, u32[]{:S(2)}, u32[]{:S(2)}) collective-permute-start(bf16[256,512]{1,0:T(8,128)(2,1)S(1)} %collective-permute-done.3.here0_ref), channel_id=1, source_target_pairs={{0,2},{2,0},{1,3},{3,1},{4,6},{6,4},{5,7},{7,5},{8,10},{10,8},{9,1... | collective-permute-start | bytes 786440 | tf_op jit(solution)/shard_map/ppermute | solution.py:652
  36.3 3.4 %early_attention.1 = (f32[512,512]{1,0:T(8,128)S(1)}, f32[512,512]{1,0:T(8,128)S(1)}, f32[512,512]{1,0:T(8,128)S(1)}, bf16[2,1024,512]{2,1,0:T(8,128)(2,1)S(1)}) custom-call(s32[24]{0:T(128)S(1)} %get-tuple-element.68.off_ref, s32[24]{0:T(128)S(1)} %get-tuple-element.69.pos_ref, s32[4]{0:T(128)S(1)} %select_reduce_fusion.6.bounds_ref, s32[1]{0:T(128)} %bitcast.6.base_ref, ...), custom_call_target="tpu_custom_call" | custom-call | flops 4000000000 | bytes 14000000 | tf_op jit(solution)/shard_map/early_attention/pallas_call | solution.py:666
  39.7 4.1 %second_attention.1 = (f32[512,512]{1,0:T(8,128)S(1)}, f32[512,512]{1,0:T(8,128)S(1)}, f32[512,512]{1,0:T(8,128)S(1)}, f32[64,512]{1,0:T(8,128)S(1)}, f32[64,128...) custom-call(s32[24]{0:T(128)S(1)} %get-tuple-element.68.off_ref, ...), custom_call_target="tpu_custom_call", output_to_operand_aliasing={{0}: (8, {}), {1}: (9, {}), {2}: (10, {})} | custom-call | flops 4000000000 | bytes 14000000 | tf_op jit(solution)/shard_map/second_attention/pallas_call | solution.py:666
  44.4 4.4 %middle_attention.1 = (f32[512,512]{1,0:T(8,128)S(1)}, f32[512,512]{1,0:T(8,128)S(1)}, f32[512,512]{1,0:T(8,128)S(1)}, f32[64,512]{1,0:T(8,128)S(1)}, f32[64,128...) custom-call(s32[7]{0:T(128)S(1)} %convert_element_type.42.valid_ref, ...), custom_call_target="tpu_custom_call", output_to_operand_aliasing={{0}: (10, {}), {1}: (11, {}), {2}: (12, {})} | custom-call | flops 5000000000 | bytes 17500000 | tf_op jit(solution)/shard_map/middle_attention/pallas_call | solution.py:666
  49.0 1.2 %collective-permute-done.11.there_ref = bf16[256,512]{1,0:T(8,128)(2,1)S(1)} collective-permute-done((bf16[256,512]{1,0:T(8,128)(2,1)S(1)}, bf16[256,512]{1,0:T(8,128)(2,1)S(1)}, u32[]{:S(2)}, u32[]{:S(2)}) %collective-permute-start.11) | collective-permute-done | bytes 262176 | tf_op jit(solution)/shard_map/ppermute | solution.py:652
  50.2 4.8 %late_attention.1 = (bf16[512,512]{1,0:T(8,128)(2,1)S(1)}, bf16[512,512]{1,0:T(8,128)(2,1)S(1)}, f32[512,512]{1,0:T(8,128)S(1)}, f32[512,512]{1,0:T(8,128)S(1)}, f32[512,512]{1,0:T(8,128)S(1)}) custom-call(s32[4]{0:T(128)S(1)} %convert_element_type.44.valid_ref, ...), custom_call_target="tpu_custom_call", output_to_operand_aliasing={{2}: (12, {}), {3}: (13, {}), {4}: (14, {})} | custom-call | flops 4000000000 | bytes 14000000 | tf_op jit(solution)/shard_map/late_attention/pallas_call | solution.py:666
  55.6 9.4 %collective-permute-done.12 = bf16[512,512]{1,0:T(8,128)(2,1)S(1)} collective-permute-done((bf16[512,512]{1,0:T(8,128)(2,1)S(1)}, bf16[512,512]{1,0:T(8,128)(2,1)S(1)}, u32[]{:S(2)}, u32[]{:S(2)}) %collective-permute-start.12) | collective-permute-done | bytes 524320 | tf_op jit(solution)/shard_map/ppermute | solution.py:652
  65.4 0.9 %collective-permute-start.13 = (f32[2,512]{1,0:T(2,128)S(1)}, f32[2,512]{1,0:T(2,128)S(1)}, u32[]{:S(2)}, u32[]{:S(2)}) collective-permute-start(f32[2,512]{1,0:T(2,128)S(1)} %pad_maximum_fusion), channel_id=1, source_target_pairs={{0,2},{2,0},{1,3},{3,1},{4,6},{6,4},{5,7},{7,5},{8,10},{10,8},{9,1... | collective-permute-start | bytes 12296 | tf_op jit(solution)/shard_map/ppermute | solution.py:652
  66.3 2.8 %collective-permute-done.13 = f32[2,512]{1,0:T(2,128)S(1)} collective-permute-done((f32[2,512]{1,0:T(2,128)S(1)}, f32[2,512]{1,0:T(2,128)S(1)}, u32[]{:S(2)}, u32[]{:S(2)}) %collective-permute-start.13) | collective-permute-done | bytes 4128 | tf_op jit(solution)/shard_map/ppermute | solution.py:652
  69.1 1.2 %fusion = bf16[1,512,512]{2,1,0:T(8,128)(2,1)} fusion(f32[512]{0:T(512)S(1)} %copy-done.4, f32[512]{0:T(512)S(1)} %copy-done.5, f32[512]{0:T(512)S(1)} %add_rsqrt_fusion, f32[512]{0:T(512)S(1)} %bitcast.40, bf16[512,512]{1,0:T(8,128)(2,1)S(1)} %collective-permute-done.12, bf16[512,512]{1,0:T(8,128)(2,1)S(1)} %get-tuple-element.93, ...), kind=kLoop, calls=%fused_computation.3 | loop fusion | flops 2621440 | bytes 2105344 | tf_op jit(solution)/shard_map/broadcast_in_dim | solution.py:812
  (82 shorter events, 10.6 us)
Async XLA Ops:
  0.0 13.2 %copy-start = (s32[1,16,8]{1,2,0:T(8,128)S(1)}, s32[1,16,8]{1,2,0:T(8,128)}, u32[]{:S(2)}) copy-start(s32[1,16,8]{1,2,0:T(8,128)} %param.18) | copy-start | bytes 1540
  1.1 22.4 %collective-permute-start = (bf16[256,512]{1,0:T(8,128)(2,1)S(1)}, bf16[256,512]{1,0:T(8,128)(2,1)S(1)}, u32[]{:S(2)}, u32[]{:S(2)}) collective-permute-start(bf16[256,512]{1,0:T(8,128)(2,1)S(1)} %get-tuple-element.112), channel_id=1, source_target_pairs={{0,4},{4,0},{8,12},{12,8},{1,5},{5,1},{9,13},{13,9},{2,6},{6,2},{1... | collective-permute-start | bytes 786440 | tf_op jit(solution)/shard_map/ppermute | solution.py:655
  4.2 14.3 %collective-permute-start.4 = (bf16[256,512]{1,0:T(8,128)(2,1)S(1)}, bf16[256,512]{1,0:T(8,128)(2,1)S(1)}, u32[]{:S(2)}, u32[]{:S(2)}) collective-permute-start(bf16[256,512]{1,0:T(8,128)(2,1)S(1)} %get-tuple-element.112), channel_id=1, source_target_pairs={{0,8},{4,12},{8,0},{12,4},{1,9},{5,13},{9,1},{13,5},{2,10},{6,14},... | collective-permute-start | bytes 786440 | tf_op jit(solution)/shard_map/ppermute | solution.py:655
  6.8 18.9 %collective-permute-start.1 = (bf16[512,512]{1,0:T(8,128)(2,1)}, bf16[512,512]{1,0:T(8,128)(2,1)S(1)}, u32[]{:S(2)}, u32[]{:S(2)}) collective-permute-start(bf16[512,512]{1,0:T(8,128)(2,1)} %bitcast.33), channel_id=1, source_target_pairs={{0,2},{2,0},{1,3},{3,1},{4,6},{6,4},{5,7},{7,5},{8,10},{10,8},{9,1... | collective-permute-start | bytes 1572872 | tf_op jit(solution)/shard_map/ppermute | solution.py:652
  18.5 8.6 %collective-permute-start.5 = (bf16[256,512]{1,0:T(8,128)(2,1)S(1)}, bf16[256,512]{1,0:T(8,128)(2,1)S(1)}, u32[]{:S(2)}, u32[]{:S(2)}) collective-permute-start(bf16[256,512]{1,0:T(8,128)(2,1)S(1)} %collective-permute-done.4.refs_0_), channel_id=1, source_target_pairs={{0,2},{2,0},{1,3},{3,1},{4,6},{6,4},{5,7},{7,5},{8,10},{10,8},{9,1... | collective-permute-start | bytes 786440 | tf_op jit(solution)/shard_map/ppermute | solution.py:652
  20.4 11.1 %collective-permute-start.2 = (bf16[256,512]{1,0:T(8,128)(2,1)S(1)}, bf16[256,512]{1,0:T(8,128)(2,1)S(1)}, u32[]{:S(2)}, u32[]{:S(2)}) collective-permute-start(bf16[256,512]{1,0:T(8,128)(2,1)S(1)} %get-tuple-element.70), channel_id=1, source_target_pairs={{0,8},{4,12},{8,0},{12,4},{1,9},{5,13},{9,1},{13,5},{2,10},{6,14},... | collective-permute-start | bytes 786440 | tf_op jit(solution)/shard_map/ppermute | solution.py:655
  20.8 10.7 %collective-permute-start.3 = (bf16[256,512]{1,0:T(8,128)(2,1)S(1)}, bf16[256,512]{1,0:T(8,128)(2,1)S(1)}, u32[]{:S(2)}, u32[]{:S(2)}) collective-permute-start(bf16[256,512]{1,0:T(8,128)(2,1)S(1)} %get-tuple-element.70), channel_id=1, source_target_pairs={{0,4},{4,0},{8,12},{12,8},{1,5},{5,1},{9,13},{13,9},{2,6},{6,2},{1... | collective-permute-start | bytes 786440 | tf_op jit(solution)/shard_map/ppermute | solution.py:655
  23.5 1.9 %copy-start.2 = (bf16[3,1024,512]{2,1,0:T(8,128)(2,1)S(1)}, bf16[3,1024,512]{2,1,0:T(8,128)(2,1)}, u32[]{:S(2)}) copy-start(bf16[3,1024,512]{2,1,0:T(8,128)(2,1)} %w_hbm.1) | copy-start | bytes 9437188
  25.6 2.2 %copy-start.1 = (bf16[1,512,512]{2,1,0:T(8,128)(2,1)S(1)}, bf16[1,512,512]{2,1,0:T(8,128)(2,1)}, u32[]{:S(2)}) copy-start(bf16[1,512,512]{2,1,0:T(8,128)(2,1)} %param.11) | copy-start | bytes 1572868
  25.7 9.9 %collective-permute-start.6 = (bf16[256,512]{1,0:T(8,128)(2,1)S(1)}, bf16[256,512]{1,0:T(8,128)(2,1)S(1)}, u32[]{:S(2)}, u32[]{:S(2)}) collective-permute-start(bf16[256,512]{1,0:T(8,128)(2,1)S(1)} %collective-permute-done.unused_hbm.refs_0_), channel_id=1, source_target_pairs={{0,2},{2,0},{1,3},{3,1},{4,6},{6,4},{5,7},{7,5},{8,10},{10,8},{9,1... | collective-permute-start | bytes 786440 | tf_op jit(solution)/shard_map/ppermute | solution.py:652
  31.5 12.9 %collective-permute-start.8 = (bf16[256,512]{1,0:T(8,128)(2,1)S(1)}, bf16[256,512]{1,0:T(8,128)(2,1)S(1)}, u32[]{:S(2)}, u32[]{:S(2)}) collective-permute-start(bf16[256,512]{1,0:T(8,128)(2,1)S(1)} %collective-permute-done.2.here1_ref), channel_id=1, source_target_pairs={{0,2},{2,0},{1,3},{3,1},{4,6},{6,4},{5,7},{7,5},{8,10},{10,8},{9,1... | collective-permute-start | bytes 786440 | tf_op jit(solution)/shard_map/ppermute | solution.py:652
  32.1 11.7 %collective-permute-start.10 = (bf16[256,512]{1,0:T(8,128)(2,1)S(1)}, bf16[256,512]{1,0:T(8,128)(2,1)S(1)}, u32[]{:S(2)}, u32[]{:S(2)}) collective-permute-start(bf16[256,512]{1,0:T(8,128)(2,1)S(1)} %collective-permute-done.2.here1_ref), channel_id=1, source_target_pairs={{0,4},{4,0},{8,12},{12,8},{1,5},{5,1},{9,13},{13,9},{2,6},{6,2},{1... | collective-permute-start | bytes 786440 | tf_op jit(solution)/shard_map/ppermute | solution.py:655
  33.9 10.5 %collective-permute-start.7 = (bf16[256,512]{1,0:T(8,128)(2,1)S(1)}, bf16[256,512]{1,0:T(8,128)(2,1)S(1)}, u32[]{:S(2)}, u32[]{:S(2)}) collective-permute-start(bf16[256,512]{1,0:T(8,128)(2,1)S(1)} %collective-permute-done.3.here0_ref), channel_id=1, source_target_pairs={{0,2},{2,0},{1,3},{3,1},{4,6},{6,4},{5,7},{7,5},{8,10},{10,8},{9,1... | collective-permute-start | bytes 786440 | tf_op jit(solution)/shard_map/ppermute | solution.py:652
  35.3 13.7 %collective-permute-start.9 = (bf16[2,256,512]{2,1,0:T(8,128)(2,1)S(1)}, bf16[2,256,512]{2,1,0:T(8,128)(2,1)S(1)}, u32[]{:S(2)}, u32[]{:S(2)}) collective-permute-start(bf16[2,256,512]{2,1,0:T(8,128)(2,1)S(1)} %piece_projections.2.refs_1_), channel_id=1, source_target_pairs={{0,4},{4,0},{8,12},{12,8},{1,5},{5,1},{9,13},{13,9},{2,6},{6,2},{1... | collective-permute-start | bytes 1572872 | tf_op jit(solution)/shard_map/ppermute | solution.py:655
  39.7 4.7 %copy-start.3 = (bf16[512,1024]{1,0:T(8,128)(2,1)S(1)}, bf16[512,1024]{1,0:T(8,128)(2,1)}, u32[]{:S(2)}) copy-start(bf16[512,1024]{1,0:T(8,128)(2,1)} %w_out_hbm.1) | copy-start | bytes 3145732
  43.8 6.4 %collective-permute-start.11 = (bf16[256,512]{1,0:T(8,128)(2,1)S(1)}, bf16[256,512]{1,0:T(8,128)(2,1)S(1)}, u32[]{:S(2)}, u32[]{:S(2)}) collective-permute-start(bf16[256,512]{1,0:T(8,128)(2,1)S(1)} %collective-permute-done.10.here_ref), channel_id=1, source_target_pairs={{0,2},{2,0},{1,3},{3,1},{4,6},{6,4},{5,7},{7,5},{8,10},{10,8},{9,1... | collective-permute-start | bytes 786440 | tf_op jit(solution)/shard_map/ppermute | solution.py:652
  50.2 18.9 %copy-start.4 = (f32[512]{0:T(512)S(1)}, f32[512]{0:T(512)}, u32[]{:S(2)}) copy-start(f32[512]{0:T(512)} %param.15) | copy-start | bytes 6148
  50.2 18.9 %copy-start.5 = (f32[512]{0:T(512)S(1)}, f32[512]{0:T(512)}, u32[]{:S(2)}) copy-start(f32[512]{0:T(512)} %param.14) | copy-start | bytes 6148
  55.0 10.0 %collective-permute-start.12 = (bf16[512,512]{1,0:T(8,128)(2,1)S(1)}, bf16[512,512]{1,0:T(8,128)(2,1)S(1)}, u32[]{:S(2)}, u32[]{:S(2)}) collective-permute-start(bf16[512,512]{1,0:T(8,128)(2,1)S(1)} %get-tuple-element.94), channel_id=1, source_target_pairs={{0,2},{2,0},{1,3},{3,1},{4,6},{6,4},{5,7},{7,5},{8,10},{10,8},{9,1... | collective-permute-start | bytes 1572872 | tf_op jit(solution)/shard_map/ppermute | solution.py:652
  65.4 3.7 %collective-permute-start.13 = (f32[2,512]{1,0:T(2,128)S(1)}, f32[2,512]{1,0:T(2,128)S(1)}, u32[]{:S(2)}, u32[]{:S(2)}) collective-permute-start(f32[2,512]{1,0:T(2,128)S(1)} %pad_maximum_fusion), channel_id=1, source_target_pairs={{0,2},{2,0},{1,3},{3,1},{4,6},{6,4},{5,7},{7,5},{8,10},{10,8},{9,1... | collective-permute-start | bytes 12296 | tf_op jit(solution)/shard_map/ppermute | solution.py:652
